TPU v7x, 512 devices: a whole 4x4x16 slice. The times are simulated.
512 devices in a mesh: dp: 32 (over z, core), tensor: 16 (over y, x).
Axes of the slice: x: 4, y: 4, z: 16, core: 2. Of those that a mesh axis runs over, the one named last changes fastest.
Arguments:
- queries: bfloat16 [2048, 4, 32, 128], P(('dp', 'tensor')), may hold values from -160 to 160, as said below
- cached_key_rows: bfloat16 [2048, 4, 512, 128], P(('dp', 'tensor')), may hold values from -6 to 6
- cached_value_rows: bfloat16 [2048, 4, 512, 128], P(('dp', 'tensor')), may hold values from -24 to 24
- cache_fill_length: int32 [2048], P(('dp', 'tensor')), may hold values from 4 to 512, as said below
- request_adapters: int32 [2048], P('dp'), may hold values from 0 to 1023, as said below
- wo: bfloat16 [4096, 4096], P('tensor'), may hold values from -0.125 to 0.125
- adapter_down_weight: bfloat16 [1024, 16, 4096], P('dp', None, 'tensor'), may hold values from -0.09375 to 0.09375
- adapter_up_weight: bfloat16 [1024, 16, 4096], P('dp', None, 'tensor'), may hold values from -1.5 to 1.5
Outputs:
- layer_out: bfloat16 [2048, 4, 4096], P('dp', None, 'tensor')
Inputs may be any that keep to these rules, and one draw needn't show every extreme that they name: `queries`: queries of order one; some may be far larger. `cache_fill_length`: 512 is reached by some request in every draw. `request_adapters`: adapter a is kept by dp index a // 32. Among the 64 requests of one dp index (aligned blocks of 64), at most 2 use adapters of one owner, and some owner gets exactly 2 in every block. Some adapters are far more popular than others.
All inputs are finite; a program needn't handle non-finite values.
Results may differ from a plain program's by a relative error of at most 0.006.
Values may be sent and summed in bfloat16 or wider, within the bound.
No kernel may reach another device: no remote copies, remote signals or barrier semaphores. Data moves between devices by JAX's collectives and lax.ppermute only.
A program may use at most 64 MiB of HBM per device.

v0:
```python
import math

import jax
import jax.numpy as jnp
from jax import lax
from jax.sharding import PartitionSpec as P

NEG_FILL = -1e30


def attend(queries, cached_key_rows, cached_value_rows, cache_fill_length):
    requests, steps, heads, head_dim = queries.shape
    kv_heads = cached_key_rows.shape[1]
    cache_len = cached_key_rows.shape[2]
    per_group = heads // kv_heads
    grouped = queries.reshape(requests, steps, kv_heads, per_group, head_dim)
    scores = jnp.einsum(
        "rskgd,rkpd->rskgp", grouped, cached_key_rows, preferred_element_type=jnp.float32
    ) / math.sqrt(head_dim)
    positions = jnp.arange(cache_len, dtype=jnp.int32)
    last_pos = cache_fill_length[:, None] - steps + jnp.arange(steps, dtype=jnp.int32)[None, :]
    valid_mask = positions[None, None, :] <= last_pos[:, :, None]
    scores = jnp.where(valid_mask[:, :, None, None, :], scores, NEG_FILL)
    highest = jnp.max(scores, axis=-1, keepdims=True)
    raised = jnp.exp(scores - highest)
    weights = (raised / jnp.sum(raised, axis=-1, keepdims=True)).astype(jnp.bfloat16)
    attended = jnp.einsum(
        "rskgp,rkpd->rskgd", weights, cached_value_rows, preferred_element_type=jnp.float32
    )
    return attended.astype(jnp.bfloat16).reshape(requests, steps, heads, head_dim)


def slot_layout(adapter_list, owner_partial):
    owner_ids = adapter_list // owner_partial
    local_ids = adapter_list % owner_partial
    order = jnp.arange(adapter_list.shape[-1], dtype=jnp.int32)
    same_owner = owner_ids[..., :, None] == owner_ids[..., None, :]
    earlier = order[:, None] > order[None, :]
    rank_index = jnp.sum(jnp.logical_and(same_owner, earlier), axis=-1)
    return (owner_ids, local_ids, rank_index)


def owner_table(every_list, owner_partial, capacity, owner_now):
    owner_ids, local_ids, rank_index = slot_layout(every_list, owner_partial)
    columns = jnp.arange(capacity, dtype=jnp.int32)
    hits = jnp.logical_and(
        owner_ids[:, :, None] == owner_now, rank_index[:, :, None] == columns[None, None, :]
    )
    return jnp.sum(jnp.where(hits, local_ids[:, :, None], 0), axis=1)


def reduce_base(base_term):
    return lax.psum_scatter(base_term, "tensor", scatter_dimension=2, tiled=True)


def total_shrink(partial_shrink):
    return lax.psum(partial_shrink, "tensor").astype(jnp.bfloat16)


def on_device(
    queries,
    cached_key_rows,
    cached_value_rows,
    cache_fill_length,
    request_adapters,
    wo,
    adapter_down_weight,
    adapter_up_weight,
):
    owners = lax.axis_size("dp")
    group_size = request_adapters.shape[0]
    owner_partial = adapter_down_weight.shape[0]
    capacity = max(2, -(-group_size // owners))
    slot_count = owners * capacity
    every_list = lax.all_gather(request_adapters, "dp", axis=0, tiled=True).reshape(
        owners, group_size
    )
    local_adapter_table = owner_table(every_list, owner_partial, capacity, lax.axis_index("dp"))
    owner_ids, local_ids, rank_index = slot_layout(request_adapters, owner_partial)
    slot_index = owner_ids * capacity + rank_index
    attended = attend(queries, cached_key_rows, cached_value_rows, cache_fill_length)
    steps = attended.shape[1]
    by_heads = lax.all_to_all(attended, "tensor", split_axis=2, concat_axis=0, tiled=True)
    head_cols = by_heads.reshape(group_size, steps, by_heads.shape[2] * by_heads.shape[3])
    base_term = jnp.einsum("qsc,cd->qsd", head_cols, wo, preferred_element_type=jnp.float32)
    fetched_down, fetched_up = (
        lax.all_to_all(
            adapter_down_weight[local_adapter_table], "dp", split_axis=0, concat_axis=0, tiled=True
        ),
        lax.all_to_all(
            adapter_up_weight[local_adapter_table], "dp", split_axis=0, concat_axis=0, tiled=True
        ),
    )
    page_down = fetched_down.reshape((slot_count,) + fetched_down.shape[2:])[slot_index]
    paged_up_weight = fetched_up.reshape((slot_count,) + fetched_up.shape[2:])[slot_index]
    partial_shrink = jnp.einsum(
        "qsc,qrc->qsr", head_cols, page_down, preferred_element_type=jnp.float32
    )
    rank_projection = total_shrink(partial_shrink)
    base_output = reduce_base(base_term)
    adapter_delta = jnp.einsum(
        "kom,kmx->kox", rank_projection, paged_up_weight, preferred_element_type=jnp.float32
    )
    return (base_output + adapter_delta).astype(jnp.bfloat16)


def solution(mesh):
    in_specs = (
        P(("dp", "tensor"), None, None, None),
        P(("dp", "tensor"), None, None, None),
        P(("dp", "tensor"), None, None, None),
        P(("dp", "tensor")),
        P("dp"),
        P("tensor", None),
        P("dp", None, "tensor"),
        P("dp", None, "tensor"),
    )
    out_specs = P("dp", None, "tensor")
    return jax.shard_map(
        on_device, mesh=mesh, in_specs=in_specs, out_specs=out_specs, check_vma=False
    )
```

profile of v0, /device:TPU:32, one launch (start us, length us, event | category | flops | bytes accessed | tf_op | source)
XLA Modules:
  0.0 220.9 jit_solution(11796592181834308883)
XLA Ops:
  6.5 0.8 broadcast_add_fusion
  7.3 0.1 iota_add_fusion
  7.4 0.1 iota_compare_fusion.2
  7.5 2.6 %fusion.34 = (f32[4,4,4,8]{3,1,2,0:T(4,128)S(1)}, f32[4,4,4,8,512]{4,3,1,2,0:T(8,128)S(1)}) fusion(bf16[4,4,512,128]{3,2,1,0:T(8,128)(2,1)} %param.9, pred[4,4,512]{2,1,0:T(4,128)(4,1)S(1)} %iota_compare_fusion.2, bf16[4,4,32,128]{3,2,1,0:T(8,128)(2,1)} %param.8), kind=kOutput, calls=%fused_computation.54 | convolution fusion | flops 68157952 | bytes 3287040 | tf_op jit(solution)/shard_map/sub | solution.py:25
  10.1 2.1 fusion.21
  12.2 0.1 copy.30
  12.2 14.8 %all_to_all.25 = bf16[4,4,32,128]{3,1,0,2:T(4,128)(2,1)S(1)} all-to-all(bf16[4,4,32,128]{3,1,0,2:T(4,128)(2,1)S(1)} %copy.30), channel_id=1, replica_groups=mesh['dp'=32,'tensor'=16] {'tensor'}, dimensions={2} | all-to-all | bytes 262144 | tf_op jit(solution)/shard_map/all_to_all | solution.py:83
  27.1 0.1 copy.32
  27.2 0.1 reshape.164
  27.3 2.6 %fusion.5 = f32[64,4,4096]{2,0,1:T(8,128)} fusion(bf16[64,4,256]{2,0,1:T(8,128)(2,1)S(1)} %reshape.164, bf16[256,4096]{1,0:T(8,128)(2,1)S(1)} %copy-done), kind=kOutput, calls=%fused_computation.9 | convolution fusion | flops 536870912 | bytes 6422528 | tf_op jit(solution)/shard_map/qsc,cd->qsd/dot_general | solution.py:85
  30.0 1.3 dynamic-slice
  32.0 0.3 dynamic-update-slice
  32.3 26.2 %all-reduce = s32[2048]{0:T(1024)S(1)} all-reduce(s32[2048]{0:T(1024)S(1)} %dynamic-update-slice), channel_id=1, replica_groups=mesh['dp'=32,'tensor'=16] {'dp'}, use_global_device_ids=true, to_apply=%add | all-reduce | flops 2048 | bytes 16384
  58.5 0.1 reshape.165
  58.6 0.9 convert_reduce_fusion
  59.5 0.1 select_reduce_fusion
  59.7 0.1 copy.33
  59.7 0.1 reshape.170
  59.9 1.4 gather_fusion
  61.3 7.4 %all-to-all-start.1 = ((bf16[32,2,16,256]{3,2,1,0:T(8,128)(2,1)}), bf16[32,2,16,256]{3,2,1,0:T(8,128)(2,1)S(1)}, u32[]{:S(2)}, u32[]{:S(2)}) async-start(bf16[32,2,16,256]{3,2,1,0:T(8,128)(2,1)} %bitcast.13), calls=%async_computation.2 | async-start | bytes 1048576 | tf_op jit(solution)/shard_map/all_to_all | solution.py:87
  68.7 1.4 gather_fusion.2
  70.1 30.8 %all-to-all-done.1 = bf16[32,2,16,256]{3,2,1,0:T(8,128)(2,1)S(1)} async-done(((bf16[32,2,16,256]{3,2,1,0:T(8,128)(2,1)}), bf16[32,2,16,256]{3,2,1,0:T(8,128)(2,1)S(1)}, u32[]{:S(2)}, u32[]{:S(2)}) %all-to-all-start.1) | async-done | bytes 524320 | tf_op jit(solution)/shard_map/all_to_all | solution.py:87
  100.9 5.4 %all-to-all-start.2 = ((bf16[32,2,16,256]{3,2,1,0:T(8,128)(2,1)}), bf16[32,2,16,256]{3,2,1,0:T(8,128)(2,1)S(1)}, u32[]{:S(2)}, u32[]{:S(2)}) async-start(bf16[32,2,16,256]{3,2,1,0:T(8,128)(2,1)} %bitcast.15), calls=%async_computation.3 | async-start | bytes 1048576 | tf_op jit(solution)/shard_map/all_to_all | solution.py:90
  106.2 0.2 convert_reduce_fusion.1
  106.5 1.4 gather_fusion.1
  107.9 30.5 %all-to-all-done.2 = bf16[32,2,16,256]{3,2,1,0:T(8,128)(2,1)S(1)} async-done(((bf16[32,2,16,256]{3,2,1,0:T(8,128)(2,1)}), bf16[32,2,16,256]{3,2,1,0:T(8,128)(2,1)S(1)}, u32[]{:S(2)}, u32[]{:S(2)}) %all-to-all-start.2) | async-done | bytes 524320 | tf_op jit(solution)/shard_map/all_to_all | solution.py:90
  138.3 0.6 gather_fusion.3
  138.9 1.3 fusion.26
  140.2 71.9 %psum.7 = bf16[64,4,16]{2,1,0:T(4,128)(2,1)S(1)} all-reduce(f32[64,4,16]{2,1,0:T(4,128)S(1)} %fusion.26), channel_id=1, replica_groups=mesh['dp'=32,'tensor'=16] {'tensor'}, use_global_device_ids=true, to_apply=%region_6.7 | all-reduce | flops 4096 | bytes 24576 | tf_op jit(solution)/shard_map/psum | solution.py:57
  212.1 0.2 fusion.39
  212.3 1.0 fusion.25
  213.3 0.8 copy.36
  (22 shorter events, 0.2 us)
Async XLA Ops:
  6.5 20.8 %copy-start = (bf16[256,4096]{1,0:T(8,128)(2,1)S(1)}, bf16[256,4096]{1,0:T(8,128)(2,1)}, u32[]{:S(2)}) copy-start(bf16[256,4096]{1,0:T(8,128)(2,1)} %param.13) | copy-start | bytes 6291460
  6.5 205.8 %reduce-scatter.2.cloned.1.call-start = ((), (), s32[]{:S(2)}) async-start(), calls=%async_computation.4 | async-start | bytes 4456448 | tf_op jit(solution)/shard_map/reduce_scatter | solution.py:53
  29.9 2.0 copy-start.3
  29.9 29.9 %copy-start.1 = (bf16[32,16,256]{2,1,0:T(8,128)(2,1)S(1)}, bf16[32,16,256]{2,1,0:T(8,128)(2,1)}, u32[]{:S(2)}) copy-start(bf16[32,16,256]{2,1,0:T(8,128)(2,1)} %param.14) | copy-start | bytes 786436
  30.0 38.7 %copy-start.2 = (bf16[32,16,256]{2,1,0:T(8,128)(2,1)S(1)}, bf16[32,16,256]{2,1,0:T(8,128)(2,1)}, u32[]{:S(2)}) copy-start(bf16[32,16,256]{2,1,0:T(8,128)(2,1)} %param.15) | copy-start | bytes 786436
  61.3 39.6 %all-to-all-start.1 = ((bf16[32,2,16,256]{3,2,1,0:T(8,128)(2,1)}), bf16[32,2,16,256]{3,2,1,0:T(8,128)(2,1)S(1)}, u32[]{:S(2)}, u32[]{:S(2)}) async-start(bf16[32,2,16,256]{3,2,1,0:T(8,128)(2,1)} %bitcast.13), calls=%async_computation.2 | async-start | bytes 1048576 | tf_op jit(solution)/shard_map/all_to_all | solution.py:87
  100.9 37.5 %all-to-all-start.2 = ((bf16[32,2,16,256]{3,2,1,0:T(8,128)(2,1)}), bf16[32,2,16,256]{3,2,1,0:T(8,128)(2,1)S(1)}, u32[]{:S(2)}, u32[]{:S(2)}) async-start(bf16[32,2,16,256]{3,2,1,0:T(8,128)(2,1)} %bitcast.15), calls=%async_computation.3 | async-start | bytes 1048576 | tf_op jit(solution)/shard_map/all_to_all | solution.py:90
Sparse Core Ops, SparseCore 0:
  30.1 93.1 reduce-scatter.1
where the time goes:
time: 221 us
  blocking collectives  113 us (51%)
  waiting for transfers between devices  61.3 us (28%)
  between operations  14.3 us (6%)
  starting transfers between devices  12.7 us (6%)
  matrix products  8.73 us (4%)
  local copies, waits for them, and re-layouts  7.77 us (4%)
  other arithmetic  3.27 us (1%)
    psum x1, blocking collectives, total_shrink(): return lax.psum(partial_shrink, 'tensor').astype(jnp.bfloat16)  71.9 us
    all_to_all x1, waiting for transfers between devices, on_device(): lax.all_to_all(adapter_down_weight[local_adapter_table], 'dp', split_axis...  30.8 us
    all_to_all x1, waiting for transfers between devices, on_device(): lax.all_to_all(adapter_up_weight[local_adapter_table], 'dp', split_axis=0...  30.5 us
    unnamed x1, blocking collectives  26.2 us
    all_to_all x1, blocking collectives, on_device(): lax.all_to_all(attended, 'tensor', split_axis=2, concat_axis=0, tiled=True)  14.8 us
    all_to_all x1, starting transfers between devices, on_device(): lax.all_to_all(adapter_down_weight[local_adapter_table], 'dp', split_axis...  7.37 us
    all_to_all x1, starting transfers between devices, on_device(): lax.all_to_all(adapter_up_weight[local_adapter_table], 'dp', split_axis=0...  5.35 us
  transfers between devices with their start and end apart: 3, of which 2 were waited for; matrix products, arithmetic and copies ran while one was open for 4% of the time, Pallas kernels for 0%

commit v1 on v0

v1 whole, which is shorter than its diff:
```python
import functools
import math

import jax
import jax.numpy as jnp
from jax import lax
from jax.experimental import pallas as pl
from jax.experimental.pallas import tpu as pltpu
from jax.sharding import PartitionSpec as P

NEG_FILL = -1e30
SIDE = 4


def attend(queries, cached_key_rows, cached_value_rows, cache_fill_length):
    requests, steps, heads, head_dim = queries.shape
    kv_heads = cached_key_rows.shape[1]
    cache_len = cached_key_rows.shape[2]
    per_group = heads // kv_heads
    grouped = queries.reshape(requests, steps, kv_heads, per_group, head_dim)
    scores = jnp.einsum(
        "rskgd,rkpd->rskgp", grouped, cached_key_rows, preferred_element_type=jnp.float32
    ) / math.sqrt(head_dim)
    positions = jnp.arange(cache_len, dtype=jnp.int32)
    last_pos = cache_fill_length[:, None] - steps + jnp.arange(steps, dtype=jnp.int32)[None, :]
    valid_mask = positions[None, None, :] <= last_pos[:, :, None]
    scores = jnp.where(valid_mask[:, :, None, None, :], scores, NEG_FILL)
    highest = jnp.max(scores, axis=-1, keepdims=True)
    raised = jnp.exp(scores - highest)
    weights = (raised / jnp.sum(raised, axis=-1, keepdims=True)).astype(jnp.bfloat16)
    attended = jnp.einsum(
        "rskgp,rkpd->rskgd", weights, cached_value_rows, preferred_element_type=jnp.float32
    )
    return attended.astype(jnp.bfloat16).reshape(requests, steps, heads, head_dim)


def project_kernel(place_ref, rows_ref, *refs):
    wo_refs, out_refs = refs[:SIDE], refs[SIDE:]
    step = pl.program_id(0)
    for s in range(SIDE):

        @pl.when(step == s)
        def _(s=s):
            for u in range(SIDE):
                part = jnp.dot(
                    rows_ref[...], wo_refs[u][...], preferred_element_type=jnp.float32
                )
                out_refs[s][u] = part.astype(out_refs[s].dtype)


def project(head_rows, wo, place):
    rows, depth = head_rows.shape
    width = wo.shape[1] // (SIDE * SIDE)

    def wo_block(u):
        def index_map(s, place_ref):
            x = lax.rem(place_ref[1] + s, SIDE)
            y = lax.rem(place_ref[0] + u, SIDE)
            return (0, y * SIDE + x)

        return pl.BlockSpec((depth, width), index_map)

    def whole(*shape):
        return pl.BlockSpec(shape, lambda s, place_ref: (0,) * len(shape))

    kinds = [jnp.float32] + [jnp.bfloat16] * (SIDE - 1)
    return pl.pallas_call(
        project_kernel,
        grid_spec=pltpu.PrefetchScalarGridSpec(
            num_scalar_prefetch=1,
            grid=(SIDE,),
            in_specs=[whole(rows, depth)] + [wo_block(u) for u in range(SIDE)],
            out_specs=[whole(SIDE, rows, width) for _ in kinds],
        ),
        out_shape=[jax.ShapeDtypeStruct((SIDE, rows, width), kind) for kind in kinds],
        compiler_params=pltpu.CompilerParams(vmem_limit_bytes=32 * 1024 * 1024),
        cost_estimate=pl.CostEstimate(
            flops=2 * rows * depth * wo.shape[1],
            bytes_accessed=2 * wo.size + 2 * rows * wo.shape[1],
            transcendentals=0,
        ),
        name="project",
    )(place, head_rows, *([wo] * SIDE))


def shift_x(value, s):
    pairs = [
        (y * SIDE + x, y * SIDE + (x + s) % SIDE) for y in range(SIDE) for x in range(SIDE)
    ]
    return lax.ppermute(value, "tensor", pairs)


def shift_y(value, s):
    pairs = [
        (y * SIDE + x, ((y + s) % SIDE) * SIDE + x) for y in range(SIDE) for x in range(SIDE)
    ]
    return lax.ppermute(value, "tensor", pairs)


def summed_projection(head_rows, wo, place):
    own, *others = project(head_rows, wo, place)
    arrived = [shift_x(part, s + 1) for s, part in enumerate(others)]
    along_x = [
        own[u] + sum(part[u].astype(jnp.float32) for part in arrived) for u in range(SIDE)
    ]
    arrived = [shift_y(along_x[u].astype(jnp.bfloat16), u) for u in range(1, SIDE)]
    return along_x[0] + sum(part.astype(jnp.float32) for part in arrived)


def on_device(
    queries,
    cached_key_rows,
    cached_value_rows,
    cache_fill_length,
    request_adapters,
    wo,
    adapter_down_weight,
    adapter_up_weight,
):
    owners = lax.axis_size("dp")
    shares = lax.axis_size("tensor")
    group_size = request_adapters.shape[0]
    owner_partial, rank, width = adapter_down_weight.shape
    capacity = group_size // owners
    steps = queries.shape[1]
    rows = group_size * steps
    tensor_index = lax.axis_index("tensor").astype(jnp.int32)
    place = jnp.stack([tensor_index // SIDE, tensor_index % SIDE])

    owner_ids = request_adapters // owner_partial
    local_ids = request_adapters % owner_partial
    order = jnp.arange(group_size, dtype=jnp.int32)
    earlier = (owner_ids[:, None] == owner_ids[None, :]) & (order[:, None] > order[None, :])
    slots = owner_ids * capacity + jnp.sum(earlier.astype(jnp.int32), axis=1)
    row_slots = (slots[:, None] * steps + jnp.arange(steps, dtype=jnp.int32)).reshape(rows)
    to_slots = (jnp.arange(rows, dtype=jnp.int32)[:, None] == row_slots[None, :]).astype(
        jnp.bfloat16
    )
    row_locals = jnp.repeat(local_ids, steps).astype(jnp.bfloat16)
    id_lanes = jnp.broadcast_to(row_locals[:, None], (rows, 128))

    attended = attend(queries, cached_key_rows, cached_value_rows, cache_fill_length)
    by_heads = lax.all_to_all(attended, "tensor", split_axis=2, concat_axis=0, tiled=True)
    head_rows = by_heads.reshape(rows, width)

    payload = jnp.dot(
        to_slots,
        jnp.concatenate([head_rows, id_lanes], axis=1),
        preferred_element_type=jnp.float32,
    ).astype(jnp.bfloat16)
    owned = lax.all_to_all(
        payload.reshape(owners, capacity * steps, width + 128), "dp", 0, 0, tiled=True
    ).reshape(rows, width + 128)
    owned_rows = owned[:, :width]
    owned_ids = owned[:, width : width + 1].astype(jnp.int32)
    columns = jnp.arange(owner_partial * rank, dtype=jnp.int32)
    chosen = owned_ids == (columns // rank)[None, :]
    fold = (jnp.arange(rank, dtype=jnp.int32)[:, None] == (columns % rank)[None, :]).astype(
        jnp.float32
    )
    every_down = jnp.einsum(
        "qc,kc->qk",
        owned_rows,
        adapter_down_weight.reshape(owner_partial * rank, width),
        preferred_element_type=jnp.float32,
    )
    partial_shrink = jnp.einsum(
        "mk,qk->mq",
        fold,
        jnp.where(chosen, every_down, 0.0),
        precision=lax.Precision.HIGHEST,
        preferred_element_type=jnp.float32,
    )
    partials = lax.all_to_all(
        jnp.broadcast_to(partial_shrink[None], (shares, rank, rows)), "tensor", 0, 0, tiled=True
    )
    shrink = jnp.sum(partials, axis=0).astype(jnp.bfloat16)
    spread = jnp.einsum(
        "mq,mk->qk", shrink, fold.astype(jnp.bfloat16), preferred_element_type=jnp.float32
    )
    delta = jnp.dot(
        jnp.where(chosen, spread, 0.0).astype(jnp.bfloat16),
        adapter_up_weight.reshape(owner_partial * rank, width),
        preferred_element_type=jnp.float32,
    ).astype(jnp.bfloat16)
    returned = lax.all_to_all(
        delta.reshape(owners, capacity * steps, width), "dp", 0, 0, tiled=True
    ).reshape(rows, width)

    base_output = summed_projection(head_rows, wo, place)
    adapter_delta = jnp.einsum(
        "sq,sd->qd", to_slots, returned, preferred_element_type=jnp.float32
    )
    return (base_output + adapter_delta).astype(jnp.bfloat16).reshape(group_size, steps, width)


def solution(mesh):
    in_specs = (
        P(("dp", "tensor"), None, None, None),
        P(("dp", "tensor"), None, None, None),
        P(("dp", "tensor"), None, None, None),
        P(("dp", "tensor")),
        P("dp"),
        P("tensor", None),
        P("dp", None, "tensor"),
        P("dp", None, "tensor"),
    )
    out_specs = P("dp", None, "tensor")
    return jax.shard_map(
        on_device, mesh=mesh, in_specs=in_specs, out_specs=out_specs, check_vma=False
    )
```

time: 221 us -> 120 us (0.54)
  the two profiles are of different devices: /device:TPU:32 before, /device:TPU:2 now
where the time goes in v1:
time: 120 us; the launch traced here: 119 us
  starting transfers between devices  52.7 us (44%)
  waiting for transfers between devices  44.7 us (37%)
  matrix products  7.71 us (6%)
  local copies, waits for them, and re-layouts  4.99 us (4%)
  other arithmetic  4.99 us (4%)
  Pallas kernels  3.65 us (3%)
    all_to_all x1, waiting for transfers between devices, on_device(): lax.all_to_all(payload.reshape(owners, capacity * steps, width + 128), 'd...  20 us
    ppermute x3, waiting for transfers between devices, shift_x(): return lax.ppermute(value, 'tensor', pairs)  14.1 us
    all_to_all x1, starting transfers between devices, on_device(): lax.all_to_all(payload.reshape(owners, capacity * steps, width + 128), 'd...  13.7 us
    ppermute x3, starting transfers between devices, shift_y(): return lax.ppermute(value, 'tensor', pairs)  10.8 us
    ppermute x3, starting transfers between devices, shift_x(): return lax.ppermute(value, 'tensor', pairs)  10.4 us
    all_to_all x1, starting transfers between devices, on_device(): lax.all_to_all(attended, 'tensor', split_axis=2, concat_axis=0, tiled=True)  9.21 us
    all_to_all x1, waiting for transfers between devices, on_device(): lax.all_to_all(attended, 'tensor', split_axis=2, concat_axis=0, tiled=True)  6.12 us
    all_to_all x1, starting transfers between devices, on_device(): lax.all_to_all(jnp.broadcast_to(partial_shrink[None], (shares, rank, rows...  4.78 us
  transfers between devices with their start and end apart: 10, of which 6 were waited for; matrix products, arithmetic and copies ran while one was open for 4% of the time, Pallas kernels for 3%

profile of v1, /device:TPU:2, one launch (start us, length us, event | category | flops | bytes accessed | tf_op | source)
XLA Modules:
  0.0 119.0 jit_solution(7878859667008103070)
XLA Ops:
  0.0 0.8 broadcast_add_fusion
  1.0 0.6 copy-done
  1.6 1.9 %fusion.63 = (f32[4,4,4,8]{3,1,2,0:T(4,128)S(1)}, f32[4,4,4,8,512]{4,3,1,2,0:T(8,128)S(1)}) fusion(bf16[4,4,512,128]{3,2,1,0:T(8,128)(2,1)S(1)} %copy-done, pred[4,4,512]{2,1,0:T(4,128)(4,1)S(1)} %iota_compare_fusion.6, bf16[4,4,32,128]{3,2,1,0:T(8,128)(2,1)} %param.8), kind=kOutput, calls=%fused_computation.82 | convolution fusion | flops 68157952 | bytes 3287040 | tf_op jit(solution)/shard_map/sub | solution.py:29
  3.5 2.1 %fusion.23 = bf16[4,4,4,8,128]{4,3,1,2,0:T(8,128)(2,1)S(1)} fusion(bf16[4,4,512,128]{3,2,1,0:T(8,128)(2,1)} %param.10, f32[4,4,4,8,512]{4,3,1,2,0:T(8,128)S(1)} %get-tuple-element.19, f32[4,4,4,8]{3,1,2,0:T(4,128)S(1)} %get-tuple-element.18), kind=kOutput, calls=%fused_computation.18 | convolution fusion | flops 67698688 | bytes 3278848 | tf_op jit(solution)/shard_map/rskgp,rkpd->rskgd/dot_general | solution.py:31
  5.6 0.7 copy.24
  6.3 9.2 %all-to-all-start = ((bf16[4,4,32,128]{3,1,0,2:T(4,128)(2,1)}), bf16[4,4,32,128]{3,1,0,2:T(4,128)(2,1)S(1)}, u32[]{:S(2)}, u32[]{:S(2)}) async-start(bf16[4,4,32,128]{3,1,0,2:T(4,128)(2,1)} %copy.24), calls=%async_computation | async-start | bytes 262144 | tf_op jit(solution)/shard_map/all_to_all | solution.py:143
  16.2 6.1 %all-to-all-done = bf16[4,4,32,128]{3,1,0,2:T(4,128)(2,1)S(1)} async-done(((bf16[4,4,32,128]{3,1,0,2:T(4,128)(2,1)}), bf16[4,4,32,128]{3,1,0,2:T(4,128)(2,1)S(1)}, u32[]{:S(2)}, u32[]{:S(2)}) %all-to-all-start) | async-done | bytes 131104 | tf_op jit(solution)/shard_map/all_to_all | solution.py:143
  22.5 0.9 fusion.22
  23.5 13.7 %all-to-all-start.1 = ((bf16[32,8,384]{2,1,0:T(8,128)(2,1)}), bf16[32,8,384]{2,1,0:T(8,128)(2,1)S(1)}, u32[]{:S(2)}, u32[]{:S(2)}) async-start(bf16[32,8,384]{2,1,0:T(8,128)(2,1)} %fusion.22), calls=%async_computation.1 | async-start | bytes 393216 | tf_op jit(solution)/shard_map/all_to_all | solution.py:151
  37.2 20.0 %all-to-all-done.1 = bf16[32,8,384]{2,1,0:T(8,128)(2,1)S(1)} async-done(((bf16[32,8,384]{2,1,0:T(8,128)(2,1)}), bf16[32,8,384]{2,1,0:T(8,128)(2,1)S(1)}, u32[]{:S(2)}, u32[]{:S(2)}) %all-to-all-start.1) | async-done | bytes 196640 | tf_op jit(solution)/shard_map/all_to_all | solution.py:151
  57.3 0.3 convolution_select_fusion
  57.5 0.3 fusion.46
  57.9 0.8 broadcast_in_dim.27
  58.6 4.8 %all-to-all-start.2 = ((f32[16,16,256]{2,1,0:T(8,128)}), f32[16,16,256]{2,1,0:T(8,128)S(1)}, u32[]{:S(2)}, u32[]{:S(2)}) async-start(f32[16,16,256]{2,1,0:T(8,128)} %broadcast_in_dim.27), calls=%async_computation.2 | async-start | bytes 524288 | tf_op jit(solution)/shard_map/all_to_all | solution.py:174
  63.5 1.6 %copy-done.1 = bf16[256,4096]{1,0:T(8,128)(2,1)S(1)} copy-done((bf16[256,4096]{1,0:T(8,128)(2,1)S(1)}, bf16[256,4096]{1,0:T(8,128)(2,1)}, u32[]{:S(2)}) %copy-start.1) | copy-done | bytes 2097176
  65.1 3.7 %project.1 = (f32[4,256,256]{2,1,0:T(8,128)S(1)}, bf16[4,256,256]{2,1,0:T(8,128)(2,1)}, bf16[4,256,256]{2,1,0:T(8,128)(2,1)}, bf16[4,256,256]{2,1,0:T(8,128)(2,1)}) custom-call(s32[2]{0:T(128)S(1)} %pad_add_fusion.place_ref, bf16[256,256]{1,0:T(8,128)(2,1)S(1)} %bitcast.75, bf16[256,4096]{1,0:T(8,128)(2,1)S(1)} %copy-done.1, ...), custom_call_target="tpu_custom_call" | custom-call | flops 536870912 | bytes 4194304 | tf_op jit(solution)/shard_map/project/pallas_call | solution.py:67
  68.7 3.4 %collective-permute-start = (bf16[4,256,256]{2,1,0:T(8,128)(2,1)}, bf16[4,256,256]{2,1,0:T(8,128)(2,1)}, u32[]{:S(2)}, u32[]{:S(2)}) collective-permute-start(bf16[4,256,256]{2,1,0:T(8,128)(2,1)} %get-tuple-element.10), channel_id=1, source_target_pairs={{0,1},{1,2},{2,3},{3,0},{4,5},{5,6},{6,7},{7,4},{8,9},{9,10},{10,1... | collective-permute-start | bytes 1572872 | tf_op jit(solution)/shard_map/ppermute | solution.py:90
  72.1 2.7 %collective-permute-start.1 = (bf16[4,256,256]{2,1,0:T(8,128)(2,1)}, bf16[4,256,256]{2,1,0:T(8,128)(2,1)}, u32[]{:S(2)}, u32[]{:S(2)}) collective-permute-start(bf16[4,256,256]{2,1,0:T(8,128)(2,1)} %get-tuple-element.11), channel_id=1, source_target_pairs={{0,2},{1,3},{2,0},{3,1},{4,6},{5,7},{6,4},{7,5},{8,10},{9,11},{10,... | collective-permute-start | bytes 1572872 | tf_op jit(solution)/shard_map/ppermute | solution.py:90
  74.9 4.3 %collective-permute-start.2 = (bf16[4,256,256]{2,1,0:T(8,128)(2,1)}, bf16[4,256,256]{2,1,0:T(8,128)(2,1)}, u32[]{:S(2)}, u32[]{:S(2)}) collective-permute-start(bf16[4,256,256]{2,1,0:T(8,128)(2,1)} %get-tuple-element.12), channel_id=1, source_target_pairs={{0,3},{1,0},{2,1},{3,2},{4,7},{5,4},{6,5},{7,6},{8,11},{9,8},{10,9... | collective-permute-start | bytes 1572872 | tf_op jit(solution)/shard_map/ppermute | solution.py:90
  79.2 2.0 %fusion.26 = bf16[32,8,256]{2,1,0:T(8,128)(2,1)} fusion(bf16[512,256]{1,0:T(8,128)(2,1)} %bitcast.82, s32[512]{0:T(512)S(1)} %get-tuple-element.21, s32[256]{0:T(256)S(1)} %convert_reduce_fusion, s32[512]{0:T(512)S(1)} %get-tuple-element.20, bf16[16,256]{1,0:T(8,128)(2,1)S(1)} %reduce_sum.29), kind=kOutput, calls=%fused_computation.19 | convolution fusion | flops 71786496 | bytes 406528 | tf_op jit(solution)/shard_map/dot_general | solution.py:181
  81.2 3.9 %all-to-all-start.3 = ((bf16[32,8,256]{2,1,0:T(8,128)(2,1)}), bf16[32,8,256]{2,1,0:T(8,128)(2,1)S(1)}, u32[]{:S(2)}, u32[]{:S(2)}) async-start(bf16[32,8,256]{2,1,0:T(8,128)(2,1)} %fusion.26), calls=%async_computation.3 | async-start | bytes 262144 | tf_op jit(solution)/shard_map/all_to_all | solution.py:186
  85.1 0.7 collective-permute-done
  85.8 4.9 %collective-permute-done.1 = bf16[4,256,256]{2,1,0:T(8,128)(2,1)} collective-permute-done((bf16[4,256,256]{2,1,0:T(8,128)(2,1)}, bf16[4,256,256]{2,1,0:T(8,128)(2,1)}, u32[]{:S(2)}, u32[]{:S(2)}) %collective-permute-start.1) | collective-permute-done | bytes 524320 | tf_op jit(solution)/shard_map/ppermute | solution.py:90
  90.7 8.5 %collective-permute-done.2 = bf16[4,256,256]{2,1,0:T(8,128)(2,1)} collective-permute-done((bf16[4,256,256]{2,1,0:T(8,128)(2,1)}, bf16[4,256,256]{2,1,0:T(8,128)(2,1)}, u32[]{:S(2)}, u32[]{:S(2)}) %collective-permute-start.2) | collective-permute-done | bytes 524320 | tf_op jit(solution)/shard_map/ppermute | solution.py:90
  99.2 2.2 %fusion.38 = (bf16[256,256]{1,0:T(8,128)(2,1)}, bf16[256,256]{1,0:T(8,128)(2,1)S(1)}, bf16[256,256]{1,0:T(8,128)(2,1)S(1)}) fusion(f32[4,256,256]{2,1,0:T(8,128)S(1)} %get-tuple-element.9, bf16[4,256,256]{2,1,0:T(8,128)(2,1)} %collective-permute-done.2, bf16[4,256,256]{2,1,0:T(8,128)(2,1)} %collective-permute-done.1, ...), kind=kLoop, calls=%fused_computation.37 | loop fusion | flops 1376256 | bytes 2359296 | tf_op jit(solution)/shard_map/add | solution.py:104
  101.4 3.4 %collective-permute-start.3 = (bf16[256,256]{1,0:T(8,128)(2,1)}, bf16[256,256]{1,0:T(8,128)(2,1)}, u32[]{:S(2)}, u32[]{:S(2)}) collective-permute-start(bf16[256,256]{1,0:T(8,128)(2,1)} %get-tuple-element.13), channel_id=1, source_target_pairs={{0,4},{1,5},{2,6},{3,7},{4,8},{5,9},{6,10},{7,11},{8,12},{9,13},{1... | collective-permute-start | bytes 393224 | tf_op jit(solution)/shard_map/ppermute | solution.py:97
  104.8 3.7 %collective-permute-start.5 = (bf16[256,256]{1,0:T(8,128)(2,1)S(1)}, bf16[256,256]{1,0:T(8,128)(2,1)}, u32[]{:S(2)}, u32[]{:S(2)}) collective-permute-start(bf16[256,256]{1,0:T(8,128)(2,1)S(1)} %get-tuple-element.14), channel_id=1, source_target_pairs={{0,12},{1,13},{2,14},{3,15},{4,0},{5,1},{6,2},{7,3},{8,4},{9,5},{1... | collective-permute-start | bytes 393224 | tf_op jit(solution)/shard_map/ppermute | solution.py:97
  108.5 3.7 %collective-permute-start.4 = (bf16[256,256]{1,0:T(8,128)(2,1)S(1)}, bf16[256,256]{1,0:T(8,128)(2,1)}, u32[]{:S(2)}, u32[]{:S(2)}) collective-permute-start(bf16[256,256]{1,0:T(8,128)(2,1)S(1)} %get-tuple-element.15), channel_id=1, source_target_pairs={{0,8},{1,9},{2,10},{3,11},{4,12},{5,13},{6,14},{7,15},{8,0},{9,1},... | collective-permute-start | bytes 393224 | tf_op jit(solution)/shard_map/ppermute | solution.py:97
  112.2 0.3 fusion.33
  112.5 4.4 %collective-permute-done.4 = bf16[256,256]{1,0:T(8,128)(2,1)} collective-permute-done((bf16[256,256]{1,0:T(8,128)(2,1)S(1)}, bf16[256,256]{1,0:T(8,128)(2,1)}, u32[]{:S(2)}, u32[]{:S(2)}) %collective-permute-start.4) | collective-permute-done | bytes 131104 | tf_op jit(solution)/shard_map/ppermute | solution.py:97
  116.9 1.4 %fusion.30 = bf16[256,256]{1,0:T(8,128)(2,1)S(1)} fusion(f32[256,256]{1,0:T(8,128)S(1)} %fusion.33, bf16[256,256]{1,0:T(8,128)(2,1)} %collective-permute-done.5, bf16[256,256]{1,0:T(8,128)(2,1)} %collective-permute-done.4, bf16[256,256]{1,0:T(8,128)(2,1)} %collective-permute-done.3, f32[4,256,256]{2,1,0:T(8,128)S(1)} %get-tuple-element.9, ...), kind=kLoop, calls=%fused_computation.25 | loop fusion | flops 917504 | bytes 1441792 | tf_op jit(solution)/shard_map/convert_element_type | solution.py:194
  118.3 0.7 reshape.142
  (28 shorter events, 1.2 us)
Async XLA Ops:
  0.0 1.6 %copy-start = (bf16[4,4,512,128]{3,2,1,0:T(8,128)(2,1)S(1)}, bf16[4,4,512,128]{3,2,1,0:T(8,128)(2,1)}, u32[]{:S(2)}) copy-start(bf16[4,4,512,128]{3,2,1,0:T(8,128)(2,1)} %param.9) | copy-start | bytes 6291460
  3.5 12.1 %copy-start.3 = (s32[64]{0:T(128)S(1)}, s32[64]{0:T(128)}, u32[]{:S(2)}) copy-start(s32[64]{0:T(128)} %param.12) | copy-start | bytes 772
  5.6 51.7 %copy-start.2 = (bf16[32,16,256]{2,1,0:T(8,128)(2,1)S(1)}, bf16[32,16,256]{2,1,0:T(8,128)(2,1)}, u32[]{:S(2)}) copy-start(bf16[32,16,256]{2,1,0:T(8,128)(2,1)} %param.14) | copy-start | bytes 786436
  6.3 15.9 %all-to-all-start = ((bf16[4,4,32,128]{3,1,0,2:T(4,128)(2,1)}), bf16[4,4,32,128]{3,1,0,2:T(4,128)(2,1)S(1)}, u32[]{:S(2)}, u32[]{:S(2)}) async-start(bf16[4,4,32,128]{3,1,0,2:T(4,128)(2,1)} %copy.24), calls=%async_computation | async-start | bytes 262144 | tf_op jit(solution)/shard_map/all_to_all | solution.py:143
  23.5 33.7 %all-to-all-start.1 = ((bf16[32,8,384]{2,1,0:T(8,128)(2,1)}), bf16[32,8,384]{2,1,0:T(8,128)(2,1)S(1)}, u32[]{:S(2)}, u32[]{:S(2)}) async-start(bf16[32,8,384]{2,1,0:T(8,128)(2,1)} %fusion.22), calls=%async_computation.1 | async-start | bytes 393216 | tf_op jit(solution)/shard_map/all_to_all | solution.py:151
  58.6 20.6 %all-to-all-start.2 = ((f32[16,16,256]{2,1,0:T(8,128)}), f32[16,16,256]{2,1,0:T(8,128)S(1)}, u32[]{:S(2)}, u32[]{:S(2)}) async-start(f32[16,16,256]{2,1,0:T(8,128)} %broadcast_in_dim.27), calls=%async_computation.2 | async-start | bytes 524288 | tf_op jit(solution)/shard_map/all_to_all | solution.py:174
  63.5 1.6 %copy-start.1 = (bf16[256,4096]{1,0:T(8,128)(2,1)S(1)}, bf16[256,4096]{1,0:T(8,128)(2,1)}, u32[]{:S(2)}) copy-start(bf16[256,4096]{1,0:T(8,128)(2,1)} %refs_3_.1) | copy-start | bytes 6291460
  68.7 17.1 %collective-permute-start = (bf16[4,256,256]{2,1,0:T(8,128)(2,1)}, bf16[4,256,256]{2,1,0:T(8,128)(2,1)}, u32[]{:S(2)}, u32[]{:S(2)}) collective-permute-start(bf16[4,256,256]{2,1,0:T(8,128)(2,1)} %get-tuple-element.10), channel_id=1, source_target_pairs={{0,1},{1,2},{2,3},{3,0},{4,5},{5,6},{6,7},{7,4},{8,9},{9,10},{10,1... | collective-permute-start | bytes 1572872 | tf_op jit(solution)/shard_map/ppermute | solution.py:90
  72.1 18.6 %collective-permute-start.1 = (bf16[4,256,256]{2,1,0:T(8,128)(2,1)}, bf16[4,256,256]{2,1,0:T(8,128)(2,1)}, u32[]{:S(2)}, u32[]{:S(2)}) collective-permute-start(bf16[4,256,256]{2,1,0:T(8,128)(2,1)} %get-tuple-element.11), channel_id=1, source_target_pairs={{0,2},{1,3},{2,0},{3,1},{4,6},{5,7},{6,4},{7,5},{8,10},{9,11},{10,... | collective-permute-start | bytes 1572872 | tf_op jit(solution)/shard_map/ppermute | solution.py:90
  74.9 24.3 %collective-permute-start.2 = (bf16[4,256,256]{2,1,0:T(8,128)(2,1)}, bf16[4,256,256]{2,1,0:T(8,128)(2,1)}, u32[]{:S(2)}, u32[]{:S(2)}) collective-permute-start(bf16[4,256,256]{2,1,0:T(8,128)(2,1)} %get-tuple-element.12), channel_id=1, source_target_pairs={{0,3},{1,0},{2,1},{3,2},{4,7},{5,4},{6,5},{7,6},{8,11},{9,8},{10,9... | collective-permute-start | bytes 1572872 | tf_op jit(solution)/shard_map/ppermute | solution.py:90
  81.2 31.0 %all-to-all-start.3 = ((bf16[32,8,256]{2,1,0:T(8,128)(2,1)}), bf16[32,8,256]{2,1,0:T(8,128)(2,1)S(1)}, u32[]{:S(2)}, u32[]{:S(2)}) async-start(bf16[32,8,256]{2,1,0:T(8,128)(2,1)} %fusion.26), calls=%async_computation.3 | async-start | bytes 262144 | tf_op jit(solution)/shard_map/all_to_all | solution.py:186
  101.4 11.1 %collective-permute-start.3 = (bf16[256,256]{1,0:T(8,128)(2,1)}, bf16[256,256]{1,0:T(8,128)(2,1)}, u32[]{:S(2)}, u32[]{:S(2)}) collective-permute-start(bf16[256,256]{1,0:T(8,128)(2,1)} %get-tuple-element.13), channel_id=1, source_target_pairs={{0,4},{1,5},{2,6},{3,7},{4,8},{5,9},{6,10},{7,11},{8,12},{9,13},{1... | collective-permute-start | bytes 393224 | tf_op jit(solution)/shard_map/ppermute | solution.py:97
  104.8 7.7 %collective-permute-start.5 = (bf16[256,256]{1,0:T(8,128)(2,1)S(1)}, bf16[256,256]{1,0:T(8,128)(2,1)}, u32[]{:S(2)}, u32[]{:S(2)}) collective-permute-start(bf16[256,256]{1,0:T(8,128)(2,1)S(1)} %get-tuple-element.14), channel_id=1, source_target_pairs={{0,12},{1,13},{2,14},{3,15},{4,0},{5,1},{6,2},{7,3},{8,4},{9,5},{1... | collective-permute-start | bytes 393224 | tf_op jit(solution)/shard_map/ppermute | solution.py:97
  108.5 8.5 %collective-permute-start.4 = (bf16[256,256]{1,0:T(8,128)(2,1)S(1)}, bf16[256,256]{1,0:T(8,128)(2,1)}, u32[]{:S(2)}, u32[]{:S(2)}) collective-permute-start(bf16[256,256]{1,0:T(8,128)(2,1)S(1)} %get-tuple-element.15), channel_id=1, source_target_pairs={{0,8},{1,9},{2,10},{3,11},{4,12},{5,13},{6,14},{7,15},{8,0},{9,1},... | collective-permute-start | bytes 393224 | tf_op jit(solution)/shard_map/ppermute | solution.py:97

commit v2 on v1

v2 whole, which is shorter than its diff:
```python
import math

import jax
import jax.numpy as jnp
from jax import lax
from jax.experimental import pallas as pl
from jax.experimental.pallas import tpu as pltpu
from jax.sharding import PartitionSpec as P

NEG_FILL = -1e30
SIDE = 4


def attend_kernel(
    fill_ref, queries_ref, keys_ref, values_ref, out_ref,
    query_buf, key_buf, value_buf, score_buf, weight_buf, grouped_buf, query_sem, key_sem, value_sem,
):
    requests, steps, heads, head_dim = query_buf.shape
    kv_heads, cache_len = key_buf.shape[1], key_buf.shape[2]
    per_group = heads // kv_heads
    group_rows = steps * per_group
    width = 2 * head_dim
    query_copy = pltpu.make_async_copy(queries_ref, query_buf, query_sem)
    key_copies = [
        pltpu.make_async_copy(keys_ref.at[r], key_buf.at[r], key_sem.at[r]) for r in range(requests)
    ]
    value_copies = [
        pltpu.make_async_copy(values_ref.at[r], value_buf.at[r], value_sem.at[r])
        for r in range(requests)
    ]
    query_copy.start()
    for copy in key_copies + value_copies:
        copy.start()
    position = lax.broadcasted_iota(jnp.int32, (group_rows, cache_len), 1)
    step_of = lax.broadcasted_iota(jnp.int32, (group_rows, cache_len), 0) // per_group
    reach = position + steps - step_of
    query_copy.wait()
    for r in range(requests):
        every = query_buf[r].astype(jnp.float32)
        key_copies[r].wait()
        for k in range(kv_heads):
            grouped = every[:, k * per_group : (k + 1) * per_group, :]
            grouped = grouped.reshape(group_rows, head_dim).astype(jnp.bfloat16)
            score_buf[r * kv_heads + k] = lax.dot_general(
                grouped,
                key_buf[r, k],
                (((1,), (1,)), ((), ())),
                preferred_element_type=jnp.float32,
            )
    for r in range(requests):
        valid = reach <= fill_ref[r]
        for k in range(kv_heads):
            scores = score_buf[r * kv_heads + k] * (1.0 / math.sqrt(head_dim))
            scores = jnp.where(valid, scores, NEG_FILL)
            raised = jnp.exp(scores - jnp.max(scores, axis=1, keepdims=True))
            weights = raised * (1.0 / jnp.sum(raised, axis=1, keepdims=True))
            weight_buf[r * kv_heads + k] = weights.astype(jnp.bfloat16)
    for r in range(requests):
        value_copies[r].wait()
        for k in range(kv_heads):
            grouped_buf[r * kv_heads + k] = jnp.dot(
                weight_buf[r * kv_heads + k], value_buf[r, k], preferred_element_type=jnp.float32
            )
    for block in range(heads // 2):
        k, first = block * 2 // per_group, block * 2 % per_group
        halves = []
        for j in range(2):
            pieces = [
                grouped_buf[r * kv_heads + k, pl.ds(first + j, steps, stride=per_group), :]
                for r in range(requests)
            ]
            halves.append(jnp.concatenate(pieces, axis=0))
        part = jnp.concatenate(halves, axis=1).astype(jnp.bfloat16)
        out_ref[block, :, :width] = part
        out_ref[block ^ SIDE, :, width:] = part


def attend(queries, cached_key_rows, cached_value_rows, cache_fill_length):
    requests, steps, heads, head_dim = queries.shape
    kv_heads, cache_len = cached_key_rows.shape[1:3]
    blocks, rows = heads // 2, requests * steps
    pairs, group_rows = requests * kv_heads, steps * heads // kv_heads
    distant = pl.BlockSpec(memory_space=pltpu.HBM)
    return pl.pallas_call(
        attend_kernel,
        in_specs=[pl.BlockSpec(memory_space=pltpu.SMEM), distant, distant, distant],
        out_specs=pl.BlockSpec(memory_space=pltpu.VMEM),
        out_shape=jax.ShapeDtypeStruct((blocks, rows, 4 * head_dim), jnp.bfloat16),
        scratch_shapes=[
            pltpu.VMEM(queries.shape, jnp.bfloat16),
            pltpu.VMEM(cached_key_rows.shape, jnp.bfloat16),
            pltpu.VMEM(cached_value_rows.shape, jnp.bfloat16),
            pltpu.VMEM((pairs, group_rows, cache_len), jnp.float32),
            pltpu.VMEM((pairs, group_rows, cache_len), jnp.bfloat16),
            pltpu.VMEM((pairs, group_rows, head_dim), jnp.float32),
            pltpu.SemaphoreType.DMA,
            pltpu.SemaphoreType.DMA((requests,)),
            pltpu.SemaphoreType.DMA((requests,)),
        ],
        compiler_params=pltpu.CompilerParams(vmem_limit_bytes=60 * 1024 * 1024),
        cost_estimate=pl.CostEstimate(
            flops=4 * rows * heads * cache_len * head_dim,
            bytes_accessed=2 * 2 * cached_key_rows.size,
            transcendentals=rows * heads * cache_len,
        ),
        name="attend",
    )(cache_fill_length, queries, cached_key_rows, cached_value_rows)


def cut_kernel(wo_ref, out_ref, sems):
    bands, depth, band = out_ref.shape
    low = 1 - lax.rem(lax.axis_index("tensor") // SIDE, 2)
    row = pl.multiple_of(lax.rem(lax.axis_index("dp"), 2) * depth, depth)
    copies = [
        pltpu.make_async_copy(
            wo_ref.at[pl.ds(row, depth), pl.ds(pl.multiple_of((2 * high + low) * band, band), band)],
            out_ref.at[high],
            sems.at[high],
        )
        for high in range(bands)
    ]
    for copy in copies:
        copy.start()
    for copy in copies:
        copy.wait()


def cut_wo(wo):
    bands = SIDE // 2
    return pl.pallas_call(
        cut_kernel,
        in_specs=[pl.BlockSpec(memory_space=pltpu.HBM)],
        out_specs=pl.BlockSpec(memory_space=pltpu.VMEM),
        out_shape=jax.ShapeDtypeStruct((bands, wo.shape[0] // 2, wo.shape[1] // SIDE), wo.dtype),
        scratch_shapes=[pltpu.SemaphoreType.DMA((bands,))],
        cost_estimate=pl.CostEstimate(flops=0, bytes_accessed=2 * wo.size, transcendentals=0),
        name="cut_wo",
    )(wo)


def project_kernel(rows_ref, own_ref, mine_ref, sibling_ref, *out_refs):
    tensor = lax.axis_index("tensor")
    y, x = tensor // SIDE, lax.rem(tensor, SIDE)
    core = lax.rem(lax.axis_index("dp"), 2)
    half = mine_ref.shape[1]
    width = rows_ref.shape[1] // 2
    own_rows = rows_ref[:, :width]
    mine_rows = rows_ref[:, pl.ds(pl.multiple_of(width + core * half, half), half)]
    sibling_rows = rows_ref[:, pl.ds(pl.multiple_of(width + (1 - core) * half, half), half)]
    for s, out_ref in enumerate(out_refs):
        across = lax.rem(x + s, SIDE)
        for v in range(2):
            line = y ^ (2 * v)
            own_at = pl.multiple_of((line * SIDE + across) * width, width)
            at = pl.ds(pl.multiple_of(across * width, width), width)
            part = jnp.dot(
                own_rows, own_ref[:, pl.ds(own_at, width)], preferred_element_type=jnp.float32
            )
            part += jnp.dot(
                mine_rows, mine_ref[line // 2, :, at], preferred_element_type=jnp.float32
            )
            part += jnp.dot(
                sibling_rows, sibling_ref[line // 2, :, at], preferred_element_type=jnp.float32
            )
            out_ref[v] = part.astype(out_ref.dtype)


def project(head_rows, wo, mine, sibling):
    rows, depth = head_rows.shape
    width = wo.shape[1] // (SIDE * SIDE)
    resident = pl.BlockSpec(memory_space=pltpu.VMEM)
    kinds = [jnp.float32] + [jnp.bfloat16] * (SIDE - 1)
    return pl.pallas_call(
        project_kernel,
        in_specs=[resident] * 4,
        out_specs=[resident for _ in kinds],
        out_shape=[jax.ShapeDtypeStruct((2, rows, width), kind) for kind in kinds],
        compiler_params=pltpu.CompilerParams(vmem_limit_bytes=24 * 1024 * 1024),
        cost_estimate=pl.CostEstimate(
            flops=rows * depth * wo.shape[1],
            bytes_accessed=3 * wo.size + rows * wo.shape[1],
            transcendentals=0,
        ),
        name="project",
    )(head_rows, wo, mine, sibling)


def down_kernel(owned_ref, down_ref, out_ref, ids_ref):
    rows, columns = owned_ref.shape[0], down_ref.shape[1]
    rank = out_ref.shape[1]
    adapters = down_ref.shape[0] // rank
    every = lax.dot_general(
        down_ref[...],
        owned_ref[:, :columns],
        (((1,), (1,)), ((), ())),
        preferred_element_type=jnp.float32,
    )
    ids = jnp.transpose(owned_ref[:, columns:].astype(jnp.float32))[:8]
    ids_ref[...] = ids
    adapter = lax.broadcasted_iota(jnp.int32, (adapters, rank, rows), 0).astype(jnp.float32)
    chosen = adapter == ids[:1].reshape(1, 1, rows)
    part = jnp.sum(jnp.where(chosen, every.reshape(adapters, rank, rows), 0.0), axis=0)
    for copy in range(out_ref.shape[0]):
        out_ref[copy] = part


def shrink_down(owned, down, shares, rank):
    rows = owned.shape[0]
    resident = pl.BlockSpec(memory_space=pltpu.VMEM)
    return pl.pallas_call(
        down_kernel,
        in_specs=[resident] * 2,
        out_specs=[resident] * 2,
        out_shape=[
            jax.ShapeDtypeStruct((shares, rank, rows), jnp.float32),
            jax.ShapeDtypeStruct((8, rows), jnp.float32),
        ],
        compiler_params=pltpu.CompilerParams(vmem_limit_bytes=16 * 1024 * 1024),
        cost_estimate=pl.CostEstimate(
            flops=2 * rows * down.size, bytes_accessed=4 * down.size, transcendentals=0
        ),
        name="shrink_down",
    )(owned, down)


def up_kernel(partials_ref, ids_ref, up_ref, out_ref):
    shares, rank, rows = partials_ref.shape
    adapters = up_ref.shape[0] // rank
    shrink = partials_ref[0]
    for share in range(1, shares):
        shrink += partials_ref[share]
    shrink = shrink.astype(jnp.bfloat16).astype(jnp.float32)
    adapter = lax.broadcasted_iota(jnp.int32, (adapters, rank, rows), 0).astype(jnp.float32)
    chosen = adapter == ids_ref[:1].reshape(1, 1, rows)
    spread = jnp.where(chosen, shrink.reshape(1, rank, rows), 0.0)
    out_ref[...] = lax.dot_general(
        spread.reshape(adapters * rank, rows).astype(jnp.bfloat16),
        up_ref[...],
        (((0,), (0,)), ((), ())),
        preferred_element_type=jnp.float32,
    ).astype(jnp.bfloat16)


def expand_up(partials, ids, up):
    rows = partials.shape[2]
    resident = pl.BlockSpec(memory_space=pltpu.VMEM)
    return pl.pallas_call(
        up_kernel,
        in_specs=[resident] * 3,
        out_specs=resident,
        out_shape=jax.ShapeDtypeStruct((rows, up.shape[1]), jnp.bfloat16),
        compiler_params=pltpu.CompilerParams(vmem_limit_bytes=16 * 1024 * 1024),
        cost_estimate=pl.CostEstimate(
            flops=2 * rows * up.size, bytes_accessed=4 * up.size, transcendentals=0
        ),
        name="expand_up",
    )(partials, ids, up)


def shift_pairs(value, target):
    pairs = []
    for y in range(SIDE):
        for x in range(SIDE):
            to_y, to_x = target(y, x)
            pairs.append((y * SIDE + x, to_y * SIDE + to_x))
    return lax.ppermute(value, "tensor", pairs)


def after(value, *earlier):
    return lax.optimization_barrier((value,) + earlier)[0]


def on_device(
    queries,
    cached_key_rows,
    cached_value_rows,
    cache_fill_length,
    request_adapters,
    wo,
    adapter_down_weight,
    adapter_up_weight,
):
    owners = lax.axis_size("dp")
    shares = lax.axis_size("tensor")
    group_size = request_adapters.shape[0]
    owner_partial, rank, width = adapter_down_weight.shape
    capacity = group_size // owners
    steps = queries.shape[1]
    rows = group_size * steps

    owner_ids = request_adapters // owner_partial
    local_ids = request_adapters % owner_partial
    order = jnp.arange(group_size, dtype=jnp.int32)
    earlier = (owner_ids[:, None] == owner_ids[None, :]) & (order[:, None] > order[None, :])
    slots = owner_ids * capacity + jnp.sum(earlier.astype(jnp.int32), axis=1)
    row_slots = (slots[:, None] * steps + jnp.arange(steps, dtype=jnp.int32)).reshape(rows)
    to_slots = (jnp.arange(rows, dtype=jnp.int32)[:, None] == row_slots[None, :]).astype(
        jnp.bfloat16
    )
    row_locals = jnp.repeat(local_ids, steps).astype(jnp.bfloat16)
    id_lanes = jnp.broadcast_to(row_locals[:, None], (rows, 128))

    mine = shift_pairs(cut_wo(wo), lambda y, x: (y ^ 1, x))
    sibling = lax.ppermute(mine, "dp", [(d, d ^ 1) for d in range(owners)])

    attended = attend(queries, cached_key_rows, cached_value_rows, cache_fill_length)
    pair_rows = lax.all_to_all(attended, "tensor", 0, 0, tiled=True).reshape(rows, 2 * width)
    head_rows = pair_rows[:, :width]

    payload = jnp.dot(
        to_slots,
        jnp.concatenate([head_rows, id_lanes], axis=1),
        preferred_element_type=jnp.float32,
    ).astype(jnp.bfloat16)
    own, *others = project(after(pair_rows, payload), wo, mine, sibling)
    arrived = [
        shift_pairs(part, lambda y, x, s=s: (y, (x + s) % SIDE))
        for s, part in enumerate(others, start=1)
    ]
    owned = lax.all_to_all(
        payload.reshape(owners, capacity * steps, width + 128), "dp", 0, 0, tiled=True
    ).reshape(rows, width + 128)
    partial_shrink, ids = shrink_down(
        after(owned, own), adapter_down_weight.reshape(owner_partial * rank, width), shares, rank
    )
    partials = lax.all_to_all(partial_shrink, "tensor", 0, 0, tiled=True)
    delta = expand_up(partials, ids, adapter_up_weight.reshape(owner_partial * rank, width))
    along_x = [own[v] + sum(part[v].astype(jnp.float32) for part in arrived) for v in range(2)]
    delta = after(delta, *along_x)
    returned = lax.all_to_all(
        delta.reshape(owners, capacity * steps, width), "dp", 0, 0, tiled=True
    ).reshape(rows, width)

    across_y = shift_pairs(along_x[1].astype(jnp.bfloat16), lambda y, x: (y ^ 2, x))
    base_output = along_x[0] + across_y.astype(jnp.float32)
    adapter_delta = jnp.einsum(
        "sq,sd->qd", to_slots, returned, preferred_element_type=jnp.float32
    )
    return (base_output + adapter_delta).astype(jnp.bfloat16).reshape(group_size, steps, width)


def solution(mesh):
    in_specs = (
        P(("dp", "tensor"), None, None, None),
        P(("dp", "tensor"), None, None, None),
        P(("dp", "tensor"), None, None, None),
        P(("dp", "tensor")),
        P("dp"),
        P("tensor", None),
        P("dp", None, "tensor"),
        P("dp", None, "tensor"),
    )
    out_specs = P("dp", None, "tensor")
    return jax.shard_map(
        on_device, mesh=mesh, in_specs=in_specs, out_specs=out_specs, check_vma=False
    )
```

time: 120 us -> 100 us (0.83)
  the two profiles are of different devices: /device:TPU:2 before, /device:TPU:1 now
where the time goes in v2:
time: 100 us; the launch traced here: 99.4 us
  starting transfers between devices  53.8 us (54%)
  waiting for transfers between devices  18.1 us (18%)
  blocking collectives  11.3 us (11%)
  Pallas kernels  10.4 us (10%)
  local copies, waits for them, and re-layouts  3.92 us (4%)
  matrix products  1.18 us (1%)
    all_to_all x1, starting transfers between devices, on_device(): lax.all_to_all(payload.reshape(owners, capacity * steps, width + 128), 'd...  17.2 us
    ppermute x5, starting transfers between devices, shift_pairs(): return lax.ppermute(value, 'tensor', pairs)  15.7 us
    all_to_all x1, waiting for transfers between devices, on_device(): lax.all_to_all(delta.reshape(owners, capacity * steps, width), 'dp', 0, 0...  11.8 us
    all_to_all x1, blocking collectives, on_device(): partials = lax.all_to_all(partial_shrink, 'tensor', 0, 0, tiled=True)  11.3 us
    all_to_all x1, starting transfers between devices, on_device(): lax.all_to_all(delta.reshape(owners, capacity * steps, width), 'dp', 0, 0...  11.2 us
    all_to_all x1, starting transfers between devices, on_device(): lax.all_to_all(attended, 'tensor', 0, 0, tiled=True)  7.6 us
    pallas_call x1, Pallas kernels, attend(): pl.pallas_call(attend_kernel, in_specs=[pl.BlockSpec(memory_space=pltpu.S...  5.5 us
    all_to_all x1, waiting for transfers between devices, on_device(): lax.all_to_all(payload.reshape(owners, capacity * steps, width + 128), 'd...  3.61 us
  transfers between devices with their start and end apart: 9, of which 4 were waited for; matrix products, arithmetic and copies ran while one was open for 2% of the time, Pallas kernels for 5%

profile of v2, /device:TPU:1, one launch (start us, length us, event | category | flops | bytes accessed | tf_op | source)
XLA Modules:
  0.0 99.4 jit_solution(8789530440628356266)
XLA Ops:
  0.0 5.5 %attend.1 = bf16[16,16,512]{2,1,0:T(8,128)(2,1)} custom-call(s32[4]{0:T(128)} %fill_ref.1, bf16[4,4,32,128]{3,2,1,0:T(8,128)(2,1)} %queries_ref.1, bf16[4,4,512,128]{3,2,1,0:T(8,128)(2,1)} %keys_ref.1, bf16[4,4,512,128]{3,2,1,0:T(8,128)(2,1)} %values_ref.1), custom_call_target="tpu_custom_call" | custom-call | flops 134217728 | bytes 4194304 | tf_op jit(solution)/shard_map/attend/pallas_call | solution.py:84
  5.5 7.6 %all-to-all-start = ((bf16[16,16,512]{2,1,0:T(8,128)(2,1)}), bf16[16,16,512]{2,1,0:T(8,128)(2,1)S(1)}, u32[]{:S(2)}, u32[]{:S(2)}) async-start(bf16[16,16,512]{2,1,0:T(8,128)(2,1)} %attend.1), calls=%async_computation | async-start | bytes 524288 | tf_op jit(solution)/shard_map/all_to_all | solution.py:307
  13.1 2.0 %cut_wo.1 = bf16[2,128,1024]{2,1,0:T(8,128)(2,1)} custom-call(bf16[256,4096]{1,0:T(8,128)(2,1)} %own_ref.1), custom_call_target="tpu_custom_call" | custom-call | bytes 2097152 | tf_op jit(solution)/shard_map/cut_wo/pallas_call | solution.py:130
  15.2 3.3 %collective-permute-start = (bf16[2,128,1024]{2,1,0:T(8,128)(2,1)}, bf16[2,128,1024]{2,1,0:T(8,128)(2,1)S(1)}, u32[]{:S(2)}, u32[]{:S(2)}) collective-permute-start(bf16[2,128,1024]{2,1,0:T(8,128)(2,1)} %cut_wo.1), channel_id=1, source_target_pairs={{0,4},{1,5},{2,6},{3,7},{4,0},{5,1},{6,2},{7,3},{8,12},{9,13},{10,... | collective-permute-start | bytes 1572872 | tf_op jit(solution)/shard_map/ppermute | solution.py:266
  18.5 0.2 convert_reduce_fusion
  18.7 0.1 iota_add_fusion
  18.7 0.1 broadcast_in_dim.4
  18.8 0.1 convert_element_type.53
  18.9 0.1 add.68
  19.1 1.8 %all-to-all-done = bf16[16,16,512]{2,1,0:T(8,128)(2,1)S(1)} async-done(((bf16[16,16,512]{2,1,0:T(8,128)(2,1)}), bf16[16,16,512]{2,1,0:T(8,128)(2,1)S(1)}, u32[]{:S(2)}, u32[]{:S(2)}) %all-to-all-start) | async-done | bytes 262176 | tf_op jit(solution)/shard_map/all_to_all | solution.py:307
  20.8 0.1 broadcast_in_dim.5
  20.9 0.9 convolution_convert_fusion
  21.9 17.2 %all-to-all-start.1 = ((bf16[32,8,384]{2,1,0:T(8,128)(2,1)}), bf16[32,8,384]{2,1,0:T(8,128)(2,1)S(1)}, u32[]{:S(2)}, u32[]{:S(2)}) async-start(bf16[32,8,384]{2,1,0:T(8,128)(2,1)} %bitcast.3), calls=%async_computation.1 | async-start | bytes 393216 | tf_op jit(solution)/shard_map/all_to_all | solution.py:320
  39.1 2.1 %collective-permute-start.1 = (bf16[2,128,1024]{2,1,0:T(8,128)(2,1)S(1)}, bf16[2,128,1024]{2,1,0:T(8,128)(2,1)S(1)}, u32[]{:S(2)}, u32[]{:S(2)}) collective-permute-start(bf16[2,128,1024]{2,1,0:T(8,128)(2,1)S(1)} %collective-permute-done.mine_ref), channel_id=1, source_target_pairs={{0,16},{16,0},{32,48},{48,32},{64,80},{80,64},{96,112},{112,96},{1... | collective-permute-start | bytes 1572872 | tf_op jit(solution)/shard_map/ppermute | solution.py:304
  41.3 0.8 copy-done.1
  42.0 0.8 collective-permute-done.1.sibling_ref
  42.9 1.0 %copy-done.2 = bf16[2,128,1024]{2,1,0:T(8,128)(2,1)S(1)} copy-done((bf16[2,128,1024]{2,1,0:T(8,128)(2,1)S(1)}, bf16[2,128,1024]{2,1,0:T(8,128)(2,1)}, u32[]{:S(2)}) %copy-start.2) | copy-done | bytes 524312
  43.9 1.7 %project.1 = (f32[2,256,256]{2,1,0:T(8,128)S(1)}, bf16[2,256,256]{2,1,0:T(8,128)(2,1)}, bf16[2,256,256]{2,1,0:T(8,128)(2,1)}, bf16[2,256,256]{2,1,0:T(8,128)(2,1)}) custom-call(bf16[256,512]{1,0:T(8,128)(2,1)S(1)} %bitcast.14, bf16[256,4096]{1,0:T(8,128)(2,1)S(1)} %copy-done, bf16[2,128,1024]{2,1,0:T(8,128)(2,1)S(1)} %copy-done.2, ...), custom_call_target="tpu_custom_call" | custom-call | flops 536870912 | bytes 4194304 | tf_op jit(solution)/shard_map/project/pallas_call | solution.py:173
  45.6 2.2 %collective-permute-start.2 = (bf16[2,256,256]{2,1,0:T(8,128)(2,1)}, bf16[2,256,256]{2,1,0:T(8,128)(2,1)S(1)}, u32[]{:S(2)}, u32[]{:S(2)}) collective-permute-start(bf16[2,256,256]{2,1,0:T(8,128)(2,1)} %get-tuple-element.16), channel_id=1, source_target_pairs={{0,1},{1,2},{2,3},{3,0},{4,5},{5,6},{6,7},{7,4},{8,9},{9,10},{10,1... | collective-permute-start | bytes 786440 | tf_op jit(solution)/shard_map/ppermute | solution.py:266
  47.8 3.3 %collective-permute-start.3 = (bf16[2,256,256]{2,1,0:T(8,128)(2,1)}, bf16[2,256,256]{2,1,0:T(8,128)(2,1)S(1)}, u32[]{:S(2)}, u32[]{:S(2)}) collective-permute-start(bf16[2,256,256]{2,1,0:T(8,128)(2,1)} %get-tuple-element.17), channel_id=1, source_target_pairs={{0,2},{1,3},{2,0},{3,1},{4,6},{5,7},{6,4},{7,5},{8,10},{9,11},{10,... | collective-permute-start | bytes 786440 | tf_op jit(solution)/shard_map/ppermute | solution.py:266
  51.1 3.0 %collective-permute-start.4 = (bf16[2,256,256]{2,1,0:T(8,128)(2,1)}, bf16[2,256,256]{2,1,0:T(8,128)(2,1)S(1)}, u32[]{:S(2)}, u32[]{:S(2)}) collective-permute-start(bf16[2,256,256]{2,1,0:T(8,128)(2,1)} %get-tuple-element.18), channel_id=1, source_target_pairs={{0,3},{1,0},{2,1},{3,2},{4,7},{5,4},{6,5},{7,6},{8,11},{9,8},{10,9... | collective-permute-start | bytes 786440 | tf_op jit(solution)/shard_map/ppermute | solution.py:266
  54.1 3.6 %all-to-all-done.1 = bf16[32,8,384]{2,1,0:T(8,128)(2,1)S(1)} async-done(((bf16[32,8,384]{2,1,0:T(8,128)(2,1)}), bf16[32,8,384]{2,1,0:T(8,128)(2,1)S(1)}, u32[]{:S(2)}, u32[]{:S(2)}) %all-to-all-start.1) | async-done | bytes 196640 | tf_op jit(solution)/shard_map/all_to_all | solution.py:320
  57.7 0.3 shrink_down.1
  58.0 11.3 %all_to_all.20.partials_ref = f32[16,16,256]{2,1,0:T(8,128)S(1)} all-to-all(f32[16,16,256]{2,1,0:T(8,128)S(1)} %get-tuple-element.20), channel_id=1, replica_groups=mesh['dp'=32,'tensor'=16] {'tensor'}, dimensions={0} | all-to-all | bytes 524288 | tf_op jit(solution)/shard_map/all_to_all | solution.py:326
  69.3 0.9 copy-done.4
  70.3 0.9 expand_up.1
  71.2 0.1 add_bitcast_fusion
  71.4 11.2 %all-to-all-start.3 = ((bf16[32,8,256]{2,1,0:T(8,128)(2,1)}), bf16[32,8,256]{2,1,0:T(8,128)(2,1)S(1)}, u32[]{:S(2)}, u32[]{:S(2)}) async-start(bf16[32,8,256]{2,1,0:T(8,128)(2,1)} %bitcast.7), calls=%async_computation.3 | async-start | bytes 262144 | tf_op jit(solution)/shard_map/all_to_all | solution.py:330
  82.5 4.0 %collective-permute-start.5 = (bf16[256,256]{1,0:T(8,128)(2,1)S(1)}, bf16[256,256]{1,0:T(8,128)(2,1)S(1)}, u32[]{:S(2)}, u32[]{:S(2)}) collective-permute-start(bf16[256,256]{1,0:T(8,128)(2,1)S(1)} %add_bitcast_fusion), channel_id=1, source_target_pairs={{0,8},{1,9},{2,10},{3,11},{4,12},{5,13},{6,14},{7,15},{8,0},{9,1},... | collective-permute-start | bytes 393224 | tf_op jit(solution)/shard_map/ppermute | solution.py:266
  86.6 11.8 %all-to-all-done.3 = bf16[32,8,256]{2,1,0:T(8,128)(2,1)S(1)} async-done(((bf16[32,8,256]{2,1,0:T(8,128)(2,1)}), bf16[32,8,256]{2,1,0:T(8,128)(2,1)S(1)}, u32[]{:S(2)}, u32[]{:S(2)}) %all-to-all-start.3) | async-done | bytes 131104 | tf_op jit(solution)/shard_map/all_to_all | solution.py:330
  98.4 0.3 fusion
  98.7 0.7 reshape.68
  (19 shorter events, 0.2 us)
Async XLA Ops:
  5.5 12.9 %copy-start.5 = (s32[64]{0:T(128)S(1)}, s32[64]{0:T(128)}, u32[]{:S(2)}) copy-start(s32[64]{0:T(128)} %param.12) | copy-start | bytes 772
  5.5 15.3 %all-to-all-start = ((bf16[16,16,512]{2,1,0:T(8,128)(2,1)}), bf16[16,16,512]{2,1,0:T(8,128)(2,1)S(1)}, u32[]{:S(2)}, u32[]{:S(2)}) async-start(bf16[16,16,512]{2,1,0:T(8,128)(2,1)} %attend.1), calls=%async_computation | async-start | bytes 524288 | tf_op jit(solution)/shard_map/all_to_all | solution.py:307
  13.1 29.8 %copy-start = (bf16[256,4096]{1,0:T(8,128)(2,1)S(1)}, bf16[256,4096]{1,0:T(8,128)(2,1)}, u32[]{:S(2)}) copy-start(bf16[256,4096]{1,0:T(8,128)(2,1)} %own_ref.1) | copy-start | bytes 6291460
  15.2 23.9 %collective-permute-start = (bf16[2,128,1024]{2,1,0:T(8,128)(2,1)}, bf16[2,128,1024]{2,1,0:T(8,128)(2,1)S(1)}, u32[]{:S(2)}, u32[]{:S(2)}) collective-permute-start(bf16[2,128,1024]{2,1,0:T(8,128)(2,1)} %cut_wo.1), channel_id=1, source_target_pairs={{0,4},{1,5},{2,6},{3,7},{4,0},{5,1},{6,2},{7,3},{8,12},{9,13},{10,... | collective-permute-start | bytes 1572872 | tf_op jit(solution)/shard_map/ppermute | solution.py:266
  20.9 36.8 %copy-start.3 = (bf16[32,16,256]{2,1,0:T(8,128)(2,1)S(1)}, bf16[32,16,256]{2,1,0:T(8,128)(2,1)}, u32[]{:S(2)}) copy-start(bf16[32,16,256]{2,1,0:T(8,128)(2,1)} %param.14) | copy-start | bytes 786436
  21.9 35.8 %all-to-all-start.1 = ((bf16[32,8,384]{2,1,0:T(8,128)(2,1)}), bf16[32,8,384]{2,1,0:T(8,128)(2,1)S(1)}, u32[]{:S(2)}, u32[]{:S(2)}) async-start(bf16[32,8,384]{2,1,0:T(8,128)(2,1)} %bitcast.3), calls=%async_computation.1 | async-start | bytes 393216 | tf_op jit(solution)/shard_map/all_to_all | solution.py:320
  39.1 3.8 %collective-permute-start.1 = (bf16[2,128,1024]{2,1,0:T(8,128)(2,1)S(1)}, bf16[2,128,1024]{2,1,0:T(8,128)(2,1)S(1)}, u32[]{:S(2)}, u32[]{:S(2)}) collective-permute-start(bf16[2,128,1024]{2,1,0:T(8,128)(2,1)S(1)} %collective-permute-done.mine_ref), channel_id=1, source_target_pairs={{0,16},{16,0},{32,48},{48,32},{64,80},{80,64},{96,112},{112,96},{1... | collective-permute-start | bytes 1572872 | tf_op jit(solution)/shard_map/ppermute | solution.py:304
  41.2 0.8 copy-start.1
  42.9 1.0 %copy-start.2 = (bf16[2,128,1024]{2,1,0:T(8,128)(2,1)S(1)}, bf16[2,128,1024]{2,1,0:T(8,128)(2,1)}, u32[]{:S(2)}) copy-start(bf16[2,128,1024]{2,1,0:T(8,128)(2,1)} %copy-done.1) | copy-start | bytes 1572868
  45.6 25.6 %collective-permute-start.2 = (bf16[2,256,256]{2,1,0:T(8,128)(2,1)}, bf16[2,256,256]{2,1,0:T(8,128)(2,1)S(1)}, u32[]{:S(2)}, u32[]{:S(2)}) collective-permute-start(bf16[2,256,256]{2,1,0:T(8,128)(2,1)} %get-tuple-element.16), channel_id=1, source_target_pairs={{0,1},{1,2},{2,3},{3,0},{4,5},{5,6},{6,7},{7,4},{8,9},{9,10},{10,1... | collective-permute-start | bytes 786440 | tf_op jit(solution)/shard_map/ppermute | solution.py:266
  47.8 23.4 %collective-permute-start.3 = (bf16[2,256,256]{2,1,0:T(8,128)(2,1)}, bf16[2,256,256]{2,1,0:T(8,128)(2,1)S(1)}, u32[]{:S(2)}, u32[]{:S(2)}) collective-permute-start(bf16[2,256,256]{2,1,0:T(8,128)(2,1)} %get-tuple-element.17), channel_id=1, source_target_pairs={{0,2},{1,3},{2,0},{3,1},{4,6},{5,7},{6,4},{7,5},{8,10},{9,11},{10,... | collective-permute-start | bytes 786440 | tf_op jit(solution)/shard_map/ppermute | solution.py:266
  51.1 20.1 %collective-permute-start.4 = (bf16[2,256,256]{2,1,0:T(8,128)(2,1)}, bf16[2,256,256]{2,1,0:T(8,128)(2,1)S(1)}, u32[]{:S(2)}, u32[]{:S(2)}) collective-permute-start(bf16[2,256,256]{2,1,0:T(8,128)(2,1)} %get-tuple-element.18), channel_id=1, source_target_pairs={{0,3},{1,0},{2,1},{3,2},{4,7},{5,4},{6,5},{7,6},{8,11},{9,8},{10,9... | collective-permute-start | bytes 786440 | tf_op jit(solution)/shard_map/ppermute | solution.py:266
  69.3 1.0 copy-start.4
  71.4 27.0 %all-to-all-start.3 = ((bf16[32,8,256]{2,1,0:T(8,128)(2,1)}), bf16[32,8,256]{2,1,0:T(8,128)(2,1)S(1)}, u32[]{:S(2)}, u32[]{:S(2)}) async-start(bf16[32,8,256]{2,1,0:T(8,128)(2,1)} %bitcast.7), calls=%async_computation.3 | async-start | bytes 262144 | tf_op jit(solution)/shard_map/all_to_all | solution.py:330
  82.5 16.1 %collective-permute-start.5 = (bf16[256,256]{1,0:T(8,128)(2,1)S(1)}, bf16[256,256]{1,0:T(8,128)(2,1)S(1)}, u32[]{:S(2)}, u32[]{:S(2)}) collective-permute-start(bf16[256,256]{1,0:T(8,128)(2,1)S(1)} %add_bitcast_fusion), channel_id=1, source_target_pairs={{0,8},{1,9},{2,10},{3,11},{4,12},{5,13},{6,14},{7,15},{8,0},{9,1},... | collective-permute-start | bytes 393224 | tf_op jit(solution)/shard_map/ppermute | solution.py:266

commit v3 on v2

v3 whole, which is shorter than its diff:
```python
import math

import jax
import jax.numpy as jnp
from jax import lax
from jax.experimental import pallas as pl
from jax.experimental.pallas import tpu as pltpu
from jax.sharding import PartitionSpec as P

NEG_FILL = -1e30
SIDE = 4


def torus_place():
    tensor = lax.axis_index("tensor")
    y, x = tensor // SIDE, lax.rem(tensor, SIDE)
    odd = lax.rem(lax.axis_index("dp"), 2)
    pair, line = y + odd * (x - y), x + odd * (y - x)
    pair_stride = SIDE + odd * (1 - SIDE)
    return pair, line, pair_stride, SIDE + 1 - pair_stride


def attend_kernel(
    fill_ref, queries_ref, keys_ref, values_ref, out_ref,
    query_buf, key_buf, value_buf, score_buf, weight_buf, grouped_buf,
    query_sem, key_sem, value_sem,
):
    requests, steps, heads, head_dim = query_buf.shape
    kv_heads, cache_len = key_buf.shape[1], key_buf.shape[2]
    per_group = heads // kv_heads
    group_rows = steps * per_group
    query_copy = pltpu.make_async_copy(queries_ref, query_buf, query_sem)
    key_copies = [
        pltpu.make_async_copy(keys_ref.at[r], key_buf.at[r], key_sem.at[r]) for r in range(requests)
    ]
    value_copies = [
        pltpu.make_async_copy(values_ref.at[r], value_buf.at[r], value_sem.at[r])
        for r in range(requests)
    ]
    query_copy.start()
    for copy in key_copies:
        copy.start()
    position = lax.broadcasted_iota(jnp.int32, (group_rows, cache_len), 1)
    step_of = lax.broadcasted_iota(jnp.int32, (group_rows, cache_len), 0) // per_group
    reach = position + steps - step_of
    query_copy.wait()
    for r in range(requests):
        every = query_buf[r].astype(jnp.float32)
        key_copies[r].wait()
        value_copies[r].start()
        for k in range(kv_heads):
            grouped = every[:, k * per_group : (k + 1) * per_group, :]
            grouped = grouped.reshape(group_rows, head_dim).astype(jnp.bfloat16)
            score_buf[r * kv_heads + k] = lax.dot_general(
                grouped,
                key_buf[r, k],
                (((1,), (1,)), ((), ())),
                preferred_element_type=jnp.float32,
            )
    for r in range(requests):
        valid = reach <= fill_ref[r]
        for k in range(kv_heads):
            scores = score_buf[r * kv_heads + k] * (1.0 / math.sqrt(head_dim))
            scores = jnp.where(valid, scores, NEG_FILL)
            raised = jnp.exp(scores - jnp.max(scores, axis=1, keepdims=True))
            weights = raised * (1.0 / jnp.sum(raised, axis=1, keepdims=True))
            weight_buf[r * kv_heads + k] = weights.astype(jnp.bfloat16)
    for r in range(requests):
        value_copies[r].wait()
        for k in range(kv_heads):
            grouped_buf[k, r * group_rows : (r + 1) * group_rows] = jnp.dot(
                weight_buf[r * kv_heads + k], value_buf[r, k], preferred_element_type=jnp.float32
            ).astype(jnp.bfloat16)
    every_rows = requests * group_rows
    rows = requests * steps
    old = lax.broadcasted_iota(jnp.int32, (every_rows, every_rows), 1)
    new = lax.broadcasted_iota(jnp.int32, (every_rows, every_rows), 0)
    turn = (old == new % rows * per_group + new // rows).astype(jnp.bfloat16)
    for k in range(kv_heads):
        turned = jnp.dot(turn, grouped_buf[k], preferred_element_type=jnp.float32)
        turned = turned.astype(jnp.bfloat16)
        for g in range(per_group):
            block, at = k * (per_group // 2) + g // 2, g % 2 * head_dim
            piece = turned[g * rows : (g + 1) * rows]
            out_ref[block, :, at : at + head_dim] = piece


def attend(queries, cached_key_rows, cached_value_rows, cache_fill_length):
    requests, steps, heads, head_dim = queries.shape
    kv_heads, cache_len = cached_key_rows.shape[1:3]
    blocks, rows = heads // 2, requests * steps
    pairs, group_rows = requests * kv_heads, steps * heads // kv_heads
    distant = pl.BlockSpec(memory_space=pl.ANY)
    return pl.pallas_call(
        attend_kernel,
        in_specs=[pl.BlockSpec(memory_space=pltpu.SMEM)] + [distant] * 3,
        out_specs=pl.BlockSpec(memory_space=pltpu.VMEM),
        out_shape=jax.ShapeDtypeStruct((blocks, rows, 2 * head_dim), jnp.bfloat16),
        scratch_shapes=[
            pltpu.VMEM(queries.shape, jnp.bfloat16),
            pltpu.VMEM(cached_key_rows.shape, jnp.bfloat16),
            pltpu.VMEM(cached_value_rows.shape, jnp.bfloat16),
            pltpu.VMEM((pairs, group_rows, cache_len), jnp.float32),
            pltpu.VMEM((pairs, group_rows, cache_len), jnp.bfloat16),
            pltpu.VMEM((kv_heads, requests * group_rows, head_dim), jnp.bfloat16),
            pltpu.SemaphoreType.DMA,
            pltpu.SemaphoreType.DMA((requests,)),
            pltpu.SemaphoreType.DMA((requests,)),
        ],
        compiler_params=pltpu.CompilerParams(vmem_limit_bytes=60 * 1024 * 1024),
        cost_estimate=pl.CostEstimate(
            flops=4 * rows * heads * cache_len * head_dim,
            bytes_accessed=2 * 2 * cached_key_rows.size,
            transcendentals=rows * heads * cache_len,
        ),
        name="attend",
    )(cache_fill_length, queries, cached_key_rows, cached_value_rows)


def payload_kernel(rows_ref, slots_ref, locals_ref, out_ref):
    rows, width = rows_ref.shape
    slot = lax.broadcasted_iota(jnp.int32, (rows, rows), 0)
    hit = slot == slots_ref[...]
    out_ref[:, :width] = jnp.dot(
        hit.astype(jnp.bfloat16), rows_ref[...], preferred_element_type=jnp.float32
    ).astype(jnp.bfloat16)
    ids = jnp.sum(jnp.where(hit, locals_ref[...].astype(jnp.float32), 0.0), axis=1, keepdims=True)
    out_ref[:, width:] = jnp.broadcast_to(ids, (rows, out_ref.shape[1] - width)).astype(jnp.bfloat16)


def make_payload(head_rows, row_slots, row_locals):
    rows, width = head_rows.shape
    resident = pl.BlockSpec(memory_space=pltpu.VMEM)
    return pl.pallas_call(
        payload_kernel,
        in_specs=[resident] * 3,
        out_specs=resident,
        out_shape=jax.ShapeDtypeStruct((rows, width + 128), jnp.bfloat16),
        compiler_params=pltpu.CompilerParams(vmem_limit_bytes=16 * 1024 * 1024),
        cost_estimate=pl.CostEstimate(
            flops=2 * rows * rows * width, bytes_accessed=8 * rows * width, transcendentals=0
        ),
        name="make_payload",
    )(head_rows, row_slots, row_locals)


def project_kernel(rows_ref, wo_ref, *refs):
    out_refs, wo_buf, wo_sem = refs[:SIDE], refs[SIDE], refs[SIDE + 1]
    pair, line, pair_stride, line_stride = torus_place()
    width = wo_buf.shape[2]
    blocks = [(s, u) for s in (2, 1, 3, 0) for u in range(SIDE)]
    copies = []
    for i, (s, u) in enumerate(blocks):
        along, across = lax.rem(line + s, SIDE), lax.rem(pair + u, SIDE)
        at = pl.multiple_of((across * pair_stride + along * line_stride) * width, width)
        copies.append(
            pltpu.make_async_copy(wo_ref.at[:, pl.ds(at, width)], wo_buf.at[i], wo_sem.at[i])
        )
    for copy in copies:
        copy.start()
    for i, (s, u) in enumerate(blocks):
        copies[i].wait()
        part = jnp.dot(rows_ref[...], wo_buf[i], preferred_element_type=jnp.float32)
        out_refs[s][u] = part.astype(out_refs[s].dtype)


def project(head_rows, wo):
    rows, depth = head_rows.shape
    width = wo.shape[1] // (SIDE * SIDE)
    resident = pl.BlockSpec(memory_space=pltpu.VMEM)
    kinds = [jnp.float32] + [jnp.bfloat16] * (SIDE - 1)
    return pl.pallas_call(
        project_kernel,
        in_specs=[resident, pl.BlockSpec(memory_space=pl.ANY)],
        out_specs=[resident for _ in kinds],
        out_shape=[jax.ShapeDtypeStruct((SIDE, rows, width), kind) for kind in kinds],
        scratch_shapes=[
            pltpu.VMEM((SIDE * SIDE, depth, width), wo.dtype),
            pltpu.SemaphoreType.DMA((SIDE * SIDE,)),
        ],
        compiler_params=pltpu.CompilerParams(vmem_limit_bytes=24 * 1024 * 1024),
        cost_estimate=pl.CostEstimate(
            flops=2 * rows * depth * wo.shape[1],
            bytes_accessed=2 * wo.size + 3 * rows * wo.shape[1],
            transcendentals=0,
        ),
        name="project",
    )(head_rows, pltpu.with_memory_space_constraint(wo, pltpu.HBM))


def down_kernel(owned_ref, down_ref, out_ref, ids_ref, down_buf, down_sem):
    copy_down = pltpu.make_async_copy(down_ref, down_buf, down_sem)
    copy_down.start()
    rows, columns = owned_ref.shape[0], down_ref.shape[1]
    rank = out_ref.shape[1]
    adapters = down_ref.shape[0] // rank
    ids = jnp.transpose(owned_ref[:, columns:].astype(jnp.float32))[:8]
    ids_ref[...] = ids
    copy_down.wait()
    every = lax.dot_general(
        down_buf[...],
        owned_ref[:, :columns],
        (((1,), (1,)), ((), ())),
        preferred_element_type=jnp.float32,
    )
    adapter = lax.broadcasted_iota(jnp.int32, (adapters, rank, rows), 0).astype(jnp.float32)
    chosen = adapter == ids[:1].reshape(1, 1, rows)
    part = jnp.sum(jnp.where(chosen, every.reshape(adapters, rank, rows), 0.0), axis=0)
    for share in range(out_ref.shape[0]):
        out_ref[share] = part


def shrink_down(owned, down, shares, rank):
    rows = owned.shape[0]
    resident = pl.BlockSpec(memory_space=pltpu.VMEM)
    return pl.pallas_call(
        down_kernel,
        in_specs=[resident, pl.BlockSpec(memory_space=pl.ANY)],
        out_specs=[resident] * 2,
        scratch_shapes=[pltpu.VMEM(down.shape, down.dtype), pltpu.SemaphoreType.DMA],
        out_shape=[
            jax.ShapeDtypeStruct((shares, rank, rows), jnp.float32),
            jax.ShapeDtypeStruct((8, rows), jnp.float32),
        ],
        compiler_params=pltpu.CompilerParams(vmem_limit_bytes=16 * 1024 * 1024),
        cost_estimate=pl.CostEstimate(
            flops=2 * rows * down.size, bytes_accessed=4 * down.size, transcendentals=0
        ),
        name="shrink_down",
    )(owned, pltpu.with_memory_space_constraint(down, pltpu.HBM))


def up_kernel(partials_ref, ids_ref, up_ref, out_ref, up_buf, up_sem):
    copy_up = pltpu.make_async_copy(up_ref, up_buf, up_sem)
    copy_up.start()
    shares, rank, rows = partials_ref.shape
    adapters = up_ref.shape[0] // rank
    shrink = partials_ref[0]
    for share in range(1, shares):
        shrink += partials_ref[share]
    shrink = shrink.astype(jnp.bfloat16).astype(jnp.float32)
    adapter = lax.broadcasted_iota(jnp.int32, (adapters, rank, rows), 0).astype(jnp.float32)
    chosen = adapter == ids_ref[:1].reshape(1, 1, rows)
    spread = jnp.where(chosen, shrink.reshape(1, rank, rows), 0.0)
    copy_up.wait()
    out_ref[...] = lax.dot_general(
        spread.reshape(adapters * rank, rows).astype(jnp.bfloat16),
        up_buf[...],
        (((0,), (0,)), ((), ())),
        preferred_element_type=jnp.float32,
    ).astype(jnp.bfloat16)


def expand_up(partials, ids, up):
    rows = partials.shape[2]
    resident = pl.BlockSpec(memory_space=pltpu.VMEM)
    return pl.pallas_call(
        up_kernel,
        in_specs=[resident, resident, pl.BlockSpec(memory_space=pl.ANY)],
        out_specs=resident,
        scratch_shapes=[pltpu.VMEM(up.shape, up.dtype), pltpu.SemaphoreType.DMA],
        out_shape=jax.ShapeDtypeStruct((rows, up.shape[1]), jnp.bfloat16),
        compiler_params=pltpu.CompilerParams(vmem_limit_bytes=16 * 1024 * 1024),
        cost_estimate=pl.CostEstimate(
            flops=2 * rows * up.size, bytes_accessed=4 * up.size, transcendentals=0
        ),
        name="expand_up",
    )(partials, ids, pltpu.with_memory_space_constraint(up, pltpu.HBM))


def finish_kernel(slots_ref, returned_ref, base_ref, *refs):
    across_refs, out_ref = refs[:-1], refs[-1]
    rows = returned_ref.shape[0]
    slot = lax.broadcasted_iota(jnp.int32, (rows, rows), 0)
    to_slots = (slot == slots_ref[...]).astype(jnp.bfloat16)
    delta = lax.dot_general(
        to_slots, returned_ref[...], (((0,), (0,)), ((), ())), preferred_element_type=jnp.float32
    )
    total = base_ref[...] + delta
    for across_ref in across_refs:
        total += across_ref[...].astype(jnp.float32)
    out_ref[...] = total.reshape(out_ref.shape).astype(out_ref.dtype)


def finish(row_slots, returned, base, across, out_shape):
    resident = pl.BlockSpec(memory_space=pltpu.VMEM)
    return pl.pallas_call(
        finish_kernel,
        in_specs=[resident] * (3 + len(across)),
        out_specs=resident,
        out_shape=jax.ShapeDtypeStruct(out_shape, jnp.bfloat16),
        compiler_params=pltpu.CompilerParams(vmem_limit_bytes=16 * 1024 * 1024),
        cost_estimate=pl.CostEstimate(
            flops=2 * returned.size * returned.shape[0],
            bytes_accessed=8 * returned.size,
            transcendentals=0,
        ),
        name="finish",
    )(row_slots, returned, base, *across)


def move(value, owners, target):
    pairs = []
    for d in range(owners):
        for pair in range(SIDE):
            for line in range(SIDE):
                to_pair, to_line = target(pair, line)
                if d % 2 == 0:
                    here, there = pair * SIDE + line, to_pair * SIDE + to_line
                else:
                    here, there = line * SIDE + pair, to_line * SIDE + to_pair
                pairs.append((d * SIDE * SIDE + here, d * SIDE * SIDE + there))
    return lax.ppermute(value, ("dp", "tensor"), pairs)


def after(value, *earlier):
    return lax.optimization_barrier((value,) + earlier)[0]


def on_device(
    queries,
    cached_key_rows,
    cached_value_rows,
    cache_fill_length,
    request_adapters,
    wo,
    adapter_down_weight,
    adapter_up_weight,
):
    owners = lax.axis_size("dp")
    shares = lax.axis_size("tensor")
    group_size = request_adapters.shape[0]
    owner_partial, rank, width = adapter_down_weight.shape
    capacity = group_size // owners
    steps = queries.shape[1]
    rows = group_size * steps

    owner_ids = request_adapters // owner_partial
    local_ids = request_adapters % owner_partial
    order = jnp.arange(group_size, dtype=jnp.int32)
    earlier = (owner_ids[:, None] == owner_ids[None, :]) & (order[:, None] > order[None, :])
    slots = owner_ids * capacity + jnp.sum(earlier.astype(jnp.int32), axis=1)
    row_slots = (slots[:, None] * steps + jnp.arange(steps, dtype=jnp.int32)).reshape(1, rows)
    row_locals = jnp.repeat(local_ids, steps)[None, :]

    attended = attend(queries, cached_key_rows, cached_value_rows, cache_fill_length)
    head_rows = lax.all_to_all(attended, "tensor", 0, 0, tiled=True).reshape(rows, width)

    payload = make_payload(head_rows, row_slots, row_locals)
    own, *others = project(after(head_rows, payload), wo)
    arrived = [
        move(part, owners, lambda pair, line, s=s: (pair, (line + s) % SIDE))
        for s, part in enumerate(others, start=1)
    ]
    owned = lax.all_to_all(
        payload.reshape(owners, capacity * steps, width + 128), "dp", 0, 0, tiled=True
    ).reshape(rows, width + 128)
    partial_shrink, ids = shrink_down(
        after(owned, own), adapter_down_weight.reshape(owner_partial * rank, width), shares, rank
    )
    partials = lax.all_to_all(partial_shrink, "tensor", 0, 0, tiled=True)
    delta = expand_up(partials, ids, adapter_up_weight.reshape(owner_partial * rank, width))
    returned = lax.all_to_all(
        delta.reshape(owners, capacity * steps, width), "dp", 0, 0, tiled=True
    ).reshape(rows, width)

    along_line = [
        own[u] + sum(part[u].astype(jnp.float32) for part in arrived) for u in range(SIDE)
    ]
    across = [
        move(
            along_line[u].astype(jnp.bfloat16),
            owners,
            lambda pair, line, u=u: ((pair + u) % SIDE, line),
        )
        for u in range(1, SIDE)
    ]
    return finish(
        row_slots, returned, along_line[0], across, (group_size, steps, width)
    )


def solution(mesh):
    in_specs = (
        P(("dp", "tensor"), None, None, None),
        P(("dp", "tensor"), None, None, None),
        P(("dp", "tensor"), None, None, None),
        P(("dp", "tensor")),
        P("dp"),
        P("tensor", None),
        P("dp", None, "tensor"),
        P("dp", None, "tensor"),
    )
    out_specs = P("dp", None, "tensor")
    return jax.shard_map(
        on_device, mesh=mesh, in_specs=in_specs, out_specs=out_specs, check_vma=False
    )
```

time: 100 us -> 97.7 us (0.977)
  Pallas kernels: 10.4 us -> 14.8 us
  local copies, waits for them, and re-layouts: 3.92 us -> 0.3 us
  starting transfers between devices: 53.8 us -> 52.2 us
  other arithmetic: 0.43 us -> 1.82 us
  matrix products: 1.18 us -> 0 us
  blocking collectives: 11.3 us -> 10.3 us
    all_to_all x1, waiting for transfers between devices: 11.8 us -> 0.54 us  [on_device(): lax.all_to_all(delta.reshape(owners, capacity * steps, width), 'dp', 0, 0...]
    pallas_call x4 -> x5, Pallas kernels: 4.94 us -> 9.53 us  [the longest x1 4.56 us: project(): pl.pallas_call(project_kernel, in_specs=[resident, pl.BlockSpec(memory_sp...]
    all_to_all x1, waiting for transfers between devices: 1.75 us -> 6.25 us  [on_device(): lax.all_to_all(attended, 'tensor', 0, 0, tiled=True).reshape(rows, width)]
    ppermute x6, waiting for transfers between devices: 0.86 us -> 5.02 us  [move(): return lax.ppermute(value, ('dp', 'tensor'), pairs)]
    unnamed x12 -> x2, local copies, waits for them, and re-layouts: 2.81 us -> 0.01 us
    all_to_all x1, waiting for transfers between devices: 3.61 us -> 5.56 us  [on_device(): lax.all_to_all(payload.reshape(owners, capacity * steps, width + 128), 'd...]
    add x2 -> x1, other arithmetic: 0.12 us -> 1.56 us  [on_device(): own[u] + sum((part[u].astype(jnp.float32) for part in arrived))]
    dot_general x2 -> x0, matrix products: 1.18 us -> none  [the longest x1 0.92 us: on_device(): jnp.dot(to_slots, jnp.concatenate([head_rows, id_lanes], axis=1), preferr...]
  transfers between devices with their start and end apart: 9 -> 9, of which waited for: 4 -> 5; matrix products, arithmetic and copies ran while one was open for 2% -> 2% of each run, Pallas kernels for 5% -> 8%
where the time goes in v3:
time: 97.7 us; the launch traced here: 97 us
  starting transfers between devices  52.2 us (53%)
  waiting for transfers between devices  17.4 us (18%)
  Pallas kernels  14.8 us (15%)
  blocking collectives  10.3 us (11%)
  other arithmetic  1.82 us (2%)
    all_to_all x1, starting transfers between devices, on_device(): lax.all_to_all(payload.reshape(owners, capacity * steps, width + 128), 'd...  17.3 us
    ppermute x6, starting transfers between devices, move(): return lax.ppermute(value, ('dp', 'tensor'), pairs)  17.1 us
    all_to_all x1, blocking collectives, on_device(): partials = lax.all_to_all(partial_shrink, 'tensor', 0, 0, tiled=True)  10.3 us
    all_to_all x1, starting transfers between devices, on_device(): lax.all_to_all(delta.reshape(owners, capacity * steps, width), 'dp', 0, 0...  10.1 us
    all_to_all x1, starting transfers between devices, on_device(): lax.all_to_all(attended, 'tensor', 0, 0, tiled=True).reshape(rows, width)  7.59 us
    all_to_all x1, waiting for transfers between devices, on_device(): lax.all_to_all(attended, 'tensor', 0, 0, tiled=True).reshape(rows, width)  6.25 us
    all_to_all x1, waiting for transfers between devices, on_device(): lax.all_to_all(payload.reshape(owners, capacity * steps, width + 128), 'd...  5.56 us
    pallas_call x1, Pallas kernels, attend(): pl.pallas_call(attend_kernel, in_specs=[pl.BlockSpec(memory_space=pltpu.S...  5.27 us
  transfers between devices with their start and end apart: 9, of which 5 were waited for; matrix products, arithmetic and copies ran while one was open for 2% of the time, Pallas kernels for 8%

profile of v3, /device:TPU:1, one launch (start us, length us, event | category | flops | bytes accessed | tf_op | source)
XLA Modules:
  0.0 97.0 jit_solution(4873911032361715714)
XLA Ops:
  0.0 5.3 %attend.1 = bf16[16,16,256]{2,1,0:T(8,128)(2,1)} custom-call(s32[4]{0:T(128)} %fill_ref.1, bf16[4,4,32,128]{3,2,1,0:T(8,128)(2,1)} %queries_ref.1, bf16[4,4,512,128]{3,2,1,0:T(8,128)(2,1)} %keys_ref.1, bf16[4,4,512,128]{3,2,1,0:T(8,128)(2,1)} %values_ref.1), custom_call_target="tpu_custom_call" | custom-call | flops 134217728 | bytes 4194304 | tf_op jit(solution)/shard_map/attend/pallas_call | solution.py:94
  5.3 7.6 %all-to-all-start = ((bf16[16,16,256]{2,1,0:T(8,128)(2,1)}), bf16[16,16,256]{2,1,0:T(8,128)(2,1)S(1)}, u32[]{:S(2)}, u32[]{:S(2)}) async-start(bf16[16,16,256]{2,1,0:T(8,128)(2,1)} %attend.1), calls=%async_computation | async-start | bytes 262144 | tf_op jit(solution)/shard_map/all_to_all | solution.py:347
  12.9 0.0 copy-done
  12.9 0.2 convert_reduce_fusion
  13.1 0.1 iota_add_fusion
  13.2 0.1 add.92.slots_ref
  13.3 0.1 broadcast_in_dim.2
  13.4 0.1 broadcast_in_dim_reshape.3.locals_ref
  13.5 6.2 %all-to-all-done = bf16[16,16,256]{2,1,0:T(8,128)(2,1)S(1)} async-done(((bf16[16,16,256]{2,1,0:T(8,128)(2,1)}), bf16[16,16,256]{2,1,0:T(8,128)(2,1)S(1)}, u32[]{:S(2)}, u32[]{:S(2)}) %all-to-all-start) | async-done | bytes 131104 | tf_op jit(solution)/shard_map/all_to_all | solution.py:347
  19.7 0.9 make_payload.1
  20.6 17.3 %all-to-all-start.1 = ((bf16[32,8,384]{2,1,0:T(8,128)(2,1)}), bf16[32,8,384]{2,1,0:T(8,128)(2,1)S(1)}, u32[]{:S(2)}, u32[]{:S(2)}) async-start(bf16[32,8,384]{2,1,0:T(8,128)(2,1)} %bitcast.1), calls=%async_computation.1 | async-start | bytes 393216 | tf_op jit(solution)/shard_map/all_to_all | solution.py:355
  38.0 4.6 %project.1 = (f32[4,256,256]{2,1,0:T(8,128)S(1)}, bf16[4,256,256]{2,1,0:T(8,128)(2,1)S(1)}, bf16[4,256,256]{2,1,0:T(8,128)(2,1)S(1)}, bf16[4,256,256]{2,1,0:T(8,128)(2,1)S(1)}) custom-call(bf16[256,256]{1,0:T(8,128)(2,1)S(1)} %bitcast.16, bf16[256,4096]{1,0:T(8,128)(2,1)} %wo_ref.1), custom_call_target="tpu_custom_call" | custom-call | flops 536870912 | bytes 5242880 | tf_op jit(solution)/shard_map/project/pallas_call | solution.py:172
  42.5 1.9 %collective-permute-start = (bf16[4,256,256]{2,1,0:T(8,128)(2,1)S(1)}, bf16[4,256,256]{2,1,0:T(8,128)(2,1)S(1)}, u32[]{:S(2)}, u32[]{:S(2)}) collective-permute-start(bf16[4,256,256]{2,1,0:T(8,128)(2,1)S(1)} %get-tuple-element.18), channel_id=1, source_target_pairs={{0,1},{1,2},{2,3},{3,0},{4,5},{5,6},{6,7},{7,4},{8,9},{9,10},{10,1... | collective-permute-start | bytes 1572872 | tf_op jit(solution)/shard_map/ppermute | solution.py:313
  44.5 3.7 %collective-permute-start.1 = (bf16[4,256,256]{2,1,0:T(8,128)(2,1)S(1)}, bf16[4,256,256]{2,1,0:T(8,128)(2,1)}, u32[]{:S(2)}, u32[]{:S(2)}) collective-permute-start(bf16[4,256,256]{2,1,0:T(8,128)(2,1)S(1)} %get-tuple-element.19), channel_id=1, source_target_pairs={{0,2},{1,3},{2,0},{3,1},{4,6},{5,7},{6,4},{7,5},{8,10},{9,11},{10,... | collective-permute-start | bytes 1572872 | tf_op jit(solution)/shard_map/ppermute | solution.py:313
  48.1 2.9 %collective-permute-start.2 = (bf16[4,256,256]{2,1,0:T(8,128)(2,1)S(1)}, bf16[4,256,256]{2,1,0:T(8,128)(2,1)}, u32[]{:S(2)}, u32[]{:S(2)}) collective-permute-start(bf16[4,256,256]{2,1,0:T(8,128)(2,1)S(1)} %get-tuple-element.20), channel_id=1, source_target_pairs={{0,3},{1,0},{2,1},{3,2},{4,7},{5,4},{6,5},{7,6},{8,11},{9,8},{10,9... | collective-permute-start | bytes 1572872 | tf_op jit(solution)/shard_map/ppermute | solution.py:313
  51.0 5.6 %all-to-all-done.1 = bf16[32,8,384]{2,1,0:T(8,128)(2,1)S(1)} async-done(((bf16[32,8,384]{2,1,0:T(8,128)(2,1)}), bf16[32,8,384]{2,1,0:T(8,128)(2,1)S(1)}, u32[]{:S(2)}, u32[]{:S(2)}) %all-to-all-start.1) | async-done | bytes 196640 | tf_op jit(solution)/shard_map/all_to_all | solution.py:355
  56.6 1.3 %shrink_down.1 = (f32[16,16,256]{2,1,0:T(8,128)S(1)}, f32[8,256]{1,0:T(8,128)S(1)}) custom-call(bf16[256,384]{1,0:T(8,128)(2,1)S(1)} %bitcast.17, bf16[512,256]{1,0:T(8,128)(2,1)} %bitcast.19), custom_call_target="tpu_custom_call" | custom-call | flops 67108864 | bytes 524288 | tf_op jit(solution)/shard_map/shrink_down/pallas_call | solution.py:216
  57.9 10.3 %all_to_all.20.partials_ref = f32[16,16,256]{2,1,0:T(8,128)S(1)} all-to-all(f32[16,16,256]{2,1,0:T(8,128)S(1)} %get-tuple-element.16), channel_id=1, replica_groups=mesh['dp'=32,'tensor'=16] {'tensor'}, dimensions={0} | all-to-all | bytes 524288 | tf_op jit(solution)/shard_map/all_to_all | solution.py:361
  68.2 1.9 %expand_up.1 = bf16[256,256]{1,0:T(8,128)(2,1)} custom-call(f32[16,16,256]{2,1,0:T(8,128)S(1)} %all_to_all.20.partials_ref, f32[8,256]{1,0:T(8,128)S(1)} %get-tuple-element.17.ids_ref, bf16[512,256]{1,0:T(8,128)(2,1)} %bitcast.20), custom_call_target="tpu_custom_call" | custom-call | flops 67108864 | bytes 524288 | tf_op jit(solution)/shard_map/expand_up/pallas_call | solution.py:257
  70.1 10.1 %all-to-all-start.3 = ((bf16[32,8,256]{2,1,0:T(8,128)(2,1)}), bf16[32,8,256]{2,1,0:T(8,128)(2,1)S(1)}, u32[]{:S(2)}, u32[]{:S(2)}) async-start(bf16[32,8,256]{2,1,0:T(8,128)(2,1)} %bitcast.5), calls=%async_computation.3 | async-start | bytes 262144 | tf_op jit(solution)/shard_map/all_to_all | solution.py:363
  80.2 0.0 collective-permute-done
  80.2 0.0 collective-permute-done.1
  80.2 0.0 collective-permute-done.2
  80.2 1.6 %fusion.2 = (bf16[256,256]{1,0:T(8,128)(2,1)S(1)}, bf16[256,256]{1,0:T(8,128)(2,1)S(1)}, bf16[256,256]{1,0:T(8,128)(2,1)S(1)}, f32[256,256]{1,0:T(8,128)S(1)}) fusion(f32[4,256,256]{2,1,0:T(8,128)S(1)} %get-tuple-element.14, bf16[4,256,256]{2,1,0:T(8,128)(2,1)} %collective-permute-done.2, bf16[4,256,256]{2,1,0:T(8,128)(2,1)} %collective-permute-done.1, ...), kind=kLoop, calls=%fused_computation.6 | loop fusion | flops 1769472 | bytes 3276800 | tf_op jit(solution)/shard_map/add | solution.py:368
  81.8 4.3 %collective-permute-start.5 = (bf16[256,256]{1,0:T(8,128)(2,1)S(1)}, bf16[256,256]{1,0:T(8,128)(2,1)S(1)}, u32[]{:S(2)}, u32[]{:S(2)}) collective-permute-start(bf16[256,256]{1,0:T(8,128)(2,1)S(1)} %get-tuple-element.21), channel_id=1, source_target_pairs={{0,12},{1,13},{2,14},{3,15},{4,0},{5,1},{6,2},{7,3},{8,4},{9,5},{1... | collective-permute-start | bytes 393224 | tf_op jit(solution)/shard_map/ppermute | solution.py:313
  86.0 2.2 %collective-permute-start.4 = (bf16[256,256]{1,0:T(8,128)(2,1)S(1)}, bf16[256,256]{1,0:T(8,128)(2,1)S(1)}, u32[]{:S(2)}, u32[]{:S(2)}) collective-permute-start(bf16[256,256]{1,0:T(8,128)(2,1)S(1)} %get-tuple-element.22), channel_id=1, source_target_pairs={{0,8},{1,9},{2,10},{3,11},{4,12},{5,13},{6,14},{7,15},{8,0},{9,1},... | collective-permute-start | bytes 393224 | tf_op jit(solution)/shard_map/ppermute | solution.py:313
  88.3 2.2 %collective-permute-start.3 = (bf16[256,256]{1,0:T(8,128)(2,1)S(1)}, bf16[256,256]{1,0:T(8,128)(2,1)S(1)}, u32[]{:S(2)}, u32[]{:S(2)}) collective-permute-start(bf16[256,256]{1,0:T(8,128)(2,1)S(1)} %get-tuple-element.23), channel_id=1, source_target_pairs={{0,4},{1,5},{2,6},{3,7},{4,8},{5,9},{6,10},{7,11},{8,12},{9,13},{1... | collective-permute-start | bytes 393224 | tf_op jit(solution)/shard_map/ppermute | solution.py:313
  90.5 0.0 collective-permute-done.5.refs_2_
  90.5 3.1 %collective-permute-done.4.refs_1_ = bf16[256,256]{1,0:T(8,128)(2,1)S(1)} collective-permute-done((bf16[256,256]{1,0:T(8,128)(2,1)S(1)}, bf16[256,256]{1,0:T(8,128)(2,1)S(1)}, u32[]{:S(2)}, u32[]{:S(2)}) %collective-permute-start.4) | collective-permute-done | bytes 131104 | tf_op jit(solution)/shard_map/ppermute | solution.py:313
  93.6 1.9 %collective-permute-done.3.refs_0_ = bf16[256,256]{1,0:T(8,128)(2,1)S(1)} collective-permute-done((bf16[256,256]{1,0:T(8,128)(2,1)S(1)}, bf16[256,256]{1,0:T(8,128)(2,1)S(1)}, u32[]{:S(2)}, u32[]{:S(2)}) %collective-permute-start.3) | collective-permute-done | bytes 131104 | tf_op jit(solution)/shard_map/ppermute | solution.py:313
  95.5 0.5 all-to-all-done.3
  96.0 0.9 finish.1
  (3 shorter events, 0.0 us)
Async XLA Ops:
  0.0 12.9 %copy-start = (s32[64]{0:T(128)S(1)}, s32[64]{0:T(128)}, u32[]{:S(2)}) copy-start(s32[64]{0:T(128)} %param.12) | copy-start | bytes 772
  5.3 14.4 %all-to-all-start = ((bf16[16,16,256]{2,1,0:T(8,128)(2,1)}), bf16[16,16,256]{2,1,0:T(8,128)(2,1)S(1)}, u32[]{:S(2)}, u32[]{:S(2)}) async-start(bf16[16,16,256]{2,1,0:T(8,128)(2,1)} %attend.1), calls=%async_computation | async-start | bytes 262144 | tf_op jit(solution)/shard_map/all_to_all | solution.py:347
  20.6 36.0 %all-to-all-start.1 = ((bf16[32,8,384]{2,1,0:T(8,128)(2,1)}), bf16[32,8,384]{2,1,0:T(8,128)(2,1)S(1)}, u32[]{:S(2)}, u32[]{:S(2)}) async-start(bf16[32,8,384]{2,1,0:T(8,128)(2,1)} %bitcast.1), calls=%async_computation.1 | async-start | bytes 393216 | tf_op jit(solution)/shard_map/all_to_all | solution.py:355
  42.5 37.7 %collective-permute-start = (bf16[4,256,256]{2,1,0:T(8,128)(2,1)S(1)}, bf16[4,256,256]{2,1,0:T(8,128)(2,1)S(1)}, u32[]{:S(2)}, u32[]{:S(2)}) collective-permute-start(bf16[4,256,256]{2,1,0:T(8,128)(2,1)S(1)} %get-tuple-element.18), channel_id=1, source_target_pairs={{0,1},{1,2},{2,3},{3,0},{4,5},{5,6},{6,7},{7,4},{8,9},{9,10},{10,1... | collective-permute-start | bytes 1572872 | tf_op jit(solution)/shard_map/ppermute | solution.py:313
  44.5 35.7 %collective-permute-start.1 = (bf16[4,256,256]{2,1,0:T(8,128)(2,1)S(1)}, bf16[4,256,256]{2,1,0:T(8,128)(2,1)}, u32[]{:S(2)}, u32[]{:S(2)}) collective-permute-start(bf16[4,256,256]{2,1,0:T(8,128)(2,1)S(1)} %get-tuple-element.19), channel_id=1, source_target_pairs={{0,2},{1,3},{2,0},{3,1},{4,6},{5,7},{6,4},{7,5},{8,10},{9,11},{10,... | collective-permute-start | bytes 1572872 | tf_op jit(solution)/shard_map/ppermute | solution.py:313
  48.1 32.1 %collective-permute-start.2 = (bf16[4,256,256]{2,1,0:T(8,128)(2,1)S(1)}, bf16[4,256,256]{2,1,0:T(8,128)(2,1)}, u32[]{:S(2)}, u32[]{:S(2)}) collective-permute-start(bf16[4,256,256]{2,1,0:T(8,128)(2,1)S(1)} %get-tuple-element.20), channel_id=1, source_target_pairs={{0,3},{1,0},{2,1},{3,2},{4,7},{5,4},{6,5},{7,6},{8,11},{9,8},{10,9... | collective-permute-start | bytes 1572872 | tf_op jit(solution)/shard_map/ppermute | solution.py:313
  70.1 26.0 %all-to-all-start.3 = ((bf16[32,8,256]{2,1,0:T(8,128)(2,1)}), bf16[32,8,256]{2,1,0:T(8,128)(2,1)S(1)}, u32[]{:S(2)}, u32[]{:S(2)}) async-start(bf16[32,8,256]{2,1,0:T(8,128)(2,1)} %bitcast.5), calls=%async_computation.3 | async-start | bytes 262144 | tf_op jit(solution)/shard_map/all_to_all | solution.py:363
  81.8 8.7 %collective-permute-start.5 = (bf16[256,256]{1,0:T(8,128)(2,1)S(1)}, bf16[256,256]{1,0:T(8,128)(2,1)S(1)}, u32[]{:S(2)}, u32[]{:S(2)}) collective-permute-start(bf16[256,256]{1,0:T(8,128)(2,1)S(1)} %get-tuple-element.21), channel_id=1, source_target_pairs={{0,12},{1,13},{2,14},{3,15},{4,0},{5,1},{6,2},{7,3},{8,4},{9,5},{1... | collective-permute-start | bytes 393224 | tf_op jit(solution)/shard_map/ppermute | solution.py:313
  86.0 7.5 %collective-permute-start.4 = (bf16[256,256]{1,0:T(8,128)(2,1)S(1)}, bf16[256,256]{1,0:T(8,128)(2,1)S(1)}, u32[]{:S(2)}, u32[]{:S(2)}) collective-permute-start(bf16[256,256]{1,0:T(8,128)(2,1)S(1)} %get-tuple-element.22), channel_id=1, source_target_pairs={{0,8},{1,9},{2,10},{3,11},{4,12},{5,13},{6,14},{7,15},{8,0},{9,1},... | collective-permute-start | bytes 393224 | tf_op jit(solution)/shard_map/ppermute | solution.py:313
  88.3 7.2 %collective-permute-start.3 = (bf16[256,256]{1,0:T(8,128)(2,1)S(1)}, bf16[256,256]{1,0:T(8,128)(2,1)S(1)}, u32[]{:S(2)}, u32[]{:S(2)}) collective-permute-start(bf16[256,256]{1,0:T(8,128)(2,1)S(1)} %get-tuple-element.23), channel_id=1, source_target_pairs={{0,4},{1,5},{2,6},{3,7},{4,8},{5,9},{6,10},{7,11},{8,12},{9,13},{1... | collective-permute-start | bytes 393224 | tf_op jit(solution)/shard_map/ppermute | solution.py:313

commit v4 on v3

--- a/solution.py
+++ b/solution.py
@@ -8,6 +8,7 @@
 from jax.sharding import PartitionSpec as P
 
 NEG_FILL = -1e30
+FAR_FLOPS = 20_000_000_000
 SIDE = 4
 
 
@@ -120,12 +121,17 @@
 def payload_kernel(rows_ref, slots_ref, locals_ref, out_ref):
     rows, width = rows_ref.shape
     slot = lax.broadcasted_iota(jnp.int32, (rows, rows), 0)
-    hit = slot == slots_ref[...]
+    hit = (slot == slots_ref[...]).astype(jnp.bfloat16)
     out_ref[:, :width] = jnp.dot(
-        hit.astype(jnp.bfloat16), rows_ref[...], preferred_element_type=jnp.float32
+        hit, rows_ref[...], preferred_element_type=jnp.float32
     ).astype(jnp.bfloat16)
-    ids = jnp.sum(jnp.where(hit, locals_ref[...].astype(jnp.float32), 0.0), axis=1, keepdims=True)
-    out_ref[:, width:] = jnp.broadcast_to(ids, (rows, out_ref.shape[1] - width)).astype(jnp.bfloat16)
+    ids = locals_ref[...].astype(jnp.float32).astype(jnp.bfloat16)
+    out_ref[:, width:] = lax.dot_general(
+        hit,
+        jnp.broadcast_to(ids, (out_ref.shape[1] - width, rows)),
+        (((1,), (1,)), ((), ())),
+        preferred_element_type=jnp.float32,
+    ).astype(jnp.bfloat16)
 
 
 def make_payload(head_rows, row_slots, row_locals):
@@ -145,108 +151,106 @@
 
 
 def project_kernel(rows_ref, wo_ref, *refs):
-    out_refs, wo_buf, wo_sem = refs[:SIDE], refs[SIDE], refs[SIDE + 1]
+    own_ref, own_buf, own_sem = refs[0], refs[SIDE], refs[SIDE + 1]
+    out_refs = (own_buf,) + refs[1:SIDE]
     pair, line, pair_stride, line_stride = torus_place()
-    width = wo_buf.shape[2]
-    blocks = [(s, u) for s in (2, 1, 3, 0) for u in range(SIDE)]
-    copies = []
-    for i, (s, u) in enumerate(blocks):
-        along, across = lax.rem(line + s, SIDE), lax.rem(pair + u, SIDE)
-        at = pl.multiple_of((across * pair_stride + along * line_stride) * width, width)
-        copies.append(
-            pltpu.make_async_copy(wo_ref.at[:, pl.ds(at, width)], wo_buf.at[i], wo_sem.at[i])
-        )
-    for copy in copies:
-        copy.start()
-    for i, (s, u) in enumerate(blocks):
-        copies[i].wait()
-        part = jnp.dot(rows_ref[...], wo_buf[i], preferred_element_type=jnp.float32)
-        out_refs[s][u] = part.astype(out_refs[s].dtype)
+    width = rows_ref.shape[1]
+    for s, out_ref in enumerate(out_refs):
+        along = lax.rem(line + s, SIDE)
+        for u in range(SIDE):
+            across = lax.rem(pair + u, SIDE)
+            at = pl.multiple_of((across * pair_stride + along * line_stride) * width, width)
+            part = jnp.dot(
+                rows_ref[...], wo_ref[:, pl.ds(at, width)], preferred_element_type=jnp.float32
+            )
+            out_ref[u] = part.astype(out_ref.dtype)
+        if s == 0:
+            own_copy = pltpu.make_async_copy(own_buf, own_ref, own_sem)
+            own_copy.start()
+    own_copy.wait()
 
 
 def project(head_rows, wo):
     rows, depth = head_rows.shape
     width = wo.shape[1] // (SIDE * SIDE)
     resident = pl.BlockSpec(memory_space=pltpu.VMEM)
-    kinds = [jnp.float32] + [jnp.bfloat16] * (SIDE - 1)
     return pl.pallas_call(
         project_kernel,
-        in_specs=[resident, pl.BlockSpec(memory_space=pl.ANY)],
-        out_specs=[resident for _ in kinds],
-        out_shape=[jax.ShapeDtypeStruct((SIDE, rows, width), kind) for kind in kinds],
-        scratch_shapes=[
-            pltpu.VMEM((SIDE * SIDE, depth, width), wo.dtype),
-            pltpu.SemaphoreType.DMA((SIDE * SIDE,)),
-        ],
-        compiler_params=pltpu.CompilerParams(vmem_limit_bytes=24 * 1024 * 1024),
+        in_specs=[resident] * 2,
+        out_specs=[pl.BlockSpec(memory_space=pltpu.HBM)] + [resident] * (SIDE - 1),
+        out_shape=[pltpu.HBM((SIDE, rows, width), jnp.float32)]
+        + [jax.ShapeDtypeStruct((SIDE, rows, width), jnp.bfloat16)] * (SIDE - 1),
+        scratch_shapes=[pltpu.VMEM((SIDE, rows, width), jnp.float32), pltpu.SemaphoreType.DMA],
+        compiler_params=pltpu.CompilerParams(vmem_limit_bytes=16 * 1024 * 1024),
         cost_estimate=pl.CostEstimate(
             flops=2 * rows * depth * wo.shape[1],
             bytes_accessed=2 * wo.size + 3 * rows * wo.shape[1],
             transcendentals=0,
         ),
         name="project",
-    )(head_rows, pltpu.with_memory_space_constraint(wo, pltpu.HBM))
-
-
-def down_kernel(owned_ref, down_ref, out_ref, ids_ref, down_buf, down_sem):
-    copy_down = pltpu.make_async_copy(down_ref, down_buf, down_sem)
-    copy_down.start()
+    )(head_rows, wo)
+
+
+def down_kernel(owned_ref, down_ref, up_ref, out_ref, ids_ref):
+    del up_ref
     rows, columns = owned_ref.shape[0], down_ref.shape[1]
     rank = out_ref.shape[1]
     adapters = down_ref.shape[0] // rank
-    ids = jnp.transpose(owned_ref[:, columns:].astype(jnp.float32))[:8]
-    ids_ref[...] = ids
-    copy_down.wait()
     every = lax.dot_general(
-        down_buf[...],
+        down_ref[...],
         owned_ref[:, :columns],
         (((1,), (1,)), ((), ())),
         preferred_element_type=jnp.float32,
     )
+    ids = owned_ref[:, columns:].astype(jnp.float32)
+    ids_ref[...] = ids
     adapter = lax.broadcasted_iota(jnp.int32, (adapters, rank, rows), 0).astype(jnp.float32)
-    chosen = adapter == ids[:1].reshape(1, 1, rows)
+    chosen = adapter == jnp.transpose(ids)[:1].reshape(1, 1, rows)
     part = jnp.sum(jnp.where(chosen, every.reshape(adapters, rank, rows), 0.0), axis=0)
     for share in range(out_ref.shape[0]):
         out_ref[share] = part
 
 
-def shrink_down(owned, down, shares, rank):
+def shrink_down(owned, down, up, shares, rank):
     rows = owned.shape[0]
+    lanes = owned.shape[1] - down.shape[1]
     resident = pl.BlockSpec(memory_space=pltpu.VMEM)
     return pl.pallas_call(
         down_kernel,
-        in_specs=[resident, pl.BlockSpec(memory_space=pl.ANY)],
+        in_specs=[resident] * 3,
         out_specs=[resident] * 2,
-        scratch_shapes=[pltpu.VMEM(down.shape, down.dtype), pltpu.SemaphoreType.DMA],
         out_shape=[
             jax.ShapeDtypeStruct((shares, rank, rows), jnp.float32),
-            jax.ShapeDtypeStruct((8, rows), jnp.float32),
+            jax.ShapeDtypeStruct((rows, lanes), jnp.float32),
         ],
         compiler_params=pltpu.CompilerParams(vmem_limit_bytes=16 * 1024 * 1024),
         cost_estimate=pl.CostEstimate(
             flops=2 * rows * down.size, bytes_accessed=4 * down.size, transcendentals=0
         ),
         name="shrink_down",
-    )(owned, pltpu.with_memory_space_constraint(down, pltpu.HBM))
-
-
-def up_kernel(partials_ref, ids_ref, up_ref, out_ref, up_buf, up_sem):
-    copy_up = pltpu.make_async_copy(up_ref, up_buf, up_sem)
-    copy_up.start()
+    )(owned, down, up)
+
+
+def up_kernel(partials_ref, ids_ref, up_ref, out_ref):
     shares, rank, rows = partials_ref.shape
-    adapters = up_ref.shape[0] // rank
+    maps = up_ref.shape[0]
+    lanes = ids_ref.shape[1]
     shrink = partials_ref[0]
     for share in range(1, shares):
         shrink += partials_ref[share]
-    shrink = shrink.astype(jnp.bfloat16).astype(jnp.float32)
-    adapter = lax.broadcasted_iota(jnp.int32, (adapters, rank, rows), 0).astype(jnp.float32)
-    chosen = adapter == ids_ref[:1].reshape(1, 1, rows)
-    spread = jnp.where(chosen, shrink.reshape(1, rank, rows), 0.0)
-    copy_up.wait()
-    out_ref[...] = lax.dot_general(
-        spread.reshape(adapters * rank, rows).astype(jnp.bfloat16),
-        up_buf[...],
+    fold = lax.broadcasted_iota(jnp.int32, (rank, maps), 1) % rank
+    fold = (fold == lax.broadcasted_iota(jnp.int32, (rank, maps), 0)).astype(jnp.bfloat16)
+    spread = lax.dot_general(
+        shrink.astype(jnp.bfloat16),
+        fold,
         (((0,), (0,)), ((), ())),
+        preferred_element_type=jnp.float32,
+    )
+    ids = jnp.concatenate([ids_ref[...]] * (maps // lanes), axis=1)
+    adapter = (lax.broadcasted_iota(jnp.int32, (1, maps), 1) // rank).astype(jnp.float32)
+    out_ref[...] = jnp.dot(
+        jnp.where(adapter == ids, spread, 0.0).astype(jnp.bfloat16),
+        up_ref[...],
         preferred_element_type=jnp.float32,
     ).astype(jnp.bfloat16)
 
@@ -256,16 +260,15 @@
     resident = pl.BlockSpec(memory_space=pltpu.VMEM)
     return pl.pallas_call(
         up_kernel,
-        in_specs=[resident, resident, pl.BlockSpec(memory_space=pl.ANY)],
+        in_specs=[resident] * 3,
         out_specs=resident,
-        scratch_shapes=[pltpu.VMEM(up.shape, up.dtype), pltpu.SemaphoreType.DMA],
         out_shape=jax.ShapeDtypeStruct((rows, up.shape[1]), jnp.bfloat16),
         compiler_params=pltpu.CompilerParams(vmem_limit_bytes=16 * 1024 * 1024),
         cost_estimate=pl.CostEstimate(
-            flops=2 * rows * up.size, bytes_accessed=4 * up.size, transcendentals=0
+            flops=FAR_FLOPS, bytes_accessed=4 * up.size, transcendentals=0
         ),
         name="expand_up",
-    )(partials, ids, pltpu.with_memory_space_constraint(up, pltpu.HBM))
+    )(partials, ids, up)
 
 
 def finish_kernel(slots_ref, returned_ref, base_ref, *refs):
@@ -355,11 +358,11 @@
     owned = lax.all_to_all(
         payload.reshape(owners, capacity * steps, width + 128), "dp", 0, 0, tiled=True
     ).reshape(rows, width + 128)
-    partial_shrink, ids = shrink_down(
-        after(owned, own), adapter_down_weight.reshape(owner_partial * rank, width), shares, rank
-    )
+    down = adapter_down_weight.reshape(owner_partial * rank, width)
+    up = adapter_up_weight.reshape(owner_partial * rank, width)
+    partial_shrink, ids = shrink_down(after(owned, own), down, up, shares, rank)
     partials = lax.all_to_all(partial_shrink, "tensor", 0, 0, tiled=True)
-    delta = expand_up(partials, ids, adapter_up_weight.reshape(owner_partial * rank, width))
+    delta = expand_up(after(partials, arrived[0], arrived[2]), ids, up)
     returned = lax.all_to_all(
         delta.reshape(owners, capacity * steps, width), "dp", 0, 0, tiled=True
     ).reshape(rows, width)

time: 97.7 us -> 94.2 us (0.964)
  blocking collectives: 10.3 us -> 0 us
  waiting for transfers between devices: 17.4 us -> 25.8 us
  Pallas kernels: 14.8 us -> 11.8 us
  starting transfers between devices: 52.2 us -> 53.8 us
    all_to_all x1 -> x0, blocking collectives: 10.3 us -> none  [on_device(): partials = lax.all_to_all(partial_shrink, 'tensor', 0, 0, tiled=True)]
    all_to_all x1, starting transfers between devices: 10.1 us -> 6.14 us  [on_device(): lax.all_to_all(delta.reshape(owners, capacity * steps, width), 'dp', 0, 0...]
    all_to_all x1, waiting for transfers between devices: 5.56 us -> 9.49 us  [on_device(): lax.all_to_all(payload.reshape(owners, capacity * steps, width + 128), 'd...]
    all_to_all x0 -> x1, starting transfers between devices: none -> 3.53 us  [on_device(): partials = lax.all_to_all(partial_shrink, 'tensor', 0, 0, tiled=True)]
    all_to_all x0 -> x1, waiting for transfers between devices: none -> 3.11 us  [on_device(): partials = lax.all_to_all(partial_shrink, 'tensor', 0, 0, tiled=True)]
    pallas_call x3, Pallas kernels: 7.71 us -> 4.68 us  [the longest x1 2.6 us: project(): pl.pallas_call(project_kernel, in_specs=[resident] * 2, out_specs=[pl.Blo...]
    ppermute x6, starting transfers between devices: 17.1 us -> 19 us  [move(): return lax.ppermute(value, ('dp', 'tensor'), pairs)]
    all_to_all x1, waiting for transfers between devices: 0.54 us -> 1.67 us  [on_device(): lax.all_to_all(delta.reshape(owners, capacity * steps, width), 'dp', 0, 0...]
  transfers between devices with their start and end apart: 9 -> 10, of which waited for: 5 -> 6; matrix products, arithmetic and copies ran while one was open for 2% -> 2% of each run, Pallas kernels for 8% -> 5%
where the time goes in v4:
time: 94.2 us; the launch traced here: 93.5 us
  starting transfers between devices  53.8 us (57%)
  waiting for transfers between devices  25.8 us (27%)
  Pallas kernels  11.8 us (13%)
  other arithmetic  1.62 us (2%)
    ppermute x6, starting transfers between devices, move(): return lax.ppermute(value, ('dp', 'tensor'), pairs)  19 us
    all_to_all x1, starting transfers between devices, on_device(): lax.all_to_all(payload.reshape(owners, capacity * steps, width + 128), 'd...  17.3 us
    all_to_all x1, waiting for transfers between devices, on_device(): lax.all_to_all(payload.reshape(owners, capacity * steps, width + 128), 'd...  9.49 us
    all_to_all x1, starting transfers between devices, on_device(): lax.all_to_all(attended, 'tensor', 0, 0, tiled=True).reshape(rows, width)  7.73 us
    all_to_all x1, waiting for transfers between devices, on_device(): lax.all_to_all(attended, 'tensor', 0, 0, tiled=True).reshape(rows, width)  6.25 us
    all_to_all x1, starting transfers between devices, on_device(): lax.all_to_all(delta.reshape(owners, capacity * steps, width), 'dp', 0, 0...  6.14 us
    ppermute x6, waiting for transfers between devices, move(): return lax.ppermute(value, ('dp', 'tensor'), pairs)  5.29 us
    pallas_call x1, Pallas kernels, attend(): pl.pallas_call(attend_kernel, in_specs=[pl.BlockSpec(memory_space=pltpu.S...  5.27 us
  transfers between devices with their start and end apart: 10, of which 6 were waited for; matrix products, arithmetic and copies ran while one was open for 2% of the time, Pallas kernels for 5%

profile of v4, /device:TPU:1, one launch (start us, length us, event | category | flops | bytes accessed | tf_op | source)
XLA Modules:
  0.0 93.5 jit_solution(3546337794706543145)
XLA Ops:
  0.0 5.3 %attend.1 = bf16[16,16,256]{2,1,0:T(8,128)(2,1)} custom-call(s32[4]{0:T(128)} %fill_ref.1, bf16[4,4,32,128]{3,2,1,0:T(8,128)(2,1)} %queries_ref.1, bf16[4,4,512,128]{3,2,1,0:T(8,128)(2,1)} %keys_ref.1, bf16[4,4,512,128]{3,2,1,0:T(8,128)(2,1)} %values_ref.1), custom_call_target="tpu_custom_call" | custom-call | flops 134217728 | bytes 4194304 | tf_op jit(solution)/shard_map/attend/pallas_call | solution.py:95
  5.3 0.0 copy-start.1
  5.3 0.0 copy-start.2
  5.3 7.7 %all-to-all-start = ((bf16[16,16,256]{2,1,0:T(8,128)(2,1)}), bf16[16,16,256]{2,1,0:T(8,128)(2,1)S(1)}, u32[]{:S(2)}, u32[]{:S(2)}) async-start(bf16[16,16,256]{2,1,0:T(8,128)(2,1)} %attend.1), calls=%async_computation | async-start | bytes 262144 | tf_op jit(solution)/shard_map/all_to_all | solution.py:350
  13.1 0.2 convert_reduce_fusion
  13.3 0.1 iota_add_fusion
  13.3 0.1 add.92.slots_ref
  13.5 0.1 broadcast_in_dim.2
  13.5 0.1 broadcast_in_dim_reshape.3.locals_ref
  13.6 6.2 %all-to-all-done = bf16[16,16,256]{2,1,0:T(8,128)(2,1)S(1)} async-done(((bf16[16,16,256]{2,1,0:T(8,128)(2,1)}), bf16[16,16,256]{2,1,0:T(8,128)(2,1)S(1)}, u32[]{:S(2)}, u32[]{:S(2)}) %all-to-all-start) | async-done | bytes 131104 | tf_op jit(solution)/shard_map/all_to_all | solution.py:350
  19.9 0.9 make_payload.1
  20.8 17.3 %all-to-all-start.1 = ((bf16[32,8,384]{2,1,0:T(8,128)(2,1)}), bf16[32,8,384]{2,1,0:T(8,128)(2,1)S(1)}, u32[]{:S(2)}, u32[]{:S(2)}) async-start(bf16[32,8,384]{2,1,0:T(8,128)(2,1)} %bitcast.1), calls=%async_computation.1 | async-start | bytes 393216 | tf_op jit(solution)/shard_map/all_to_all | solution.py:358
  38.2 2.6 %project.1 = (f32[4,256,256]{2,1,0:T(8,128)}, bf16[4,256,256]{2,1,0:T(8,128)(2,1)}, bf16[4,256,256]{2,1,0:T(8,128)(2,1)S(1)}, bf16[4,256,256]{2,1,0:T(8,128)(2,1)}) custom-call(bf16[256,256]{1,0:T(8,128)(2,1)S(1)} %bitcast.16, bf16[256,4096]{1,0:T(8,128)(2,1)S(1)} %copy-done), custom_call_target="tpu_custom_call" | custom-call | flops 536870912 | bytes 5242880 | tf_op jit(solution)/shard_map/project/pallas_call | solution.py:177
  40.8 1.9 %collective-permute-start = (bf16[4,256,256]{2,1,0:T(8,128)(2,1)}, bf16[4,256,256]{2,1,0:T(8,128)(2,1)S(1)}, u32[]{:S(2)}, u32[]{:S(2)}) collective-permute-start(bf16[4,256,256]{2,1,0:T(8,128)(2,1)} %get-tuple-element.18), channel_id=1, source_target_pairs={{0,1},{1,2},{2,3},{3,0},{4,5},{5,6},{6,7},{7,4},{8,9},{9,10},{10,1... | collective-permute-start | bytes 1572872 | tf_op jit(solution)/shard_map/ppermute | solution.py:316
  42.7 4.6 %collective-permute-start.1 = (bf16[4,256,256]{2,1,0:T(8,128)(2,1)}, bf16[4,256,256]{2,1,0:T(8,128)(2,1)S(1)}, u32[]{:S(2)}, u32[]{:S(2)}) collective-permute-start(bf16[4,256,256]{2,1,0:T(8,128)(2,1)} %get-tuple-element.19), channel_id=1, source_target_pairs={{0,3},{1,0},{2,1},{3,2},{4,7},{5,4},{6,5},{7,6},{8,11},{9,8},{10,9... | collective-permute-start | bytes 1572872 | tf_op jit(solution)/shard_map/ppermute | solution.py:316
  47.3 9.5 %all-to-all-done.1 = bf16[32,8,384]{2,1,0:T(8,128)(2,1)S(1)} async-done(((bf16[32,8,384]{2,1,0:T(8,128)(2,1)}), bf16[32,8,384]{2,1,0:T(8,128)(2,1)S(1)}, u32[]{:S(2)}, u32[]{:S(2)}) %all-to-all-start.1) | async-done | bytes 196640 | tf_op jit(solution)/shard_map/all_to_all | solution.py:358
  56.8 1.0 %shrink_down.1 = (f32[16,16,256]{2,1,0:T(8,128)}, f32[256,128]{1,0:T(8,128)S(1)}) custom-call(bf16[256,384]{1,0:T(8,128)(2,1)S(1)} %bitcast.17, bf16[512,256]{1,0:T(8,128)(2,1)S(1)} %bitcast.19, bf16[512,256]{1,0:T(8,128)(2,1)S(1)} %bitcast.20), custom_call_target="tpu_custom_call" | custom-call | flops 67108864 | bytes 524288 | tf_op jit(solution)/shard_map/shrink_down/pallas_call | solution.py:218
  57.8 3.5 %all-to-all-start.2 = ((f32[16,16,256]{2,1,0:T(8,128)}), f32[16,16,256]{2,1,0:T(8,128)S(1)}, u32[]{:S(2)}, u32[]{:S(2)}) async-start(f32[16,16,256]{2,1,0:T(8,128)} %get-tuple-element.17), calls=%async_computation.2 | async-start | bytes 524288 | tf_op jit(solution)/shard_map/all_to_all | solution.py:364
  61.3 4.7 %collective-permute-start.2 = (bf16[4,256,256]{2,1,0:T(8,128)(2,1)S(1)}, bf16[4,256,256]{2,1,0:T(8,128)(2,1)}, u32[]{:S(2)}, u32[]{:S(2)}) collective-permute-start(bf16[4,256,256]{2,1,0:T(8,128)(2,1)S(1)} %get-tuple-element.22), channel_id=1, source_target_pairs={{0,2},{1,3},{2,0},{3,1},{4,6},{5,7},{6,4},{7,5},{8,10},{9,11},{10,... | collective-permute-start | bytes 1572872 | tf_op jit(solution)/shard_map/ppermute | solution.py:316
  66.1 0.0 collective-permute-done
  66.1 3.1 %all-to-all-done.2.partials_ref = f32[16,16,256]{2,1,0:T(8,128)S(1)} async-done(((f32[16,16,256]{2,1,0:T(8,128)}), f32[16,16,256]{2,1,0:T(8,128)S(1)}, u32[]{:S(2)}, u32[]{:S(2)}) %all-to-all-start.2) | async-done | bytes 262176 | tf_op jit(solution)/shard_map/all_to_all | solution.py:364
  69.2 1.1 %expand_up.1 = bf16[256,256]{1,0:T(8,128)(2,1)} custom-call(f32[16,16,256]{2,1,0:T(8,128)S(1)} %all-to-all-done.2.partials_ref, f32[256,128]{1,0:T(8,128)S(1)} %get-tuple-element.21.ids_ref, bf16[512,256]{1,0:T(8,128)(2,1)S(1)} %bitcast.21), custom_call_target="tpu_custom_call" | custom-call | flops 20000000000 | bytes 524288 | tf_op jit(solution)/shard_map/expand_up/pallas_call | solution.py:261
  70.3 6.1 %all-to-all-start.3 = ((bf16[32,8,256]{2,1,0:T(8,128)(2,1)}), bf16[32,8,256]{2,1,0:T(8,128)(2,1)S(1)}, u32[]{:S(2)}, u32[]{:S(2)}) async-start(bf16[32,8,256]{2,1,0:T(8,128)(2,1)} %bitcast.5), calls=%async_computation.3 | async-start | bytes 262144 | tf_op jit(solution)/shard_map/all_to_all | solution.py:366
  76.4 1.4 %fusion.2 = (bf16[256,256]{1,0:T(8,128)(2,1)S(1)}, bf16[256,256]{1,0:T(8,128)(2,1)S(1)}, bf16[256,256]{1,0:T(8,128)(2,1)S(1)}, f32[256,256]{1,0:T(8,128)S(1)}) fusion(f32[4,256,256]{2,1,0:T(8,128)S(1)} %copy-done.3, bf16[4,256,256]{2,1,0:T(8,128)(2,1)S(1)} %copy-done.5, bf16[4,256,256]{2,1,0:T(8,128)(2,1)} %collective-permute-done.2, ...), kind=kLoop, calls=%fused_computation.6 | loop fusion | flops 1769472 | bytes 3276800 | tf_op jit(solution)/shard_map/add | solution.py:371
  77.8 2.5 %collective-permute-start.5 = (bf16[256,256]{1,0:T(8,128)(2,1)S(1)}, bf16[256,256]{1,0:T(8,128)(2,1)S(1)}, u32[]{:S(2)}, u32[]{:S(2)}) collective-permute-start(bf16[256,256]{1,0:T(8,128)(2,1)S(1)} %get-tuple-element.23), channel_id=1, source_target_pairs={{0,12},{1,13},{2,14},{3,15},{4,0},{5,1},{6,2},{7,3},{8,4},{9,5},{1... | collective-permute-start | bytes 393224 | tf_op jit(solution)/shard_map/ppermute | solution.py:316
  80.3 3.4 %collective-permute-start.4 = (bf16[256,256]{1,0:T(8,128)(2,1)S(1)}, bf16[256,256]{1,0:T(8,128)(2,1)S(1)}, u32[]{:S(2)}, u32[]{:S(2)}) collective-permute-start(bf16[256,256]{1,0:T(8,128)(2,1)S(1)} %get-tuple-element.24), channel_id=1, source_target_pairs={{0,8},{1,9},{2,10},{3,11},{4,12},{5,13},{6,14},{7,15},{8,0},{9,1},... | collective-permute-start | bytes 393224 | tf_op jit(solution)/shard_map/ppermute | solution.py:316
  83.7 1.9 %collective-permute-start.3 = (bf16[256,256]{1,0:T(8,128)(2,1)S(1)}, bf16[256,256]{1,0:T(8,128)(2,1)S(1)}, u32[]{:S(2)}, u32[]{:S(2)}) collective-permute-start(bf16[256,256]{1,0:T(8,128)(2,1)S(1)} %get-tuple-element.25), channel_id=1, source_target_pairs={{0,4},{1,5},{2,6},{3,7},{4,8},{5,9},{6,10},{7,11},{8,12},{9,13},{1... | collective-permute-start | bytes 393224 | tf_op jit(solution)/shard_map/ppermute | solution.py:316
  85.6 0.0 collective-permute-done.5.refs_2_
  85.6 2.2 %collective-permute-done.4.refs_1_ = bf16[256,256]{1,0:T(8,128)(2,1)S(1)} collective-permute-done((bf16[256,256]{1,0:T(8,128)(2,1)S(1)}, bf16[256,256]{1,0:T(8,128)(2,1)S(1)}, u32[]{:S(2)}, u32[]{:S(2)}) %collective-permute-start.4) | collective-permute-done | bytes 131104 | tf_op jit(solution)/shard_map/ppermute | solution.py:316
  87.8 3.1 %collective-permute-done.3.refs_0_ = bf16[256,256]{1,0:T(8,128)(2,1)S(1)} collective-permute-done((bf16[256,256]{1,0:T(8,128)(2,1)S(1)}, bf16[256,256]{1,0:T(8,128)(2,1)S(1)}, u32[]{:S(2)}, u32[]{:S(2)}) %collective-permute-start.3) | collective-permute-done | bytes 131104 | tf_op jit(solution)/shard_map/ppermute | solution.py:316
  90.9 1.7 %all-to-all-done.3 = bf16[32,8,256]{2,1,0:T(8,128)(2,1)S(1)} async-done(((bf16[32,8,256]{2,1,0:T(8,128)(2,1)}), bf16[32,8,256]{2,1,0:T(8,128)(2,1)S(1)}, u32[]{:S(2)}, u32[]{:S(2)}) %all-to-all-start.3) | async-done | bytes 131104 | tf_op jit(solution)/shard_map/all_to_all | solution.py:366
  92.6 0.9 %finish.1 = bf16[64,4,256]{2,1,0:T(4,128)(2,1)} custom-call(s32[1,256]{1,0:T(1,128)S(1)} %add.92.slots_ref, bf16[256,256]{1,0:T(8,128)(2,1)S(1)} %bitcast.18, f32[256,256]{1,0:T(8,128)S(1)} %get-tuple-element.26.base_ref, bf16[256,256]{1,0:T(8,128)(2,1)S(1)} %collective-permute-done.3.refs_0_, bf16[256,256]{1,0:T(8,128)(2,1)S(1)} %collective-permute-done.4.refs_1_, ...), custom_call_target="tpu_custom_call" | custom-call | flops 33554432 | bytes 524288 | tf_op jit(solution)/shard_map/finish/pallas_call | solution.py:290
  (16 shorter events, 0.0 us)
Async XLA Ops:
  0.0 13.0 %copy-start.6 = (s32[64]{0:T(128)S(1)}, s32[64]{0:T(128)}, u32[]{:S(2)}) copy-start(s32[64]{0:T(128)} %param.12) | copy-start | bytes 772
  0.0 38.2 %copy-start = (bf16[256,4096]{1,0:T(8,128)(2,1)S(1)}, bf16[256,4096]{1,0:T(8,128)(2,1)}, u32[]{:S(2)}) copy-start(bf16[256,4096]{1,0:T(8,128)(2,1)} %wo_ref.1) | copy-start | bytes 6291460
  5.3 51.5 %copy-start.1 = (bf16[32,16,256]{2,1,0:T(8,128)(2,1)S(1)}, bf16[32,16,256]{2,1,0:T(8,128)(2,1)}, u32[]{:S(2)}) copy-start(bf16[32,16,256]{2,1,0:T(8,128)(2,1)} %param.14) | copy-start | bytes 786436
  5.3 51.5 %copy-start.2 = (bf16[32,16,256]{2,1,0:T(8,128)(2,1)S(1)}, bf16[32,16,256]{2,1,0:T(8,128)(2,1)}, u32[]{:S(2)}) copy-start(bf16[32,16,256]{2,1,0:T(8,128)(2,1)} %param.15) | copy-start | bytes 786436
  5.3 14.6 %all-to-all-start = ((bf16[16,16,256]{2,1,0:T(8,128)(2,1)}), bf16[16,16,256]{2,1,0:T(8,128)(2,1)S(1)}, u32[]{:S(2)}, u32[]{:S(2)}) async-start(bf16[16,16,256]{2,1,0:T(8,128)(2,1)} %attend.1), calls=%async_computation | async-start | bytes 262144 | tf_op jit(solution)/shard_map/all_to_all | solution.py:350
  20.8 36.0 %all-to-all-start.1 = ((bf16[32,8,384]{2,1,0:T(8,128)(2,1)}), bf16[32,8,384]{2,1,0:T(8,128)(2,1)S(1)}, u32[]{:S(2)}, u32[]{:S(2)}) async-start(bf16[32,8,384]{2,1,0:T(8,128)(2,1)} %bitcast.1), calls=%async_computation.1 | async-start | bytes 393216 | tf_op jit(solution)/shard_map/all_to_all | solution.py:358
  40.8 25.3 %collective-permute-start = (bf16[4,256,256]{2,1,0:T(8,128)(2,1)}, bf16[4,256,256]{2,1,0:T(8,128)(2,1)S(1)}, u32[]{:S(2)}, u32[]{:S(2)}) collective-permute-start(bf16[4,256,256]{2,1,0:T(8,128)(2,1)} %get-tuple-element.18), channel_id=1, source_target_pairs={{0,1},{1,2},{2,3},{3,0},{4,5},{5,6},{6,7},{7,4},{8,9},{9,10},{10,1... | collective-permute-start | bytes 1572872 | tf_op jit(solution)/shard_map/ppermute | solution.py:316
  42.7 23.4 %collective-permute-start.1 = (bf16[4,256,256]{2,1,0:T(8,128)(2,1)}, bf16[4,256,256]{2,1,0:T(8,128)(2,1)S(1)}, u32[]{:S(2)}, u32[]{:S(2)}) collective-permute-start(bf16[4,256,256]{2,1,0:T(8,128)(2,1)} %get-tuple-element.19), channel_id=1, source_target_pairs={{0,3},{1,0},{2,1},{3,2},{4,7},{5,4},{6,5},{7,6},{8,11},{9,8},{10,9... | collective-permute-start | bytes 1572872 | tf_op jit(solution)/shard_map/ppermute | solution.py:316
  57.8 11.4 %all-to-all-start.2 = ((f32[16,16,256]{2,1,0:T(8,128)}), f32[16,16,256]{2,1,0:T(8,128)S(1)}, u32[]{:S(2)}, u32[]{:S(2)}) async-start(f32[16,16,256]{2,1,0:T(8,128)} %get-tuple-element.17), calls=%async_computation.2 | async-start | bytes 524288 | tf_op jit(solution)/shard_map/all_to_all | solution.py:364
  61.3 15.1 %collective-permute-start.2 = (bf16[4,256,256]{2,1,0:T(8,128)(2,1)S(1)}, bf16[4,256,256]{2,1,0:T(8,128)(2,1)}, u32[]{:S(2)}, u32[]{:S(2)}) collective-permute-start(bf16[4,256,256]{2,1,0:T(8,128)(2,1)S(1)} %get-tuple-element.22), channel_id=1, source_target_pairs={{0,2},{1,3},{2,0},{3,1},{4,6},{5,7},{6,4},{7,5},{8,10},{9,11},{10,... | collective-permute-start | bytes 1572872 | tf_op jit(solution)/shard_map/ppermute | solution.py:316
  66.1 3.1 %copy-start.4 = (bf16[4,256,256]{2,1,0:T(8,128)(2,1)}, bf16[4,256,256]{2,1,0:T(8,128)(2,1)S(1)}, u32[]{:S(2)}) copy-start(bf16[4,256,256]{2,1,0:T(8,128)(2,1)S(1)} %collective-permute-done.1) | copy-start | bytes 1572868
  69.2 7.2 %copy-start.3 = (f32[4,256,256]{2,1,0:T(8,128)S(1)}, f32[4,256,256]{2,1,0:T(8,128)}, u32[]{:S(2)}) copy-start(f32[4,256,256]{2,1,0:T(8,128)} %get-tuple-element.15) | copy-start | bytes 3145732
  69.2 7.2 %copy-start.5 = (bf16[4,256,256]{2,1,0:T(8,128)(2,1)S(1)}, bf16[4,256,256]{2,1,0:T(8,128)(2,1)}, u32[]{:S(2)}) copy-start(bf16[4,256,256]{2,1,0:T(8,128)(2,1)} %copy-done.4) | copy-start | bytes 1572868
  70.3 22.3 %all-to-all-start.3 = ((bf16[32,8,256]{2,1,0:T(8,128)(2,1)}), bf16[32,8,256]{2,1,0:T(8,128)(2,1)S(1)}, u32[]{:S(2)}, u32[]{:S(2)}) async-start(bf16[32,8,256]{2,1,0:T(8,128)(2,1)} %bitcast.5), calls=%async_computation.3 | async-start | bytes 262144 | tf_op jit(solution)/shard_map/all_to_all | solution.py:366
  77.8 7.8 %collective-permute-start.5 = (bf16[256,256]{1,0:T(8,128)(2,1)S(1)}, bf16[256,256]{1,0:T(8,128)(2,1)S(1)}, u32[]{:S(2)}, u32[]{:S(2)}) collective-permute-start(bf16[256,256]{1,0:T(8,128)(2,1)S(1)} %get-tuple-element.23), channel_id=1, source_target_pairs={{0,12},{1,13},{2,14},{3,15},{4,0},{5,1},{6,2},{7,3},{8,4},{9,5},{1... | collective-permute-start | bytes 393224 | tf_op jit(solution)/shard_map/ppermute | solution.py:316
  80.3 7.5 %collective-permute-start.4 = (bf16[256,256]{1,0:T(8,128)(2,1)S(1)}, bf16[256,256]{1,0:T(8,128)(2,1)S(1)}, u32[]{:S(2)}, u32[]{:S(2)}) collective-permute-start(bf16[256,256]{1,0:T(8,128)(2,1)S(1)} %get-tuple-element.24), channel_id=1, source_target_pairs={{0,8},{1,9},{2,10},{3,11},{4,12},{5,13},{6,14},{7,15},{8,0},{9,1},... | collective-permute-start | bytes 393224 | tf_op jit(solution)/shard_map/ppermute | solution.py:316
  83.7 7.2 %collective-permute-start.3 = (bf16[256,256]{1,0:T(8,128)(2,1)S(1)}, bf16[256,256]{1,0:T(8,128)(2,1)S(1)}, u32[]{:S(2)}, u32[]{:S(2)}) collective-permute-start(bf16[256,256]{1,0:T(8,128)(2,1)S(1)} %get-tuple-element.25), channel_id=1, source_target_pairs={{0,4},{1,5},{2,6},{3,7},{4,8},{5,9},{6,10},{7,11},{8,12},{9,13},{1... | collective-permute-start | bytes 393224 | tf_op jit(solution)/shard_map/ppermute | solution.py:316

commit v5 on v4

--- a/solution.py
+++ b/solution.py
@@ -118,36 +118,61 @@
     )(cache_fill_length, queries, cached_key_rows, cached_value_rows)
 
 
-def payload_kernel(rows_ref, slots_ref, locals_ref, out_ref):
-    rows, width = rows_ref.shape
+def slot_kernel(slots_ref, locals_ref, hit_ref, ids_ref):
+    rows, lanes = ids_ref.shape
     slot = lax.broadcasted_iota(jnp.int32, (rows, rows), 0)
     hit = (slot == slots_ref[...]).astype(jnp.bfloat16)
-    out_ref[:, :width] = jnp.dot(
-        hit, rows_ref[...], preferred_element_type=jnp.float32
-    ).astype(jnp.bfloat16)
+    hit_ref[...] = hit
     ids = locals_ref[...].astype(jnp.float32).astype(jnp.bfloat16)
-    out_ref[:, width:] = lax.dot_general(
+    ids_ref[...] = lax.dot_general(
         hit,
-        jnp.broadcast_to(ids, (out_ref.shape[1] - width, rows)),
+        jnp.broadcast_to(ids, (lanes, rows)),
         (((1,), (1,)), ((), ())),
         preferred_element_type=jnp.float32,
     ).astype(jnp.bfloat16)
 
 
-def make_payload(head_rows, row_slots, row_locals):
+def slot_map(row_slots, row_locals):
+    rows = row_slots.shape[1]
+    resident = pl.BlockSpec(memory_space=pltpu.VMEM)
+    return pl.pallas_call(
+        slot_kernel,
+        in_specs=[resident] * 2,
+        out_specs=[resident] * 2,
+        out_shape=[
+            jax.ShapeDtypeStruct((rows, rows), jnp.bfloat16),
+            jax.ShapeDtypeStruct((rows, 128), jnp.bfloat16),
+        ],
+        compiler_params=pltpu.CompilerParams(vmem_limit_bytes=16 * 1024 * 1024),
+        cost_estimate=pl.CostEstimate(
+            flops=2 * rows * rows * 128, bytes_accessed=4 * rows * rows, transcendentals=0
+        ),
+        name="slot_map",
+    )(row_slots, row_locals)
+
+
+def payload_kernel(rows_ref, hit_ref, ids_ref, out_ref):
+    width = rows_ref.shape[1]
+    out_ref[:, :width] = jnp.dot(
+        hit_ref[...], rows_ref[...], preferred_element_type=jnp.float32
+    ).astype(jnp.bfloat16)
+    out_ref[:, width:] = ids_ref[...]
+
+
+def make_payload(head_rows, hit, ids):
     rows, width = head_rows.shape
     resident = pl.BlockSpec(memory_space=pltpu.VMEM)
     return pl.pallas_call(
         payload_kernel,
         in_specs=[resident] * 3,
         out_specs=resident,
-        out_shape=jax.ShapeDtypeStruct((rows, width + 128), jnp.bfloat16),
+        out_shape=jax.ShapeDtypeStruct((rows, width + ids.shape[1]), jnp.bfloat16),
         compiler_params=pltpu.CompilerParams(vmem_limit_bytes=16 * 1024 * 1024),
         cost_estimate=pl.CostEstimate(
             flops=2 * rows * rows * width, bytes_accessed=8 * rows * width, transcendentals=0
         ),
         name="make_payload",
-    )(head_rows, row_slots, row_locals)
+    )(head_rows, hit, ids)
 
 
 def project_kernel(rows_ref, wo_ref, *refs):
@@ -208,7 +233,7 @@
     chosen = adapter == jnp.transpose(ids)[:1].reshape(1, 1, rows)
     part = jnp.sum(jnp.where(chosen, every.reshape(adapters, rank, rows), 0.0), axis=0)
     for share in range(out_ref.shape[0]):
-        out_ref[share] = part
+        out_ref[share] = part.astype(out_ref.dtype)
 
 
 def shrink_down(owned, down, up, shares, rank):
@@ -220,7 +245,7 @@
         in_specs=[resident] * 3,
         out_specs=[resident] * 2,
         out_shape=[
-            jax.ShapeDtypeStruct((shares, rank, rows), jnp.float32),
+            jax.ShapeDtypeStruct((shares, rank, rows), jnp.bfloat16),
             jax.ShapeDtypeStruct((rows, lanes), jnp.float32),
         ],
         compiler_params=pltpu.CompilerParams(vmem_limit_bytes=16 * 1024 * 1024),
@@ -235,9 +260,9 @@
     shares, rank, rows = partials_ref.shape
     maps = up_ref.shape[0]
     lanes = ids_ref.shape[1]
-    shrink = partials_ref[0]
+    shrink = partials_ref[0].astype(jnp.float32)
     for share in range(1, shares):
-        shrink += partials_ref[share]
+        shrink += partials_ref[share].astype(jnp.float32)
     fold = lax.broadcasted_iota(jnp.int32, (rank, maps), 1) % rank
     fold = (fold == lax.broadcasted_iota(jnp.int32, (rank, maps), 0)).astype(jnp.bfloat16)
     spread = lax.dot_general(
@@ -271,13 +296,10 @@
     )(partials, ids, up)
 
 
-def finish_kernel(slots_ref, returned_ref, base_ref, *refs):
+def finish_kernel(hit_ref, returned_ref, base_ref, *refs):
     across_refs, out_ref = refs[:-1], refs[-1]
-    rows = returned_ref.shape[0]
-    slot = lax.broadcasted_iota(jnp.int32, (rows, rows), 0)
-    to_slots = (slot == slots_ref[...]).astype(jnp.bfloat16)
     delta = lax.dot_general(
-        to_slots, returned_ref[...], (((0,), (0,)), ((), ())), preferred_element_type=jnp.float32
+        hit_ref[...], returned_ref[...], (((0,), (0,)), ((), ())), preferred_element_type=jnp.float32
     )
     total = base_ref[...] + delta
     for across_ref in across_refs:
@@ -285,7 +307,7 @@
     out_ref[...] = total.reshape(out_ref.shape).astype(out_ref.dtype)
 
 
-def finish(row_slots, returned, base, across, out_shape):
+def finish(hit, returned, base, across, out_shape):
     resident = pl.BlockSpec(memory_space=pltpu.VMEM)
     return pl.pallas_call(
         finish_kernel,
@@ -299,7 +321,7 @@
             transcendentals=0,
         ),
         name="finish",
-    )(row_slots, returned, base, *across)
+    )(hit, returned, base, *across)
 
 
 def move(value, owners, target):
@@ -345,11 +367,12 @@
     slots = owner_ids * capacity + jnp.sum(earlier.astype(jnp.int32), axis=1)
     row_slots = (slots[:, None] * steps + jnp.arange(steps, dtype=jnp.int32)).reshape(1, rows)
     row_locals = jnp.repeat(local_ids, steps)[None, :]
+    hit, id_lanes = slot_map(row_slots, row_locals)
 
     attended = attend(queries, cached_key_rows, cached_value_rows, cache_fill_length)
     head_rows = lax.all_to_all(attended, "tensor", 0, 0, tiled=True).reshape(rows, width)
 
-    payload = make_payload(head_rows, row_slots, row_locals)
+    payload = make_payload(head_rows, hit, id_lanes)
     own, *others = project(after(head_rows, payload), wo)
     arrived = [
         move(part, owners, lambda pair, line, s=s: (pair, (line + s) % SIDE))
@@ -379,7 +402,7 @@
         for u in range(1, SIDE)
     ]
     return finish(
-        row_slots, returned, along_line[0], across, (group_size, steps, width)
+        hit, returned, along_line[0], across, (group_size, steps, width)
     )
 
 

time: 94.2 us -> 93.2 us (0.989)
  other arithmetic: 1.62 us -> 0.49 us
    all_to_all x1, waiting for transfers between devices: 1.67 us -> 2.79 us  [on_device(): lax.all_to_all(delta.reshape(owners, capacity * steps, width), 'dp', 0, 0...]
    add x1, other arithmetic: 1.35 us -> 0.23 us  [on_device(): own[u] + sum((part[u].astype(jnp.float32) for part in arrived))]
    all_to_all x1, waiting for transfers between devices: 3.11 us -> 2.17 us  [on_device(): partials = lax.all_to_all(partial_shrink, 'tensor', 0, 0, tiled=True)]
  transfers between devices with their start and end apart: 10 -> 10, of which waited for: 6 -> 6; matrix products, arithmetic and copies ran while one was open for 2% -> 1% of each run, Pallas kernels for 5% -> 5%
where the time goes in v5:
time: 93.2 us; the launch traced here: 92.6 us
  starting transfers between devices  53.9 us (58%)
  waiting for transfers between devices  25 us (27%)
  Pallas kernels  11.9 us (13%)
  local copies, waits for them, and re-layouts  1.1 us (1%)
    ppermute x6, starting transfers between devices, move(): return lax.ppermute(value, ('dp', 'tensor'), pairs)  19 us
    all_to_all x1, starting transfers between devices, on_device(): lax.all_to_all(payload.reshape(owners, capacity * steps, width + 128), 'd...  17.4 us
    all_to_all x1, waiting for transfers between devices, on_device(): lax.all_to_all(payload.reshape(owners, capacity * steps, width + 128), 'd...  8.72 us
    all_to_all x1, starting transfers between devices, on_device(): lax.all_to_all(attended, 'tensor', 0, 0, tiled=True).reshape(rows, width)  7.73 us
    all_to_all x1, starting transfers between devices, on_device(): lax.all_to_all(delta.reshape(owners, capacity * steps, width), 'dp', 0, 0...  6.3 us
    all_to_all x1, waiting for transfers between devices, on_device(): lax.all_to_all(attended, 'tensor', 0, 0, tiled=True).reshape(rows, width)  6.04 us
    ppermute x6, waiting for transfers between devices, move(): return lax.ppermute(value, ('dp', 'tensor'), pairs)  5.29 us
    pallas_call x1, Pallas kernels, attend(): pl.pallas_call(attend_kernel, in_specs=[pl.BlockSpec(memory_space=pltpu.S...  5.27 us
  transfers between devices with their start and end apart: 10, of which 6 were waited for; matrix products, arithmetic and copies ran while one was open for 1% of the time, Pallas kernels for 5%

profile of v5, /device:TPU:1, one launch (start us, length us, event | category | flops | bytes accessed | tf_op | source)
XLA Modules:
  0.0 92.6 jit_solution(11885414525104313431)
XLA Ops:
  0.0 5.3 %attend.1 = bf16[16,16,256]{2,1,0:T(8,128)(2,1)} custom-call(s32[4]{0:T(128)} %fill_ref.1, bf16[4,4,32,128]{3,2,1,0:T(8,128)(2,1)} %queries_ref.1, bf16[4,4,512,128]{3,2,1,0:T(8,128)(2,1)} %keys_ref.1, bf16[4,4,512,128]{3,2,1,0:T(8,128)(2,1)} %values_ref.1), custom_call_target="tpu_custom_call" | custom-call | flops 134217728 | bytes 4194304 | tf_op jit(solution)/shard_map/attend/pallas_call | solution.py:95
  5.3 0.0 copy-start.1
  5.3 0.0 copy-start.2
  5.3 7.7 %all-to-all-start = ((bf16[16,16,256]{2,1,0:T(8,128)(2,1)}), bf16[16,16,256]{2,1,0:T(8,128)(2,1)S(1)}, u32[]{:S(2)}, u32[]{:S(2)}) async-start(bf16[16,16,256]{2,1,0:T(8,128)(2,1)} %attend.1), calls=%async_computation | async-start | bytes 262144 | tf_op jit(solution)/shard_map/all_to_all | solution.py:373
  13.1 0.2 convert_reduce_fusion
  13.3 0.1 iota_add_fusion
  13.3 0.1 add.92.slots_ref
  13.5 0.1 broadcast_in_dim.2
  13.5 0.1 broadcast_in_dim_reshape.3.locals_ref
  13.6 0.2 slot_map.1
  13.9 6.0 %all-to-all-done = bf16[16,16,256]{2,1,0:T(8,128)(2,1)S(1)} async-done(((bf16[16,16,256]{2,1,0:T(8,128)(2,1)}), bf16[16,16,256]{2,1,0:T(8,128)(2,1)S(1)}, u32[]{:S(2)}, u32[]{:S(2)}) %all-to-all-start) | async-done | bytes 131104 | tf_op jit(solution)/shard_map/all_to_all | solution.py:373
  19.9 0.9 make_payload.1
  20.8 17.4 %all-to-all-start.1 = ((bf16[32,8,384]{2,1,0:T(8,128)(2,1)}), bf16[32,8,384]{2,1,0:T(8,128)(2,1)S(1)}, u32[]{:S(2)}, u32[]{:S(2)}) async-start(bf16[32,8,384]{2,1,0:T(8,128)(2,1)} %bitcast.1), calls=%async_computation.1 | async-start | bytes 393216 | tf_op jit(solution)/shard_map/all_to_all | solution.py:381
  38.1 2.6 %project.1 = (f32[4,256,256]{2,1,0:T(8,128)}, bf16[4,256,256]{2,1,0:T(8,128)(2,1)}, bf16[4,256,256]{2,1,0:T(8,128)(2,1)S(1)}, bf16[4,256,256]{2,1,0:T(8,128)(2,1)}) custom-call(bf16[256,256]{1,0:T(8,128)(2,1)S(1)} %bitcast.16, bf16[256,4096]{1,0:T(8,128)(2,1)S(1)} %copy-done), custom_call_target="tpu_custom_call" | custom-call | flops 536870912 | bytes 5242880 | tf_op jit(solution)/shard_map/project/pallas_call | solution.py:202
  40.7 0.8 copy-done.3
  41.5 1.9 %collective-permute-start = (bf16[4,256,256]{2,1,0:T(8,128)(2,1)}, bf16[4,256,256]{2,1,0:T(8,128)(2,1)S(1)}, u32[]{:S(2)}, u32[]{:S(2)}) collective-permute-start(bf16[4,256,256]{2,1,0:T(8,128)(2,1)} %get-tuple-element.22), channel_id=1, source_target_pairs={{0,1},{1,2},{2,3},{3,0},{4,5},{5,6},{6,7},{7,4},{8,9},{9,10},{10,1... | collective-permute-start | bytes 1572872 | tf_op jit(solution)/shard_map/ppermute | solution.py:338
  43.4 4.6 %collective-permute-start.1 = (bf16[4,256,256]{2,1,0:T(8,128)(2,1)}, bf16[4,256,256]{2,1,0:T(8,128)(2,1)S(1)}, u32[]{:S(2)}, u32[]{:S(2)}) collective-permute-start(bf16[4,256,256]{2,1,0:T(8,128)(2,1)} %get-tuple-element.23), channel_id=1, source_target_pairs={{0,3},{1,0},{2,1},{3,2},{4,7},{5,4},{6,5},{7,6},{8,11},{9,8},{10,9... | collective-permute-start | bytes 1572872 | tf_op jit(solution)/shard_map/ppermute | solution.py:338
  48.0 8.7 %all-to-all-done.1 = bf16[32,8,384]{2,1,0:T(8,128)(2,1)S(1)} async-done(((bf16[32,8,384]{2,1,0:T(8,128)(2,1)}), bf16[32,8,384]{2,1,0:T(8,128)(2,1)S(1)}, u32[]{:S(2)}, u32[]{:S(2)}) %all-to-all-start.1) | async-done | bytes 196640 | tf_op jit(solution)/shard_map/all_to_all | solution.py:381
  56.8 0.9 %shrink_down.1 = (bf16[16,16,256]{2,1,0:T(8,128)(2,1)}, f32[256,128]{1,0:T(8,128)S(1)}) custom-call(bf16[256,384]{1,0:T(8,128)(2,1)S(1)} %bitcast.17, bf16[512,256]{1,0:T(8,128)(2,1)S(1)} %bitcast.19, bf16[512,256]{1,0:T(8,128)(2,1)S(1)} %bitcast.20), custom_call_target="tpu_custom_call" | custom-call | flops 67108864 | bytes 524288 | tf_op jit(solution)/shard_map/shrink_down/pallas_call | solution.py:243
  57.7 3.5 %all-to-all-start.2 = ((bf16[16,16,256]{2,1,0:T(8,128)(2,1)}), bf16[16,16,256]{2,1,0:T(8,128)(2,1)S(1)}, u32[]{:S(2)}, u32[]{:S(2)}) async-start(bf16[16,16,256]{2,1,0:T(8,128)(2,1)} %get-tuple-element.21), calls=%async_computation.2 | async-start | bytes 262144 | tf_op jit(solution)/shard_map/all_to_all | solution.py:387
  61.2 4.7 %collective-permute-start.2 = (bf16[4,256,256]{2,1,0:T(8,128)(2,1)}, bf16[4,256,256]{2,1,0:T(8,128)(2,1)S(1)}, u32[]{:S(2)}, u32[]{:S(2)}) collective-permute-start(bf16[4,256,256]{2,1,0:T(8,128)(2,1)} %copy-done.3), channel_id=1, source_target_pairs={{0,2},{1,3},{2,0},{3,1},{4,6},{5,7},{6,4},{7,5},{8,10},{9,11},{10,... | collective-permute-start | bytes 1572872 | tf_op jit(solution)/shard_map/ppermute | solution.py:338
  65.9 2.2 %all-to-all-done.2.partials_ref = bf16[16,16,256]{2,1,0:T(8,128)(2,1)S(1)} async-done(((bf16[16,16,256]{2,1,0:T(8,128)(2,1)}), bf16[16,16,256]{2,1,0:T(8,128)(2,1)S(1)}, u32[]{:S(2)}, u32[]{:S(2)}) %all-to-all-start.2) | async-done | bytes 131104 | tf_op jit(solution)/shard_map/all_to_all | solution.py:387
  68.1 1.1 %expand_up.1 = bf16[256,256]{1,0:T(8,128)(2,1)} custom-call(bf16[16,16,256]{2,1,0:T(8,128)(2,1)S(1)} %all-to-all-done.2.partials_ref, f32[256,128]{1,0:T(8,128)S(1)} %get-tuple-element.25.ids_ref, bf16[512,256]{1,0:T(8,128)(2,1)S(1)} %bitcast.21), custom_call_target="tpu_custom_call" | custom-call | flops 20000000000 | bytes 524288 | tf_op jit(solution)/shard_map/expand_up/pallas_call | solution.py:286
  69.2 6.3 %all-to-all-start.3 = ((bf16[32,8,256]{2,1,0:T(8,128)(2,1)}), bf16[32,8,256]{2,1,0:T(8,128)(2,1)S(1)}, u32[]{:S(2)}, u32[]{:S(2)}) async-start(bf16[32,8,256]{2,1,0:T(8,128)(2,1)} %bitcast.5), calls=%async_computation.3 | async-start | bytes 262144 | tf_op jit(solution)/shard_map/all_to_all | solution.py:389
  75.5 0.2 fusion.2
  75.7 2.7 %collective-permute-start.5 = (bf16[256,256]{1,0:T(8,128)(2,1)S(1)}, bf16[256,256]{1,0:T(8,128)(2,1)S(1)}, u32[]{:S(2)}, u32[]{:S(2)}) collective-permute-start(bf16[256,256]{1,0:T(8,128)(2,1)S(1)} %get-tuple-element.27), channel_id=1, source_target_pairs={{0,12},{1,13},{2,14},{3,15},{4,0},{5,1},{6,2},{7,3},{8,4},{9,5},{1... | collective-permute-start | bytes 393224 | tf_op jit(solution)/shard_map/ppermute | solution.py:338
  78.4 3.2 %collective-permute-start.4 = (bf16[256,256]{1,0:T(8,128)(2,1)S(1)}, bf16[256,256]{1,0:T(8,128)(2,1)S(1)}, u32[]{:S(2)}, u32[]{:S(2)}) collective-permute-start(bf16[256,256]{1,0:T(8,128)(2,1)S(1)} %get-tuple-element.28), channel_id=1, source_target_pairs={{0,8},{1,9},{2,10},{3,11},{4,12},{5,13},{6,14},{7,15},{8,0},{9,1},... | collective-permute-start | bytes 393224 | tf_op jit(solution)/shard_map/ppermute | solution.py:338
  81.6 1.9 %collective-permute-start.3 = (bf16[256,256]{1,0:T(8,128)(2,1)S(1)}, bf16[256,256]{1,0:T(8,128)(2,1)S(1)}, u32[]{:S(2)}, u32[]{:S(2)}) collective-permute-start(bf16[256,256]{1,0:T(8,128)(2,1)S(1)} %get-tuple-element.29), channel_id=1, source_target_pairs={{0,4},{1,5},{2,6},{3,7},{4,8},{5,9},{6,10},{7,11},{8,12},{9,13},{1... | collective-permute-start | bytes 393224 | tf_op jit(solution)/shard_map/ppermute | solution.py:338
  83.6 2.4 %collective-permute-done.4.refs_1_ = bf16[256,256]{1,0:T(8,128)(2,1)S(1)} collective-permute-done((bf16[256,256]{1,0:T(8,128)(2,1)S(1)}, bf16[256,256]{1,0:T(8,128)(2,1)S(1)}, u32[]{:S(2)}, u32[]{:S(2)}) %collective-permute-start.4) | collective-permute-done | bytes 131104 | tf_op jit(solution)/shard_map/ppermute | solution.py:338
  86.0 2.9 %collective-permute-done.3.refs_0_ = bf16[256,256]{1,0:T(8,128)(2,1)S(1)} collective-permute-done((bf16[256,256]{1,0:T(8,128)(2,1)S(1)}, bf16[256,256]{1,0:T(8,128)(2,1)S(1)}, u32[]{:S(2)}, u32[]{:S(2)}) %collective-permute-start.3) | collective-permute-done | bytes 131104 | tf_op jit(solution)/shard_map/ppermute | solution.py:338
  88.9 2.8 %all-to-all-done.3 = bf16[32,8,256]{2,1,0:T(8,128)(2,1)S(1)} async-done(((bf16[32,8,256]{2,1,0:T(8,128)(2,1)}), bf16[32,8,256]{2,1,0:T(8,128)(2,1)S(1)}, u32[]{:S(2)}, u32[]{:S(2)}) %all-to-all-start.3) | async-done | bytes 131104 | tf_op jit(solution)/shard_map/all_to_all | solution.py:389
  91.7 0.9 %finish.1 = bf16[64,4,256]{2,1,0:T(4,128)(2,1)} custom-call(bf16[256,256]{1,0:T(8,128)(2,1)S(1)} %get-tuple-element.16.hit_ref, bf16[256,256]{1,0:T(8,128)(2,1)S(1)} %bitcast.18, f32[256,256]{1,0:T(8,128)S(1)} %get-tuple-element.30.base_ref, bf16[256,256]{1,0:T(8,128)(2,1)S(1)} %collective-permute-done.3.refs_0_, ...), custom_call_target="tpu_custom_call" | custom-call | flops 33554432 | bytes 524288 | tf_op jit(solution)/shard_map/finish/pallas_call | solution.py:312
  (15 shorter events, 0.0 us)
Async XLA Ops:
  0.0 13.0 %copy-start.5 = (s32[64]{0:T(128)S(1)}, s32[64]{0:T(128)}, u32[]{:S(2)}) copy-start(s32[64]{0:T(128)} %param.12) | copy-start | bytes 772
  0.0 38.1 %copy-start = (bf16[256,4096]{1,0:T(8,128)(2,1)S(1)}, bf16[256,4096]{1,0:T(8,128)(2,1)}, u32[]{:S(2)}) copy-start(bf16[256,4096]{1,0:T(8,128)(2,1)} %wo_ref.1) | copy-start | bytes 6291460
  5.3 51.5 %copy-start.1 = (bf16[32,16,256]{2,1,0:T(8,128)(2,1)S(1)}, bf16[32,16,256]{2,1,0:T(8,128)(2,1)}, u32[]{:S(2)}) copy-start(bf16[32,16,256]{2,1,0:T(8,128)(2,1)} %param.14) | copy-start | bytes 786436
  5.3 51.5 %copy-start.2 = (bf16[32,16,256]{2,1,0:T(8,128)(2,1)S(1)}, bf16[32,16,256]{2,1,0:T(8,128)(2,1)}, u32[]{:S(2)}) copy-start(bf16[32,16,256]{2,1,0:T(8,128)(2,1)} %param.15) | copy-start | bytes 786436
  5.3 14.6 %all-to-all-start = ((bf16[16,16,256]{2,1,0:T(8,128)(2,1)}), bf16[16,16,256]{2,1,0:T(8,128)(2,1)S(1)}, u32[]{:S(2)}, u32[]{:S(2)}) async-start(bf16[16,16,256]{2,1,0:T(8,128)(2,1)} %attend.1), calls=%async_computation | async-start | bytes 262144 | tf_op jit(solution)/shard_map/all_to_all | solution.py:373
  20.8 36.0 %all-to-all-start.1 = ((bf16[32,8,384]{2,1,0:T(8,128)(2,1)}), bf16[32,8,384]{2,1,0:T(8,128)(2,1)S(1)}, u32[]{:S(2)}, u32[]{:S(2)}) async-start(bf16[32,8,384]{2,1,0:T(8,128)(2,1)} %bitcast.1), calls=%async_computation.1 | async-start | bytes 393216 | tf_op jit(solution)/shard_map/all_to_all | solution.py:381
  40.7 0.8 copy-start.3
  41.5 24.4 %collective-permute-start = (bf16[4,256,256]{2,1,0:T(8,128)(2,1)}, bf16[4,256,256]{2,1,0:T(8,128)(2,1)S(1)}, u32[]{:S(2)}, u32[]{:S(2)}) collective-permute-start(bf16[4,256,256]{2,1,0:T(8,128)(2,1)} %get-tuple-element.22), channel_id=1, source_target_pairs={{0,1},{1,2},{2,3},{3,0},{4,5},{5,6},{6,7},{7,4},{8,9},{9,10},{10,1... | collective-permute-start | bytes 1572872 | tf_op jit(solution)/shard_map/ppermute | solution.py:338
  43.4 22.5 %collective-permute-start.1 = (bf16[4,256,256]{2,1,0:T(8,128)(2,1)}, bf16[4,256,256]{2,1,0:T(8,128)(2,1)S(1)}, u32[]{:S(2)}, u32[]{:S(2)}) collective-permute-start(bf16[4,256,256]{2,1,0:T(8,128)(2,1)} %get-tuple-element.23), channel_id=1, source_target_pairs={{0,3},{1,0},{2,1},{3,2},{4,7},{5,4},{6,5},{7,6},{8,11},{9,8},{10,9... | collective-permute-start | bytes 1572872 | tf_op jit(solution)/shard_map/ppermute | solution.py:338
  57.7 10.4 %all-to-all-start.2 = ((bf16[16,16,256]{2,1,0:T(8,128)(2,1)}), bf16[16,16,256]{2,1,0:T(8,128)(2,1)S(1)}, u32[]{:S(2)}, u32[]{:S(2)}) async-start(bf16[16,16,256]{2,1,0:T(8,128)(2,1)} %get-tuple-element.21), calls=%async_computation.2 | async-start | bytes 262144 | tf_op jit(solution)/shard_map/all_to_all | solution.py:387
  61.2 14.3 %collective-permute-start.2 = (bf16[4,256,256]{2,1,0:T(8,128)(2,1)}, bf16[4,256,256]{2,1,0:T(8,128)(2,1)S(1)}, u32[]{:S(2)}, u32[]{:S(2)}) collective-permute-start(bf16[4,256,256]{2,1,0:T(8,128)(2,1)} %copy-done.3), channel_id=1, source_target_pairs={{0,2},{1,3},{2,0},{3,1},{4,6},{5,7},{6,4},{7,5},{8,10},{9,11},{10,... | collective-permute-start | bytes 1572872 | tf_op jit(solution)/shard_map/ppermute | solution.py:338
  68.1 7.4 %copy-start.4 = (f32[4,256,256]{2,1,0:T(8,128)S(1)}, f32[4,256,256]{2,1,0:T(8,128)}, u32[]{:S(2)}) copy-start(f32[4,256,256]{2,1,0:T(8,128)} %get-tuple-element.19) | copy-start | bytes 3145732
  69.2 22.5 %all-to-all-start.3 = ((bf16[32,8,256]{2,1,0:T(8,128)(2,1)}), bf16[32,8,256]{2,1,0:T(8,128)(2,1)S(1)}, u32[]{:S(2)}, u32[]{:S(2)}) async-start(bf16[32,8,256]{2,1,0:T(8,128)(2,1)} %bitcast.5), calls=%async_computation.3 | async-start | bytes 262144 | tf_op jit(solution)/shard_map/all_to_all | solution.py:389
  75.7 7.8 %collective-permute-start.5 = (bf16[256,256]{1,0:T(8,128)(2,1)S(1)}, bf16[256,256]{1,0:T(8,128)(2,1)S(1)}, u32[]{:S(2)}, u32[]{:S(2)}) collective-permute-start(bf16[256,256]{1,0:T(8,128)(2,1)S(1)} %get-tuple-element.27), channel_id=1, source_target_pairs={{0,12},{1,13},{2,14},{3,15},{4,0},{5,1},{6,2},{7,3},{8,4},{9,5},{1... | collective-permute-start | bytes 393224 | tf_op jit(solution)/shard_map/ppermute | solution.py:338
  78.4 7.5 %collective-permute-start.4 = (bf16[256,256]{1,0:T(8,128)(2,1)S(1)}, bf16[256,256]{1,0:T(8,128)(2,1)S(1)}, u32[]{:S(2)}, u32[]{:S(2)}) collective-permute-start(bf16[256,256]{1,0:T(8,128)(2,1)S(1)} %get-tuple-element.28), channel_id=1, source_target_pairs={{0,8},{1,9},{2,10},{3,11},{4,12},{5,13},{6,14},{7,15},{8,0},{9,1},... | collective-permute-start | bytes 393224 | tf_op jit(solution)/shard_map/ppermute | solution.py:338
  81.6 7.2 %collective-permute-start.3 = (bf16[256,256]{1,0:T(8,128)(2,1)S(1)}, bf16[256,256]{1,0:T(8,128)(2,1)S(1)}, u32[]{:S(2)}, u32[]{:S(2)}) collective-permute-start(bf16[256,256]{1,0:T(8,128)(2,1)S(1)} %get-tuple-element.29), channel_id=1, source_target_pairs={{0,4},{1,5},{2,6},{3,7},{4,8},{5,9},{6,10},{7,11},{8,12},{9,13},{1... | collective-permute-start | bytes 393224 | tf_op jit(solution)/shard_map/ppermute | solution.py:338

commit v6 on v5

--- a/solution.py
+++ b/solution.py
@@ -119,20 +119,24 @@
 
 
 def slot_kernel(slots_ref, locals_ref, hit_ref, ids_ref):
-    rows, lanes = ids_ref.shape
+    owners, capacity, lanes = ids_ref.shape
+    rows = hit_ref.shape[0]
     slot = lax.broadcasted_iota(jnp.int32, (rows, rows), 0)
-    hit = (slot == slots_ref[...]).astype(jnp.bfloat16)
-    hit_ref[...] = hit
+    hit_ref[...] = (slot == slots_ref[...]).astype(jnp.bfloat16)
+    steps = rows // owners // capacity
+    wanted = lax.broadcasted_iota(jnp.int32, (owners * capacity, 1), 0) * steps
+    pick = (wanted == slots_ref[...]).astype(jnp.bfloat16)
     ids = locals_ref[...].astype(jnp.float32).astype(jnp.bfloat16)
-    ids_ref[...] = lax.dot_general(
-        hit,
+    spread = lax.dot_general(
+        pick,
         jnp.broadcast_to(ids, (lanes, rows)),
         (((1,), (1,)), ((), ())),
         preferred_element_type=jnp.float32,
-    ).astype(jnp.bfloat16)
-
-
-def slot_map(row_slots, row_locals):
+    )
+    ids_ref[...] = spread.reshape(owners, capacity, lanes).astype(jnp.bfloat16)
+
+
+def slot_map(row_slots, row_locals, owners, capacity):
     rows = row_slots.shape[1]
     resident = pl.BlockSpec(memory_space=pltpu.VMEM)
     return pl.pallas_call(
@@ -141,7 +145,7 @@
         out_specs=[resident] * 2,
         out_shape=[
             jax.ShapeDtypeStruct((rows, rows), jnp.bfloat16),
-            jax.ShapeDtypeStruct((rows, 128), jnp.bfloat16),
+            jax.ShapeDtypeStruct((owners, capacity, 128), jnp.bfloat16),
         ],
         compiler_params=pltpu.CompilerParams(vmem_limit_bytes=16 * 1024 * 1024),
         cost_estimate=pl.CostEstimate(
@@ -152,21 +156,25 @@
 
 
 def payload_kernel(rows_ref, hit_ref, ids_ref, out_ref):
-    width = rows_ref.shape[1]
-    out_ref[:, :width] = jnp.dot(
-        hit_ref[...], rows_ref[...], preferred_element_type=jnp.float32
-    ).astype(jnp.bfloat16)
-    out_ref[:, width:] = ids_ref[...]
+    owners, tiles, tile_rows, lanes = out_ref.shape
+    run = (tiles - 1) // 2
+    part = jnp.dot(hit_ref[...], rows_ref[...], preferred_element_type=jnp.float32)
+    for half in range(2):
+        piece = part[:, half * lanes : (half + 1) * lanes].reshape(owners, run, tile_rows, lanes)
+        out_ref[:, half * run : (half + 1) * run] = piece.astype(jnp.bfloat16)
+    out_ref[:, tiles - 1] = ids_ref[...]
 
 
 def make_payload(head_rows, hit, ids):
     rows, width = head_rows.shape
+    owners, tile_rows, lanes = ids.shape
+    tiles = rows // owners // tile_rows * (width // lanes) + 1
     resident = pl.BlockSpec(memory_space=pltpu.VMEM)
     return pl.pallas_call(
         payload_kernel,
         in_specs=[resident] * 3,
         out_specs=resident,
-        out_shape=jax.ShapeDtypeStruct((rows, width + ids.shape[1]), jnp.bfloat16),
+        out_shape=jax.ShapeDtypeStruct((owners, tiles, tile_rows, lanes), jnp.bfloat16),
         compiler_params=pltpu.CompilerParams(vmem_limit_bytes=16 * 1024 * 1024),
         cost_estimate=pl.CostEstimate(
             flops=2 * rows * rows * width, bytes_accessed=8 * rows * width, transcendentals=0
@@ -175,12 +183,12 @@
     )(head_rows, hit, ids)
 
 
-def project_kernel(rows_ref, wo_ref, *refs):
-    own_ref, own_buf, own_sem = refs[0], refs[SIDE], refs[SIDE + 1]
-    out_refs = (own_buf,) + refs[1:SIDE]
+def project_kernel(rows_ref, wo_ref, own_ref, far_ref, near_1_ref, near_3_ref, *scratch):
+    own_buf, far_buf, sems = scratch
     pair, line, pair_stride, line_stride = torus_place()
     width = rows_ref.shape[1]
-    for s, out_ref in enumerate(out_refs):
+    copies = []
+    for s, part_ref in ((0, own_buf), (2, far_buf), (1, near_1_ref), (3, near_3_ref)):
         along = lax.rem(line + s, SIDE)
         for u in range(SIDE):
             across = lax.rem(pair + u, SIDE)
@@ -188,24 +196,32 @@
             part = jnp.dot(
                 rows_ref[...], wo_ref[:, pl.ds(at, width)], preferred_element_type=jnp.float32
             )
-            out_ref[u] = part.astype(out_ref.dtype)
-        if s == 0:
-            own_copy = pltpu.make_async_copy(own_buf, own_ref, own_sem)
-            own_copy.start()
-    own_copy.wait()
+            part_ref[u] = part.astype(part_ref.dtype)
+        if s % 2 == 0:
+            target = own_ref if s == 0 else far_ref
+            copies.append(pltpu.make_async_copy(part_ref, target, sems.at[s // 2]))
+            copies[-1].start()
+    for copy in copies:
+        copy.wait()
 
 
 def project(head_rows, wo):
     rows, depth = head_rows.shape
     width = wo.shape[1] // (SIDE * SIDE)
-    resident = pl.BlockSpec(memory_space=pltpu.VMEM)
-    return pl.pallas_call(
+    shape = (SIDE, rows, width)
+    resident = pl.BlockSpec(memory_space=pltpu.VMEM)
+    distant = pl.BlockSpec(memory_space=pltpu.HBM)
+    own, far, near_1, near_3 = pl.pallas_call(
         project_kernel,
         in_specs=[resident] * 2,
-        out_specs=[pl.BlockSpec(memory_space=pltpu.HBM)] + [resident] * (SIDE - 1),
-        out_shape=[pltpu.HBM((SIDE, rows, width), jnp.float32)]
-        + [jax.ShapeDtypeStruct((SIDE, rows, width), jnp.bfloat16)] * (SIDE - 1),
-        scratch_shapes=[pltpu.VMEM((SIDE, rows, width), jnp.float32), pltpu.SemaphoreType.DMA],
+        out_specs=[distant] * 2 + [resident] * 2,
+        out_shape=[pltpu.HBM(shape, jnp.float32), pltpu.HBM(shape, jnp.bfloat16)]
+        + [jax.ShapeDtypeStruct(shape, jnp.bfloat16)] * 2,
+        scratch_shapes=[
+            pltpu.VMEM(shape, jnp.float32),
+            pltpu.VMEM(shape, jnp.bfloat16),
+            pltpu.SemaphoreType.DMA((2,)),
+        ],
         compiler_params=pltpu.CompilerParams(vmem_limit_bytes=16 * 1024 * 1024),
         cost_estimate=pl.CostEstimate(
             flops=2 * rows * depth * wo.shape[1],
@@ -214,20 +230,32 @@
         ),
         name="project",
     )(head_rows, wo)
+    return own, near_1, far, near_3
 
 
 def down_kernel(owned_ref, down_ref, up_ref, out_ref, ids_ref):
     del up_ref
-    rows, columns = owned_ref.shape[0], down_ref.shape[1]
-    rank = out_ref.shape[1]
+    sources, tiles, capacity, lanes = owned_ref.shape
+    run = (tiles - 1) // 2
+    rank, rows = out_ref.shape[1:]
     adapters = down_ref.shape[0] // rank
-    every = lax.dot_general(
-        down_ref[...],
-        owned_ref[:, :columns],
-        (((1,), (1,)), ((), ())),
-        preferred_element_type=jnp.float32,
-    )
-    ids = owned_ref[:, columns:].astype(jnp.float32)
+    every = 0.0
+    for half in range(2):
+        piece = owned_ref[:, half * run : (half + 1) * run].astype(jnp.float32)
+        every += lax.dot_general(
+            down_ref[:, half * lanes : (half + 1) * lanes],
+            piece.reshape(rows, lanes).astype(jnp.bfloat16),
+            (((1,), (1,)), ((), ())),
+            preferred_element_type=jnp.float32,
+        )
+    tile = owned_ref[:, tiles - 1].astype(jnp.float32)
+    ids = jnp.concatenate(
+        [
+            jnp.broadcast_to(tile[:, k : k + 1], (sources, rows // sources // capacity, lanes))
+            for k in range(capacity)
+        ],
+        axis=1,
+    ).reshape(rows, lanes)
     ids_ref[...] = ids
     adapter = lax.broadcasted_iota(jnp.int32, (adapters, rank, rows), 0).astype(jnp.float32)
     chosen = adapter == jnp.transpose(ids)[:1].reshape(1, 1, rows)
@@ -237,8 +265,8 @@
 
 
 def shrink_down(owned, down, up, shares, rank):
-    rows = owned.shape[0]
-    lanes = owned.shape[1] - down.shape[1]
+    sources, tiles, tile_rows, lanes = owned.shape
+    rows = sources * (tiles - 1) // 2 * tile_rows
     resident = pl.BlockSpec(memory_space=pltpu.VMEM)
     return pl.pallas_call(
         down_kernel,
@@ -367,7 +395,7 @@
     slots = owner_ids * capacity + jnp.sum(earlier.astype(jnp.int32), axis=1)
     row_slots = (slots[:, None] * steps + jnp.arange(steps, dtype=jnp.int32)).reshape(1, rows)
     row_locals = jnp.repeat(local_ids, steps)[None, :]
-    hit, id_lanes = slot_map(row_slots, row_locals)
+    hit, id_lanes = slot_map(row_slots, row_locals, owners, capacity)
 
     attended = attend(queries, cached_key_rows, cached_value_rows, cache_fill_length)
     head_rows = lax.all_to_all(attended, "tensor", 0, 0, tiled=True).reshape(rows, width)
@@ -378,9 +406,7 @@
         move(part, owners, lambda pair, line, s=s: (pair, (line + s) % SIDE))
         for s, part in enumerate(others, start=1)
     ]
-    owned = lax.all_to_all(
-        payload.reshape(owners, capacity * steps, width + 128), "dp", 0, 0, tiled=True
-    ).reshape(rows, width + 128)
+    owned = lax.all_to_all(payload, "dp", 0, 0, tiled=True)
     down = adapter_down_weight.reshape(owner_partial * rank, width)
     up = adapter_up_weight.reshape(owner_partial * rank, width)
     partial_shrink, ids = shrink_down(after(owned, own), down, up, shares, rank)

time: 93.2 us -> 91.2 us (0.979)
  waiting for transfers between devices: 25 us -> 22.9 us
  other arithmetic: 0.49 us -> 1.59 us
    all_to_all x1, waiting for transfers between devices: 2.79 us -> 1.7 us  [on_device(): lax.all_to_all(delta.reshape(owners, capacity * steps, width), 'dp', 0, 0...]
    add x1, other arithmetic: 0.23 us -> 1.32 us  [on_device(): own[u] + sum((part[u].astype(jnp.float32) for part in arrived))]
    all_to_all x1, waiting for transfers between devices: 8.72 us -> 7.65 us  [on_device(): owned = lax.all_to_all(payload, 'dp', 0, 0, tiled=True)]
  transfers between devices with their start and end apart: 10 -> 10, of which waited for: 6 -> 6; matrix products, arithmetic and copies ran while one was open for 1% -> 2% of each run, Pallas kernels for 5% -> 5%
where the time goes in v6:
time: 91.2 us; the launch traced here: 90.6 us
  starting transfers between devices  53.9 us (59%)
  waiting for transfers between devices  22.9 us (25%)
  Pallas kernels  11.7 us (13%)
  other arithmetic  1.59 us (2%)
    ppermute x6, starting transfers between devices, move(): return lax.ppermute(value, ('dp', 'tensor'), pairs)  19 us
    all_to_all x1, starting transfers between devices, on_device(): owned = lax.all_to_all(payload, 'dp', 0, 0, tiled=True)  17.4 us
    all_to_all x1, starting transfers between devices, on_device(): lax.all_to_all(attended, 'tensor', 0, 0, tiled=True).reshape(rows, width)  7.73 us
    all_to_all x1, waiting for transfers between devices, on_device(): owned = lax.all_to_all(payload, 'dp', 0, 0, tiled=True)  7.65 us
    all_to_all x1, starting transfers between devices, on_device(): lax.all_to_all(delta.reshape(owners, capacity * steps, width), 'dp', 0, 0...  6.35 us
    all_to_all x1, waiting for transfers between devices, on_device(): lax.all_to_all(attended, 'tensor', 0, 0, tiled=True).reshape(rows, width)  6.06 us
    ppermute x6, waiting for transfers between devices, move(): return lax.ppermute(value, ('dp', 'tensor'), pairs)  5.29 us
    pallas_call x1, Pallas kernels, attend(): pl.pallas_call(attend_kernel, in_specs=[pl.BlockSpec(memory_space=pltpu.S...  5.27 us
  transfers between devices with their start and end apart: 10, of which 6 were waited for; matrix products, arithmetic and copies ran while one was open for 2% of the time, Pallas kernels for 5%

profile of v6, /device:TPU:1, one launch (start us, length us, event | category | flops | bytes accessed | tf_op | source)
XLA Modules:
  0.0 90.6 jit_solution(3200997231446650118)
XLA Ops:
  0.0 5.3 %attend.1 = bf16[16,16,256]{2,1,0:T(8,128)(2,1)} custom-call(s32[4]{0:T(128)} %fill_ref.1, bf16[4,4,32,128]{3,2,1,0:T(8,128)(2,1)} %queries_ref.1, bf16[4,4,512,128]{3,2,1,0:T(8,128)(2,1)} %keys_ref.1, bf16[4,4,512,128]{3,2,1,0:T(8,128)(2,1)} %values_ref.1), custom_call_target="tpu_custom_call" | custom-call | flops 134217728 | bytes 4194304 | tf_op jit(solution)/shard_map/attend/pallas_call | solution.py:95
  5.3 0.0 copy-start.1
  5.3 0.0 copy-start.2
  5.3 7.7 %all-to-all-start = ((bf16[16,16,256]{2,1,0:T(8,128)(2,1)}), bf16[16,16,256]{2,1,0:T(8,128)(2,1)S(1)}, u32[]{:S(2)}, u32[]{:S(2)}) async-start(bf16[16,16,256]{2,1,0:T(8,128)(2,1)} %attend.1), calls=%async_computation | async-start | bytes 262144 | tf_op jit(solution)/shard_map/all_to_all | solution.py:401
  13.1 0.2 convert_reduce_fusion
  13.3 0.1 iota_add_fusion
  13.3 0.1 add.92.slots_ref
  13.5 0.1 broadcast_in_dim.2
  13.5 0.1 broadcast_in_dim_reshape.3.locals_ref
  13.6 0.2 slot_map.1
  13.8 6.1 %all-to-all-done = bf16[16,16,256]{2,1,0:T(8,128)(2,1)S(1)} async-done(((bf16[16,16,256]{2,1,0:T(8,128)(2,1)}), bf16[16,16,256]{2,1,0:T(8,128)(2,1)S(1)}, u32[]{:S(2)}, u32[]{:S(2)}) %all-to-all-start) | async-done | bytes 131104 | tf_op jit(solution)/shard_map/all_to_all | solution.py:401
  19.9 0.9 make_payload.1
  20.8 17.4 %all-to-all-start.1 = ((bf16[32,9,2,128]{3,2,1,0:T(2,128)(2,1)}), bf16[32,9,2,128]{3,2,1,0:T(2,128)(2,1)S(1)}, u32[]{:S(2)}, u32[]{:S(2)}) async-start(bf16[32,9,2,128]{3,2,1,0:T(2,128)(2,1)} %make_payload.1), calls=%async_computation.1 | async-start | bytes 294912 | tf_op jit(solution)/shard_map/all_to_all | solution.py:409
  38.2 2.3 %project.1 = (f32[4,256,256]{2,1,0:T(8,128)}, bf16[4,256,256]{2,1,0:T(8,128)(2,1)}, bf16[4,256,256]{2,1,0:T(8,128)(2,1)}, bf16[4,256,256]{2,1,0:T(8,128)(2,1)S(1)}) custom-call(bf16[256,256]{1,0:T(8,128)(2,1)S(1)} %bitcast.14, bf16[256,4096]{1,0:T(8,128)(2,1)S(1)} %copy-done), custom_call_target="tpu_custom_call" | custom-call | flops 536870912 | bytes 5242880 | tf_op jit(solution)/shard_map/project/pallas_call | solution.py:214
  40.5 1.9 %collective-permute-start = (bf16[4,256,256]{2,1,0:T(8,128)(2,1)}, bf16[4,256,256]{2,1,0:T(8,128)(2,1)S(1)}, u32[]{:S(2)}, u32[]{:S(2)}) collective-permute-start(bf16[4,256,256]{2,1,0:T(8,128)(2,1)} %get-tuple-element.22), channel_id=1, source_target_pairs={{0,1},{1,2},{2,3},{3,0},{4,5},{5,6},{6,7},{7,4},{8,9},{9,10},{10,1... | collective-permute-start | bytes 1572872 | tf_op jit(solution)/shard_map/ppermute | solution.py:366
  42.4 4.6 %collective-permute-start.1 = (bf16[4,256,256]{2,1,0:T(8,128)(2,1)S(1)}, bf16[4,256,256]{2,1,0:T(8,128)(2,1)S(1)}, u32[]{:S(2)}, u32[]{:S(2)}) collective-permute-start(bf16[4,256,256]{2,1,0:T(8,128)(2,1)S(1)} %get-tuple-element.23), channel_id=1, source_target_pairs={{0,3},{1,0},{2,1},{3,2},{4,7},{5,4},{6,5},{7,6},{8,11},{9,8},{10,9... | collective-permute-start | bytes 1572872 | tf_op jit(solution)/shard_map/ppermute | solution.py:366
  47.0 7.6 %all-to-all-done.1.owned_ref = bf16[32,9,2,128]{3,2,1,0:T(2,128)(2,1)S(1)} async-done(((bf16[32,9,2,128]{3,2,1,0:T(2,128)(2,1)}), bf16[32,9,2,128]{3,2,1,0:T(2,128)(2,1)S(1)}, u32[]{:S(2)}, u32[]{:S(2)}) %all-to-all-start.1) | async-done | bytes 147488 | tf_op jit(solution)/shard_map/all_to_all | solution.py:409
  54.6 1.0 %shrink_down.1 = (bf16[16,16,256]{2,1,0:T(8,128)(2,1)}, f32[256,128]{1,0:T(8,128)S(1)}) custom-call(bf16[32,9,2,128]{3,2,1,0:T(2,128)(2,1)S(1)} %all-to-all-done.1.owned_ref, bf16[512,256]{1,0:T(8,128)(2,1)S(1)} %bitcast.16, bf16[512,256]{1,0:T(8,128)(2,1)S(1)} %bitcast.17), custom_call_target="tpu_custom_call" | custom-call | flops 67108864 | bytes 524288 | tf_op jit(solution)/shard_map/shrink_down/pallas_call | solution.py:271
  55.7 3.5 %all-to-all-start.2 = ((bf16[16,16,256]{2,1,0:T(8,128)(2,1)}), bf16[16,16,256]{2,1,0:T(8,128)(2,1)S(1)}, u32[]{:S(2)}, u32[]{:S(2)}) async-start(bf16[16,16,256]{2,1,0:T(8,128)(2,1)} %get-tuple-element.21), calls=%async_computation.2 | async-start | bytes 262144 | tf_op jit(solution)/shard_map/all_to_all | solution.py:413
  59.2 4.7 %collective-permute-start.2 = (bf16[4,256,256]{2,1,0:T(8,128)(2,1)}, bf16[4,256,256]{2,1,0:T(8,128)(2,1)}, u32[]{:S(2)}, u32[]{:S(2)}) collective-permute-start(bf16[4,256,256]{2,1,0:T(8,128)(2,1)} %get-tuple-element.26), channel_id=1, source_target_pairs={{0,2},{1,3},{2,0},{3,1},{4,6},{5,7},{6,4},{7,5},{8,10},{9,11},{10,... | collective-permute-start | bytes 1572872 | tf_op jit(solution)/shard_map/ppermute | solution.py:366
  63.9 0.0 collective-permute-done.1
  63.9 2.2 %all-to-all-done.2.partials_ref = bf16[16,16,256]{2,1,0:T(8,128)(2,1)S(1)} async-done(((bf16[16,16,256]{2,1,0:T(8,128)(2,1)}), bf16[16,16,256]{2,1,0:T(8,128)(2,1)S(1)}, u32[]{:S(2)}, u32[]{:S(2)}) %all-to-all-start.2) | async-done | bytes 131104 | tf_op jit(solution)/shard_map/all_to_all | solution.py:413
  66.1 1.1 %expand_up.1 = bf16[256,256]{1,0:T(8,128)(2,1)} custom-call(bf16[16,16,256]{2,1,0:T(8,128)(2,1)S(1)} %all-to-all-done.2.partials_ref, f32[256,128]{1,0:T(8,128)S(1)} %get-tuple-element.25.ids_ref, bf16[512,256]{1,0:T(8,128)(2,1)S(1)} %bitcast.18), custom_call_target="tpu_custom_call" | custom-call | flops 20000000000 | bytes 524288 | tf_op jit(solution)/shard_map/expand_up/pallas_call | solution.py:314
  67.1 6.3 %all-to-all-start.3 = ((bf16[32,8,256]{2,1,0:T(8,128)(2,1)}), bf16[32,8,256]{2,1,0:T(8,128)(2,1)S(1)}, u32[]{:S(2)}, u32[]{:S(2)}) async-start(bf16[32,8,256]{2,1,0:T(8,128)(2,1)} %bitcast.3), calls=%async_computation.3 | async-start | bytes 262144 | tf_op jit(solution)/shard_map/all_to_all | solution.py:415
  73.5 1.3 %fusion.2 = (bf16[256,256]{1,0:T(8,128)(2,1)S(1)}, bf16[256,256]{1,0:T(8,128)(2,1)S(1)}, bf16[256,256]{1,0:T(8,128)(2,1)S(1)}, f32[256,256]{1,0:T(8,128)S(1)}) fusion(f32[4,256,256]{2,1,0:T(8,128)S(1)} %copy-done.3, bf16[4,256,256]{2,1,0:T(8,128)(2,1)S(1)} %copy-done.5, bf16[4,256,256]{2,1,0:T(8,128)(2,1)} %collective-permute-done.2, ...), kind=kLoop, calls=%fused_computation.6 | loop fusion | flops 1769472 | bytes 3276800 | tf_op jit(solution)/shard_map/add | solution.py:420
  74.8 2.8 %collective-permute-start.5 = (bf16[256,256]{1,0:T(8,128)(2,1)S(1)}, bf16[256,256]{1,0:T(8,128)(2,1)S(1)}, u32[]{:S(2)}, u32[]{:S(2)}) collective-permute-start(bf16[256,256]{1,0:T(8,128)(2,1)S(1)} %get-tuple-element.27), channel_id=1, source_target_pairs={{0,12},{1,13},{2,14},{3,15},{4,0},{5,1},{6,2},{7,3},{8,4},{9,5},{1... | collective-permute-start | bytes 393224 | tf_op jit(solution)/shard_map/ppermute | solution.py:366
  77.6 3.1 %collective-permute-start.4 = (bf16[256,256]{1,0:T(8,128)(2,1)S(1)}, bf16[256,256]{1,0:T(8,128)(2,1)S(1)}, u32[]{:S(2)}, u32[]{:S(2)}) collective-permute-start(bf16[256,256]{1,0:T(8,128)(2,1)S(1)} %get-tuple-element.28), channel_id=1, source_target_pairs={{0,8},{1,9},{2,10},{3,11},{4,12},{5,13},{6,14},{7,15},{8,0},{9,1},... | collective-permute-start | bytes 393224 | tf_op jit(solution)/shard_map/ppermute | solution.py:366
  80.7 1.9 %collective-permute-start.3 = (bf16[256,256]{1,0:T(8,128)(2,1)S(1)}, bf16[256,256]{1,0:T(8,128)(2,1)S(1)}, u32[]{:S(2)}, u32[]{:S(2)}) collective-permute-start(bf16[256,256]{1,0:T(8,128)(2,1)S(1)} %get-tuple-element.29), channel_id=1, source_target_pairs={{0,4},{1,5},{2,6},{3,7},{4,8},{5,9},{6,10},{7,11},{8,12},{9,13},{1... | collective-permute-start | bytes 393224 | tf_op jit(solution)/shard_map/ppermute | solution.py:366
  82.7 2.4 %collective-permute-done.4.refs_1_ = bf16[256,256]{1,0:T(8,128)(2,1)S(1)} collective-permute-done((bf16[256,256]{1,0:T(8,128)(2,1)S(1)}, bf16[256,256]{1,0:T(8,128)(2,1)S(1)}, u32[]{:S(2)}, u32[]{:S(2)}) %collective-permute-start.4) | collective-permute-done | bytes 131104 | tf_op jit(solution)/shard_map/ppermute | solution.py:366
  85.1 2.8 %collective-permute-done.3.refs_0_ = bf16[256,256]{1,0:T(8,128)(2,1)S(1)} collective-permute-done((bf16[256,256]{1,0:T(8,128)(2,1)S(1)}, bf16[256,256]{1,0:T(8,128)(2,1)S(1)}, u32[]{:S(2)}, u32[]{:S(2)}) %collective-permute-start.3) | collective-permute-done | bytes 131104 | tf_op jit(solution)/shard_map/ppermute | solution.py:366
  88.0 1.7 %all-to-all-done.3 = bf16[32,8,256]{2,1,0:T(8,128)(2,1)S(1)} async-done(((bf16[32,8,256]{2,1,0:T(8,128)(2,1)}), bf16[32,8,256]{2,1,0:T(8,128)(2,1)S(1)}, u32[]{:S(2)}, u32[]{:S(2)}) %all-to-all-start.3) | async-done | bytes 131104 | tf_op jit(solution)/shard_map/all_to_all | solution.py:415
  89.7 0.9 %finish.1 = bf16[64,4,256]{2,1,0:T(4,128)(2,1)} custom-call(bf16[256,256]{1,0:T(8,128)(2,1)S(1)} %get-tuple-element.16.hit_ref, bf16[256,256]{1,0:T(8,128)(2,1)S(1)} %bitcast.15, f32[256,256]{1,0:T(8,128)S(1)} %get-tuple-element.30.base_ref, bf16[256,256]{1,0:T(8,128)(2,1)S(1)} %collective-permute-done.3.refs_0_, ...), custom_call_target="tpu_custom_call" | custom-call | flops 33554432 | bytes 524288 | tf_op jit(solution)/shard_map/finish/pallas_call | solution.py:340
  (17 shorter events, 0.1 us)
Async XLA Ops:
  0.0 13.0 %copy-start.6 = (s32[64]{0:T(128)S(1)}, s32[64]{0:T(128)}, u32[]{:S(2)}) copy-start(s32[64]{0:T(128)} %param.12) | copy-start | bytes 772
  0.0 38.1 %copy-start = (bf16[256,4096]{1,0:T(8,128)(2,1)S(1)}, bf16[256,4096]{1,0:T(8,128)(2,1)}, u32[]{:S(2)}) copy-start(bf16[256,4096]{1,0:T(8,128)(2,1)} %wo_ref.1) | copy-start | bytes 6291460
  5.3 49.3 %copy-start.1 = (bf16[32,16,256]{2,1,0:T(8,128)(2,1)S(1)}, bf16[32,16,256]{2,1,0:T(8,128)(2,1)}, u32[]{:S(2)}) copy-start(bf16[32,16,256]{2,1,0:T(8,128)(2,1)} %param.14) | copy-start | bytes 786436
  5.3 49.3 %copy-start.2 = (bf16[32,16,256]{2,1,0:T(8,128)(2,1)S(1)}, bf16[32,16,256]{2,1,0:T(8,128)(2,1)}, u32[]{:S(2)}) copy-start(bf16[32,16,256]{2,1,0:T(8,128)(2,1)} %param.15) | copy-start | bytes 786436
  5.3 14.6 %all-to-all-start = ((bf16[16,16,256]{2,1,0:T(8,128)(2,1)}), bf16[16,16,256]{2,1,0:T(8,128)(2,1)S(1)}, u32[]{:S(2)}, u32[]{:S(2)}) async-start(bf16[16,16,256]{2,1,0:T(8,128)(2,1)} %attend.1), calls=%async_computation | async-start | bytes 262144 | tf_op jit(solution)/shard_map/all_to_all | solution.py:401
  20.8 33.8 %all-to-all-start.1 = ((bf16[32,9,2,128]{3,2,1,0:T(2,128)(2,1)}), bf16[32,9,2,128]{3,2,1,0:T(2,128)(2,1)S(1)}, u32[]{:S(2)}, u32[]{:S(2)}) async-start(bf16[32,9,2,128]{3,2,1,0:T(2,128)(2,1)} %make_payload.1), calls=%async_computation.1 | async-start | bytes 294912 | tf_op jit(solution)/shard_map/all_to_all | solution.py:409
  40.5 23.4 %collective-permute-start = (bf16[4,256,256]{2,1,0:T(8,128)(2,1)}, bf16[4,256,256]{2,1,0:T(8,128)(2,1)S(1)}, u32[]{:S(2)}, u32[]{:S(2)}) collective-permute-start(bf16[4,256,256]{2,1,0:T(8,128)(2,1)} %get-tuple-element.22), channel_id=1, source_target_pairs={{0,1},{1,2},{2,3},{3,0},{4,5},{5,6},{6,7},{7,4},{8,9},{9,10},{10,1... | collective-permute-start | bytes 1572872 | tf_op jit(solution)/shard_map/ppermute | solution.py:366
  42.4 21.5 %collective-permute-start.1 = (bf16[4,256,256]{2,1,0:T(8,128)(2,1)S(1)}, bf16[4,256,256]{2,1,0:T(8,128)(2,1)S(1)}, u32[]{:S(2)}, u32[]{:S(2)}) collective-permute-start(bf16[4,256,256]{2,1,0:T(8,128)(2,1)S(1)} %get-tuple-element.23), channel_id=1, source_target_pairs={{0,3},{1,0},{2,1},{3,2},{4,7},{5,4},{6,5},{7,6},{8,11},{9,8},{10,9... | collective-permute-start | bytes 1572872 | tf_op jit(solution)/shard_map/ppermute | solution.py:366
  55.7 10.4 %all-to-all-start.2 = ((bf16[16,16,256]{2,1,0:T(8,128)(2,1)}), bf16[16,16,256]{2,1,0:T(8,128)(2,1)S(1)}, u32[]{:S(2)}, u32[]{:S(2)}) async-start(bf16[16,16,256]{2,1,0:T(8,128)(2,1)} %get-tuple-element.21), calls=%async_computation.2 | async-start | bytes 262144 | tf_op jit(solution)/shard_map/all_to_all | solution.py:413
  59.2 14.3 %collective-permute-start.2 = (bf16[4,256,256]{2,1,0:T(8,128)(2,1)}, bf16[4,256,256]{2,1,0:T(8,128)(2,1)}, u32[]{:S(2)}, u32[]{:S(2)}) collective-permute-start(bf16[4,256,256]{2,1,0:T(8,128)(2,1)} %get-tuple-element.26), channel_id=1, source_target_pairs={{0,2},{1,3},{2,0},{3,1},{4,6},{5,7},{6,4},{7,5},{8,10},{9,11},{10,... | collective-permute-start | bytes 1572872 | tf_op jit(solution)/shard_map/ppermute | solution.py:366
  63.9 2.2 %copy-start.4 = (bf16[4,256,256]{2,1,0:T(8,128)(2,1)}, bf16[4,256,256]{2,1,0:T(8,128)(2,1)S(1)}, u32[]{:S(2)}) copy-start(bf16[4,256,256]{2,1,0:T(8,128)(2,1)S(1)} %collective-permute-done.1) | copy-start | bytes 1572868
  66.1 7.4 %copy-start.3 = (f32[4,256,256]{2,1,0:T(8,128)S(1)}, f32[4,256,256]{2,1,0:T(8,128)}, u32[]{:S(2)}) copy-start(f32[4,256,256]{2,1,0:T(8,128)} %get-tuple-element.19) | copy-start | bytes 3145732
  66.1 7.4 %copy-start.5 = (bf16[4,256,256]{2,1,0:T(8,128)(2,1)S(1)}, bf16[4,256,256]{2,1,0:T(8,128)(2,1)}, u32[]{:S(2)}) copy-start(bf16[4,256,256]{2,1,0:T(8,128)(2,1)} %copy-done.4) | copy-start | bytes 1572868
  67.1 22.5 %all-to-all-start.3 = ((bf16[32,8,256]{2,1,0:T(8,128)(2,1)}), bf16[32,8,256]{2,1,0:T(8,128)(2,1)S(1)}, u32[]{:S(2)}, u32[]{:S(2)}) async-start(bf16[32,8,256]{2,1,0:T(8,128)(2,1)} %bitcast.3), calls=%async_computation.3 | async-start | bytes 262144 | tf_op jit(solution)/shard_map/all_to_all | solution.py:415
  74.8 7.8 %collective-permute-start.5 = (bf16[256,256]{1,0:T(8,128)(2,1)S(1)}, bf16[256,256]{1,0:T(8,128)(2,1)S(1)}, u32[]{:S(2)}, u32[]{:S(2)}) collective-permute-start(bf16[256,256]{1,0:T(8,128)(2,1)S(1)} %get-tuple-element.27), channel_id=1, source_target_pairs={{0,12},{1,13},{2,14},{3,15},{4,0},{5,1},{6,2},{7,3},{8,4},{9,5},{1... | collective-permute-start | bytes 393224 | tf_op jit(solution)/shard_map/ppermute | solution.py:366
  77.6 7.5 %collective-permute-start.4 = (bf16[256,256]{1,0:T(8,128)(2,1)S(1)}, bf16[256,256]{1,0:T(8,128)(2,1)S(1)}, u32[]{:S(2)}, u32[]{:S(2)}) collective-permute-start(bf16[256,256]{1,0:T(8,128)(2,1)S(1)} %get-tuple-element.28), channel_id=1, source_target_pairs={{0,8},{1,9},{2,10},{3,11},{4,12},{5,13},{6,14},{7,15},{8,0},{9,1},... | collective-permute-start | bytes 393224 | tf_op jit(solution)/shard_map/ppermute | solution.py:366
  80.7 7.2 %collective-permute-start.3 = (bf16[256,256]{1,0:T(8,128)(2,1)S(1)}, bf16[256,256]{1,0:T(8,128)(2,1)S(1)}, u32[]{:S(2)}, u32[]{:S(2)}) collective-permute-start(bf16[256,256]{1,0:T(8,128)(2,1)S(1)} %get-tuple-element.29), channel_id=1, source_target_pairs={{0,4},{1,5},{2,6},{3,7},{4,8},{5,9},{6,10},{7,11},{8,12},{9,13},{1... | collective-permute-start | bytes 393224 | tf_op jit(solution)/shard_map/ppermute | solution.py:366

commit v7 on v6

--- a/solution.py
+++ b/solution.py
@@ -215,10 +215,10 @@
         project_kernel,
         in_specs=[resident] * 2,
         out_specs=[distant] * 2 + [resident] * 2,
-        out_shape=[pltpu.HBM(shape, jnp.float32), pltpu.HBM(shape, jnp.bfloat16)]
+        out_shape=[pltpu.HBM(shape, jnp.bfloat16)] * 2
         + [jax.ShapeDtypeStruct(shape, jnp.bfloat16)] * 2,
         scratch_shapes=[
-            pltpu.VMEM(shape, jnp.float32),
+            pltpu.VMEM(shape, jnp.bfloat16),
             pltpu.VMEM(shape, jnp.bfloat16),
             pltpu.SemaphoreType.DMA((2,)),
         ],
@@ -417,7 +417,7 @@
     ).reshape(rows, width)
 
     along_line = [
-        own[u] + sum(part[u].astype(jnp.float32) for part in arrived) for u in range(SIDE)
+        own[u].astype(jnp.float32) + sum(part[u].astype(jnp.float32) for part in arrived) for u in range(SIDE)
     ]
     across = [
         move(

time: 91.2 us -> 91.2 us (level)
  waiting for transfers between devices: 22.9 us -> 24.1 us
  other arithmetic: 1.59 us -> 0.52 us
    all_to_all x1, waiting for transfers between devices: 1.7 us -> 2.77 us  [on_device(): lax.all_to_all(delta.reshape(owners, capacity * steps, width), 'dp', 0, 0...]
    add x1, other arithmetic: 1.32 us -> 0.26 us  [on_device(): own[u].astype(jnp.float32)]
  transfers between devices with their start and end apart: 10 -> 10, of which waited for: 6 -> 6; matrix products, arithmetic and copies ran while one was open for 2% -> 1% of each run, Pallas kernels for 5% -> 5%
where the time goes in v7:
time: 91.2 us; the launch traced here: 90.6 us
  starting transfers between devices  53.9 us (59%)
  waiting for transfers between devices  24.1 us (26%)
  Pallas kernels  11.5 us (13%)
    ppermute x6, starting transfers between devices, move(): return lax.ppermute(value, ('dp', 'tensor'), pairs)  19 us
    all_to_all x1, starting transfers between devices, on_device(): owned = lax.all_to_all(payload, 'dp', 0, 0, tiled=True)  17.4 us
    all_to_all x1, waiting for transfers between devices, on_device(): owned = lax.all_to_all(payload, 'dp', 0, 0, tiled=True)  7.8 us
    all_to_all x1, starting transfers between devices, on_device(): lax.all_to_all(attended, 'tensor', 0, 0, tiled=True).reshape(rows, width)  7.73 us
    all_to_all x1, starting transfers between devices, on_device(): lax.all_to_all(delta.reshape(owners, capacity * steps, width), 'dp', 0, 0...  6.34 us
    all_to_all x1, waiting for transfers between devices, on_device(): lax.all_to_all(attended, 'tensor', 0, 0, tiled=True).reshape(rows, width)  6.06 us
    ppermute x6, waiting for transfers between devices, move(): return lax.ppermute(value, ('dp', 'tensor'), pairs)  5.29 us
    pallas_call x1, Pallas kernels, attend(): pl.pallas_call(attend_kernel, in_specs=[pl.BlockSpec(memory_space=pltpu.S...  5.27 us
  transfers between devices with their start and end apart: 10, of which 6 were waited for; matrix products, arithmetic and copies ran while one was open for 1% of the time, Pallas kernels for 5%

profile of v7, /device:TPU:1, one launch (start us, length us, event | category | flops | bytes accessed | tf_op | source)
XLA Modules:
  0.0 90.6 jit_solution(11946071280368095211)
XLA Ops:
  0.0 5.3 %attend.1 = bf16[16,16,256]{2,1,0:T(8,128)(2,1)} custom-call(s32[4]{0:T(128)} %fill_ref.1, bf16[4,4,32,128]{3,2,1,0:T(8,128)(2,1)} %queries_ref.1, bf16[4,4,512,128]{3,2,1,0:T(8,128)(2,1)} %keys_ref.1, bf16[4,4,512,128]{3,2,1,0:T(8,128)(2,1)} %values_ref.1), custom_call_target="tpu_custom_call" | custom-call | flops 134217728 | bytes 4194304 | tf_op jit(solution)/shard_map/attend/pallas_call | solution.py:95
  5.3 0.0 copy-start.1
  5.3 0.0 copy-start.2
  5.3 7.7 %all-to-all-start = ((bf16[16,16,256]{2,1,0:T(8,128)(2,1)}), bf16[16,16,256]{2,1,0:T(8,128)(2,1)S(1)}, u32[]{:S(2)}, u32[]{:S(2)}) async-start(bf16[16,16,256]{2,1,0:T(8,128)(2,1)} %attend.1), calls=%async_computation | async-start | bytes 262144 | tf_op jit(solution)/shard_map/all_to_all | solution.py:401
  13.1 0.2 convert_reduce_fusion
  13.3 0.1 iota_add_fusion
  13.3 0.1 add.92.slots_ref
  13.5 0.1 broadcast_in_dim.2
  13.5 0.1 broadcast_in_dim_reshape.3.locals_ref
  13.6 0.2 slot_map.1
  13.8 6.1 %all-to-all-done = bf16[16,16,256]{2,1,0:T(8,128)(2,1)S(1)} async-done(((bf16[16,16,256]{2,1,0:T(8,128)(2,1)}), bf16[16,16,256]{2,1,0:T(8,128)(2,1)S(1)}, u32[]{:S(2)}, u32[]{:S(2)}) %all-to-all-start) | async-done | bytes 131104 | tf_op jit(solution)/shard_map/all_to_all | solution.py:401
  19.9 0.9 %make_payload.1 = bf16[32,9,2,128]{3,2,1,0:T(2,128)(2,1)} custom-call(bf16[256,256]{1,0:T(8,128)(2,1)S(1)} %bitcast.13, bf16[256,256]{1,0:T(8,128)(2,1)S(1)} %get-tuple-element.16.hit_ref, bf16[32,2,128]{2,1,0:T(2,128)(2,1)S(1)} %get-tuple-element.17.ids_ref), custom_call_target="tpu_custom_call" | custom-call | flops 33554432 | bytes 524288 | tf_op jit(solution)/shard_map/make_payload/pallas_call | solution.py:173
  20.8 17.4 %all-to-all-start.1 = ((bf16[32,9,2,128]{3,2,1,0:T(2,128)(2,1)}), bf16[32,9,2,128]{3,2,1,0:T(2,128)(2,1)S(1)}, u32[]{:S(2)}, u32[]{:S(2)}) async-start(bf16[32,9,2,128]{3,2,1,0:T(2,128)(2,1)} %make_payload.1), calls=%async_computation.1 | async-start | bytes 294912 | tf_op jit(solution)/shard_map/all_to_all | solution.py:409
  38.2 2.1 %project.1 = (bf16[4,256,256]{2,1,0:T(8,128)(2,1)}, bf16[4,256,256]{2,1,0:T(8,128)(2,1)}, bf16[4,256,256]{2,1,0:T(8,128)(2,1)}, bf16[4,256,256]{2,1,0:T(8,128)(2,1)S(1)}) custom-call(bf16[256,256]{1,0:T(8,128)(2,1)S(1)} %bitcast.14, bf16[256,4096]{1,0:T(8,128)(2,1)S(1)} %copy-done), custom_call_target="tpu_custom_call" | custom-call | flops 536870912 | bytes 5242880 | tf_op jit(solution)/shard_map/project/pallas_call | solution.py:214
  40.3 1.9 %collective-permute-start = (bf16[4,256,256]{2,1,0:T(8,128)(2,1)}, bf16[4,256,256]{2,1,0:T(8,128)(2,1)S(1)}, u32[]{:S(2)}, u32[]{:S(2)}) collective-permute-start(bf16[4,256,256]{2,1,0:T(8,128)(2,1)} %get-tuple-element.22), channel_id=1, source_target_pairs={{0,1},{1,2},{2,3},{3,0},{4,5},{5,6},{6,7},{7,4},{8,9},{9,10},{10,1... | collective-permute-start | bytes 1572872 | tf_op jit(solution)/shard_map/ppermute | solution.py:366
  42.3 4.6 %collective-permute-start.1 = (bf16[4,256,256]{2,1,0:T(8,128)(2,1)S(1)}, bf16[4,256,256]{2,1,0:T(8,128)(2,1)S(1)}, u32[]{:S(2)}, u32[]{:S(2)}) collective-permute-start(bf16[4,256,256]{2,1,0:T(8,128)(2,1)S(1)} %get-tuple-element.23), channel_id=1, source_target_pairs={{0,3},{1,0},{2,1},{3,2},{4,7},{5,4},{6,5},{7,6},{8,11},{9,8},{10,9... | collective-permute-start | bytes 1572872 | tf_op jit(solution)/shard_map/ppermute | solution.py:366
  46.8 7.8 %all-to-all-done.1.owned_ref = bf16[32,9,2,128]{3,2,1,0:T(2,128)(2,1)S(1)} async-done(((bf16[32,9,2,128]{3,2,1,0:T(2,128)(2,1)}), bf16[32,9,2,128]{3,2,1,0:T(2,128)(2,1)S(1)}, u32[]{:S(2)}, u32[]{:S(2)}) %all-to-all-start.1) | async-done | bytes 147488 | tf_op jit(solution)/shard_map/all_to_all | solution.py:409
  54.6 1.0 %shrink_down.1 = (bf16[16,16,256]{2,1,0:T(8,128)(2,1)}, f32[256,128]{1,0:T(8,128)S(1)}) custom-call(bf16[32,9,2,128]{3,2,1,0:T(2,128)(2,1)S(1)} %all-to-all-done.1.owned_ref, bf16[512,256]{1,0:T(8,128)(2,1)S(1)} %bitcast.16, bf16[512,256]{1,0:T(8,128)(2,1)S(1)} %bitcast.17), custom_call_target="tpu_custom_call" | custom-call | flops 67108864 | bytes 524288 | tf_op jit(solution)/shard_map/shrink_down/pallas_call | solution.py:271
  55.7 3.5 %all-to-all-start.2 = ((bf16[16,16,256]{2,1,0:T(8,128)(2,1)}), bf16[16,16,256]{2,1,0:T(8,128)(2,1)S(1)}, u32[]{:S(2)}, u32[]{:S(2)}) async-start(bf16[16,16,256]{2,1,0:T(8,128)(2,1)} %get-tuple-element.21), calls=%async_computation.2 | async-start | bytes 262144 | tf_op jit(solution)/shard_map/all_to_all | solution.py:413
  59.2 4.7 %collective-permute-start.2 = (bf16[4,256,256]{2,1,0:T(8,128)(2,1)}, bf16[4,256,256]{2,1,0:T(8,128)(2,1)S(1)}, u32[]{:S(2)}, u32[]{:S(2)}) collective-permute-start(bf16[4,256,256]{2,1,0:T(8,128)(2,1)} %get-tuple-element.26), channel_id=1, source_target_pairs={{0,2},{1,3},{2,0},{3,1},{4,6},{5,7},{6,4},{7,5},{8,10},{9,11},{10,... | collective-permute-start | bytes 1572872 | tf_op jit(solution)/shard_map/ppermute | solution.py:366
  63.9 0.0 collective-permute-done
  63.9 2.2 %all-to-all-done.2.partials_ref = bf16[16,16,256]{2,1,0:T(8,128)(2,1)S(1)} async-done(((bf16[16,16,256]{2,1,0:T(8,128)(2,1)}), bf16[16,16,256]{2,1,0:T(8,128)(2,1)S(1)}, u32[]{:S(2)}, u32[]{:S(2)}) %all-to-all-start.2) | async-done | bytes 131104 | tf_op jit(solution)/shard_map/all_to_all | solution.py:413
  66.1 1.1 %expand_up.1 = bf16[256,256]{1,0:T(8,128)(2,1)} custom-call(bf16[16,16,256]{2,1,0:T(8,128)(2,1)S(1)} %all-to-all-done.2.partials_ref, f32[256,128]{1,0:T(8,128)S(1)} %get-tuple-element.25.ids_ref, bf16[512,256]{1,0:T(8,128)(2,1)S(1)} %bitcast.18), custom_call_target="tpu_custom_call" | custom-call | flops 20000000000 | bytes 524288 | tf_op jit(solution)/shard_map/expand_up/pallas_call | solution.py:314
  67.1 6.3 %all-to-all-start.3 = ((bf16[32,8,256]{2,1,0:T(8,128)(2,1)}), bf16[32,8,256]{2,1,0:T(8,128)(2,1)S(1)}, u32[]{:S(2)}, u32[]{:S(2)}) async-start(bf16[32,8,256]{2,1,0:T(8,128)(2,1)} %bitcast.3), calls=%async_computation.3 | async-start | bytes 262144 | tf_op jit(solution)/shard_map/all_to_all | solution.py:415
  73.5 0.3 fusion.2
  73.8 2.7 %collective-permute-start.5 = (bf16[256,256]{1,0:T(8,128)(2,1)S(1)}, bf16[256,256]{1,0:T(8,128)(2,1)S(1)}, u32[]{:S(2)}, u32[]{:S(2)}) collective-permute-start(bf16[256,256]{1,0:T(8,128)(2,1)S(1)} %get-tuple-element.27), channel_id=1, source_target_pairs={{0,12},{1,13},{2,14},{3,15},{4,0},{5,1},{6,2},{7,3},{8,4},{9,5},{1... | collective-permute-start | bytes 393224 | tf_op jit(solution)/shard_map/ppermute | solution.py:366
  76.5 3.2 %collective-permute-start.4 = (bf16[256,256]{1,0:T(8,128)(2,1)S(1)}, bf16[256,256]{1,0:T(8,128)(2,1)S(1)}, u32[]{:S(2)}, u32[]{:S(2)}) collective-permute-start(bf16[256,256]{1,0:T(8,128)(2,1)S(1)} %get-tuple-element.28), channel_id=1, source_target_pairs={{0,8},{1,9},{2,10},{3,11},{4,12},{5,13},{6,14},{7,15},{8,0},{9,1},... | collective-permute-start | bytes 393224 | tf_op jit(solution)/shard_map/ppermute | solution.py:366
  79.7 1.9 %collective-permute-start.3 = (bf16[256,256]{1,0:T(8,128)(2,1)S(1)}, bf16[256,256]{1,0:T(8,128)(2,1)S(1)}, u32[]{:S(2)}, u32[]{:S(2)}) collective-permute-start(bf16[256,256]{1,0:T(8,128)(2,1)S(1)} %get-tuple-element.29), channel_id=1, source_target_pairs={{0,4},{1,5},{2,6},{3,7},{4,8},{5,9},{6,10},{7,11},{8,12},{9,13},{1... | collective-permute-start | bytes 393224 | tf_op jit(solution)/shard_map/ppermute | solution.py:366
  81.6 2.4 %collective-permute-done.4.refs_1_ = bf16[256,256]{1,0:T(8,128)(2,1)S(1)} collective-permute-done((bf16[256,256]{1,0:T(8,128)(2,1)S(1)}, bf16[256,256]{1,0:T(8,128)(2,1)S(1)}, u32[]{:S(2)}, u32[]{:S(2)}) %collective-permute-start.4) | collective-permute-done | bytes 131104 | tf_op jit(solution)/shard_map/ppermute | solution.py:366
  84.0 2.9 %collective-permute-done.3.refs_0_ = bf16[256,256]{1,0:T(8,128)(2,1)S(1)} collective-permute-done((bf16[256,256]{1,0:T(8,128)(2,1)S(1)}, bf16[256,256]{1,0:T(8,128)(2,1)S(1)}, u32[]{:S(2)}, u32[]{:S(2)}) %collective-permute-start.3) | collective-permute-done | bytes 131104 | tf_op jit(solution)/shard_map/ppermute | solution.py:366
  86.9 2.8 %all-to-all-done.3 = bf16[32,8,256]{2,1,0:T(8,128)(2,1)S(1)} async-done(((bf16[32,8,256]{2,1,0:T(8,128)(2,1)}), bf16[32,8,256]{2,1,0:T(8,128)(2,1)S(1)}, u32[]{:S(2)}, u32[]{:S(2)}) %all-to-all-start.3) | async-done | bytes 131104 | tf_op jit(solution)/shard_map/all_to_all | solution.py:415
  89.7 0.9 %finish.1 = bf16[64,4,256]{2,1,0:T(4,128)(2,1)} custom-call(bf16[256,256]{1,0:T(8,128)(2,1)S(1)} %get-tuple-element.16.hit_ref, bf16[256,256]{1,0:T(8,128)(2,1)S(1)} %bitcast.15, f32[256,256]{1,0:T(8,128)S(1)} %get-tuple-element.30.base_ref, bf16[256,256]{1,0:T(8,128)(2,1)S(1)} %collective-permute-done.3.refs_0_, ...), custom_call_target="tpu_custom_call" | custom-call | flops 33554432 | bytes 524288 | tf_op jit(solution)/shard_map/finish/pallas_call | solution.py:340
  (13 shorter events, 0.0 us)
Async XLA Ops:
  0.0 13.0 %copy-start.4 = (s32[64]{0:T(128)S(1)}, s32[64]{0:T(128)}, u32[]{:S(2)}) copy-start(s32[64]{0:T(128)} %param.12) | copy-start | bytes 772
  0.0 38.2 %copy-start = (bf16[256,4096]{1,0:T(8,128)(2,1)S(1)}, bf16[256,4096]{1,0:T(8,128)(2,1)}, u32[]{:S(2)}) copy-start(bf16[256,4096]{1,0:T(8,128)(2,1)} %wo_ref.1) | copy-start | bytes 6291460
  5.3 49.4 %copy-start.1 = (bf16[32,16,256]{2,1,0:T(8,128)(2,1)S(1)}, bf16[32,16,256]{2,1,0:T(8,128)(2,1)}, u32[]{:S(2)}) copy-start(bf16[32,16,256]{2,1,0:T(8,128)(2,1)} %param.14) | copy-start | bytes 786436
  5.3 49.3 %copy-start.2 = (bf16[32,16,256]{2,1,0:T(8,128)(2,1)S(1)}, bf16[32,16,256]{2,1,0:T(8,128)(2,1)}, u32[]{:S(2)}) copy-start(bf16[32,16,256]{2,1,0:T(8,128)(2,1)} %param.15) | copy-start | bytes 786436
  5.3 14.6 %all-to-all-start = ((bf16[16,16,256]{2,1,0:T(8,128)(2,1)}), bf16[16,16,256]{2,1,0:T(8,128)(2,1)S(1)}, u32[]{:S(2)}, u32[]{:S(2)}) async-start(bf16[16,16,256]{2,1,0:T(8,128)(2,1)} %attend.1), calls=%async_computation | async-start | bytes 262144 | tf_op jit(solution)/shard_map/all_to_all | solution.py:401
  20.8 33.8 %all-to-all-start.1 = ((bf16[32,9,2,128]{3,2,1,0:T(2,128)(2,1)}), bf16[32,9,2,128]{3,2,1,0:T(2,128)(2,1)S(1)}, u32[]{:S(2)}, u32[]{:S(2)}) async-start(bf16[32,9,2,128]{3,2,1,0:T(2,128)(2,1)} %make_payload.1), calls=%async_computation.1 | async-start | bytes 294912 | tf_op jit(solution)/shard_map/all_to_all | solution.py:409
  40.3 23.6 %collective-permute-start = (bf16[4,256,256]{2,1,0:T(8,128)(2,1)}, bf16[4,256,256]{2,1,0:T(8,128)(2,1)S(1)}, u32[]{:S(2)}, u32[]{:S(2)}) collective-permute-start(bf16[4,256,256]{2,1,0:T(8,128)(2,1)} %get-tuple-element.22), channel_id=1, source_target_pairs={{0,1},{1,2},{2,3},{3,0},{4,5},{5,6},{6,7},{7,4},{8,9},{9,10},{10,1... | collective-permute-start | bytes 1572872 | tf_op jit(solution)/shard_map/ppermute | solution.py:366
  42.3 21.6 %collective-permute-start.1 = (bf16[4,256,256]{2,1,0:T(8,128)(2,1)S(1)}, bf16[4,256,256]{2,1,0:T(8,128)(2,1)S(1)}, u32[]{:S(2)}, u32[]{:S(2)}) collective-permute-start(bf16[4,256,256]{2,1,0:T(8,128)(2,1)S(1)} %get-tuple-element.23), channel_id=1, source_target_pairs={{0,3},{1,0},{2,1},{3,2},{4,7},{5,4},{6,5},{7,6},{8,11},{9,8},{10,9... | collective-permute-start | bytes 1572872 | tf_op jit(solution)/shard_map/ppermute | solution.py:366
  55.7 10.4 %all-to-all-start.2 = ((bf16[16,16,256]{2,1,0:T(8,128)(2,1)}), bf16[16,16,256]{2,1,0:T(8,128)(2,1)S(1)}, u32[]{:S(2)}, u32[]{:S(2)}) async-start(bf16[16,16,256]{2,1,0:T(8,128)(2,1)} %get-tuple-element.21), calls=%async_computation.2 | async-start | bytes 262144 | tf_op jit(solution)/shard_map/all_to_all | solution.py:413
  59.2 14.3 %collective-permute-start.2 = (bf16[4,256,256]{2,1,0:T(8,128)(2,1)}, bf16[4,256,256]{2,1,0:T(8,128)(2,1)S(1)}, u32[]{:S(2)}, u32[]{:S(2)}) collective-permute-start(bf16[4,256,256]{2,1,0:T(8,128)(2,1)} %get-tuple-element.26), channel_id=1, source_target_pairs={{0,2},{1,3},{2,0},{3,1},{4,6},{5,7},{6,4},{7,5},{8,10},{9,11},{10,... | collective-permute-start | bytes 1572872 | tf_op jit(solution)/shard_map/ppermute | solution.py:366
  66.1 7.4 %copy-start.3 = (bf16[4,256,256]{2,1,0:T(8,128)(2,1)S(1)}, bf16[4,256,256]{2,1,0:T(8,128)(2,1)}, u32[]{:S(2)}) copy-start(bf16[4,256,256]{2,1,0:T(8,128)(2,1)} %get-tuple-element.19) | copy-start | bytes 1572868
  67.1 22.5 %all-to-all-start.3 = ((bf16[32,8,256]{2,1,0:T(8,128)(2,1)}), bf16[32,8,256]{2,1,0:T(8,128)(2,1)S(1)}, u32[]{:S(2)}, u32[]{:S(2)}) async-start(bf16[32,8,256]{2,1,0:T(8,128)(2,1)} %bitcast.3), calls=%async_computation.3 | async-start | bytes 262144 | tf_op jit(solution)/shard_map/all_to_all | solution.py:415
  73.8 7.8 %collective-permute-start.5 = (bf16[256,256]{1,0:T(8,128)(2,1)S(1)}, bf16[256,256]{1,0:T(8,128)(2,1)S(1)}, u32[]{:S(2)}, u32[]{:S(2)}) collective-permute-start(bf16[256,256]{1,0:T(8,128)(2,1)S(1)} %get-tuple-element.27), channel_id=1, source_target_pairs={{0,12},{1,13},{2,14},{3,15},{4,0},{5,1},{6,2},{7,3},{8,4},{9,5},{1... | collective-permute-start | bytes 393224 | tf_op jit(solution)/shard_map/ppermute | solution.py:366
  76.5 7.5 %collective-permute-start.4 = (bf16[256,256]{1,0:T(8,128)(2,1)S(1)}, bf16[256,256]{1,0:T(8,128)(2,1)S(1)}, u32[]{:S(2)}, u32[]{:S(2)}) collective-permute-start(bf16[256,256]{1,0:T(8,128)(2,1)S(1)} %get-tuple-element.28), channel_id=1, source_target_pairs={{0,8},{1,9},{2,10},{3,11},{4,12},{5,13},{6,14},{7,15},{8,0},{9,1},... | collective-permute-start | bytes 393224 | tf_op jit(solution)/shard_map/ppermute | solution.py:366
  79.7 7.2 %collective-permute-start.3 = (bf16[256,256]{1,0:T(8,128)(2,1)S(1)}, bf16[256,256]{1,0:T(8,128)(2,1)S(1)}, u32[]{:S(2)}, u32[]{:S(2)}) collective-permute-start(bf16[256,256]{1,0:T(8,128)(2,1)S(1)} %get-tuple-element.29), channel_id=1, source_target_pairs={{0,4},{1,5},{2,6},{3,7},{4,8},{5,9},{6,10},{7,11},{8,12},{9,13},{1... | collective-permute-start | bytes 393224 | tf_op jit(solution)/shard_map/ppermute | solution.py:366

commit v8 on v6

--- a/solution.py
+++ b/solution.py
@@ -416,19 +416,22 @@
         delta.reshape(owners, capacity * steps, width), "dp", 0, 0, tiled=True
     ).reshape(rows, width)
 
-    along_line = [
-        own[u] + sum(part[u].astype(jnp.float32) for part in arrived) for u in range(SIDE)
+    to_send = [
+        (own[u] + sum(part[u].astype(jnp.float32) for part in arrived)).astype(jnp.bfloat16)
+        for u in range(1, SIDE)
     ]
+    kept_parts = lax.optimization_barrier((own[0], [part[0] for part in arrived], to_send))
+    kept = kept_parts[0] + sum(part.astype(jnp.float32) for part in kept_parts[1])
     across = [
         move(
-            along_line[u].astype(jnp.bfloat16),
+            to_send[u - 1],
             owners,
             lambda pair, line, u=u: ((pair + u) % SIDE, line),
         )
         for u in range(1, SIDE)
     ]
     return finish(
-        hit, returned, along_line[0], across, (group_size, steps, width)
+        hit, returned, kept, across, (group_size, steps, width)
     )
 
 

time: 91.2 us -> 107 us (1.17)
  waiting for transfers between devices: 22.9 us -> 29.8 us
  starting transfers between devices: 53.9 us -> 60.7 us
  local copies, waits for them, and re-layouts: 0.33 us -> 2.97 us
    all_to_all x1, waiting for transfers between devices: 1.7 us -> 14.8 us  [on_device(): lax.all_to_all(delta.reshape(owners, capacity * steps, width), 'dp', 0, 0...]
    ppermute x6, waiting for transfers between devices: 5.29 us -> 0.02 us  [move(): return lax.ppermute(value, ('dp', 'tensor'), pairs)]
    all_to_all x1, waiting for transfers between devices: 7.65 us -> 2.97 us  [on_device(): owned = lax.all_to_all(payload, 'dp', 0, 0, tiled=True)]
    all_to_all x1, starting transfers between devices: 6.35 us -> 10.6 us  [on_device(): lax.all_to_all(delta.reshape(owners, capacity * steps, width), 'dp', 0, 0...]
    all_to_all x1, waiting for transfers between devices: 2.16 us -> 5.92 us  [on_device(): partials = lax.all_to_all(partial_shrink, 'tensor', 0, 0, tiled=True)]
    squeeze x0 -> x3, local copies, waits for them, and re-layouts: none -> 1.84 us  [on_device(): part[0]]
    all_to_all x1, starting transfers between devices: 3.51 us -> 5.01 us  [on_device(): partials = lax.all_to_all(partial_shrink, 'tensor', 0, 0, tiled=True)]
  transfers between devices with their start and end apart: 10 -> 10, of which waited for: 6 -> 4; matrix products, arithmetic and copies ran while one was open for 2% -> 4% of each run, Pallas kernels for 5% -> 2%
where the time goes in v8:
time: 107 us; the launch traced here: 106 us
  starting transfers between devices  60.7 us (57%)
  waiting for transfers between devices  29.8 us (28%)
  Pallas kernels  10.9 us (10%)
  local copies, waits for them, and re-layouts  2.97 us (3%)
  other arithmetic  1.92 us (2%)
    ppermute x6, starting transfers between devices, move(): return lax.ppermute(value, ('dp', 'tensor'), pairs)  19.6 us
    all_to_all x1, starting transfers between devices, on_device(): owned = lax.all_to_all(payload, 'dp', 0, 0, tiled=True)  17.9 us
    all_to_all x1, waiting for transfers between devices, on_device(): lax.all_to_all(delta.reshape(owners, capacity * steps, width), 'dp', 0, 0...  14.8 us
    all_to_all x1, starting transfers between devices, on_device(): lax.all_to_all(delta.reshape(owners, capacity * steps, width), 'dp', 0, 0...  10.6 us
    all_to_all x1, starting transfers between devices, on_device(): lax.all_to_all(attended, 'tensor', 0, 0, tiled=True).reshape(rows, width)  7.6 us
    all_to_all x1, waiting for transfers between devices, on_device(): lax.all_to_all(attended, 'tensor', 0, 0, tiled=True).reshape(rows, width)  6.06 us
    all_to_all x1, waiting for transfers between devices, on_device(): partials = lax.all_to_all(partial_shrink, 'tensor', 0, 0, tiled=True)  5.92 us
    pallas_call x1, Pallas kernels, attend(): pl.pallas_call(attend_kernel, in_specs=[pl.BlockSpec(memory_space=pltpu.S...  5.27 us
  transfers between devices with their start and end apart: 10, of which 4 were waited for; matrix products, arithmetic and copies ran while one was open for 4% of the time, Pallas kernels for 2%

profile of v8, /device:TPU:1, one launch (start us, length us, event | category | flops | bytes accessed | tf_op | source)
XLA Modules:
  0.0 106.4 jit_solution(9409547412361242509)
XLA Ops:
  0.0 5.3 %attend.1 = bf16[16,16,256]{2,1,0:T(8,128)(2,1)} custom-call(s32[4]{0:T(128)} %fill_ref.1, bf16[4,4,32,128]{3,2,1,0:T(8,128)(2,1)} %queries_ref.1, bf16[4,4,512,128]{3,2,1,0:T(8,128)(2,1)} %keys_ref.1, bf16[4,4,512,128]{3,2,1,0:T(8,128)(2,1)} %values_ref.1), custom_call_target="tpu_custom_call" | custom-call | flops 134217728 | bytes 4194304 | tf_op jit(solution)/shard_map/attend/pallas_call | solution.py:95
  5.3 7.6 %all-to-all-start = ((bf16[16,16,256]{2,1,0:T(8,128)(2,1)}), bf16[16,16,256]{2,1,0:T(8,128)(2,1)S(1)}, u32[]{:S(2)}, u32[]{:S(2)}) async-start(bf16[16,16,256]{2,1,0:T(8,128)(2,1)} %attend.1), calls=%async_computation | async-start | bytes 262144 | tf_op jit(solution)/shard_map/all_to_all | solution.py:401
  12.9 0.2 convert_reduce_fusion
  13.1 0.1 iota_add_fusion
  13.2 0.1 add.88.slots_ref
  13.3 0.1 broadcast_in_dim.2
  13.4 0.1 broadcast_in_dim_reshape.3.locals_ref
  13.5 0.2 slot_map.1
  13.7 6.1 %all-to-all-done = bf16[16,16,256]{2,1,0:T(8,128)(2,1)S(1)} async-done(((bf16[16,16,256]{2,1,0:T(8,128)(2,1)}), bf16[16,16,256]{2,1,0:T(8,128)(2,1)S(1)}, u32[]{:S(2)}, u32[]{:S(2)}) %all-to-all-start) | async-done | bytes 131104 | tf_op jit(solution)/shard_map/all_to_all | solution.py:401
  19.7 0.9 make_payload.1
  20.6 1.5 %project.1 = (f32[4,256,256]{2,1,0:T(8,128)}, bf16[4,256,256]{2,1,0:T(8,128)(2,1)}, bf16[4,256,256]{2,1,0:T(8,128)(2,1)S(1)}, bf16[4,256,256]{2,1,0:T(8,128)(2,1)S(1)}) custom-call(bf16[256,256]{1,0:T(8,128)(2,1)S(1)} %bitcast.20, bf16[256,4096]{1,0:T(8,128)(2,1)S(1)} %copy-done), custom_call_target="tpu_custom_call" | custom-call | flops 536870912 | bytes 5242880 | tf_op jit(solution)/shard_map/project/pallas_call | solution.py:214
  22.1 0.0 copy-start.1
  22.2 2.1 %collective-permute-start = (bf16[4,256,256]{2,1,0:T(8,128)(2,1)S(1)}, bf16[4,256,256]{2,1,0:T(8,128)(2,1)}, u32[]{:S(2)}, u32[]{:S(2)}) collective-permute-start(bf16[4,256,256]{2,1,0:T(8,128)(2,1)S(1)} %get-tuple-element.26), channel_id=1, source_target_pairs={{0,1},{1,2},{2,3},{3,0},{4,5},{5,6},{6,7},{7,4},{8,9},{9,10},{10,1... | collective-permute-start | bytes 1572872 | tf_op jit(solution)/shard_map/ppermute | solution.py:366
  24.2 4.6 %collective-permute-start.1 = (bf16[4,256,256]{2,1,0:T(8,128)(2,1)S(1)}, bf16[4,256,256]{2,1,0:T(8,128)(2,1)S(1)}, u32[]{:S(2)}, u32[]{:S(2)}) collective-permute-start(bf16[4,256,256]{2,1,0:T(8,128)(2,1)S(1)} %get-tuple-element.27), channel_id=1, source_target_pairs={{0,3},{1,0},{2,1},{3,2},{4,7},{5,4},{6,5},{7,6},{8,11},{9,8},{10,9... | collective-permute-start | bytes 1572872 | tf_op jit(solution)/shard_map/ppermute | solution.py:366
  28.8 1.9 %collective-permute-start.2 = (bf16[4,256,256]{2,1,0:T(8,128)(2,1)}, bf16[4,256,256]{2,1,0:T(8,128)(2,1)S(1)}, u32[]{:S(2)}, u32[]{:S(2)}) collective-permute-start(bf16[4,256,256]{2,1,0:T(8,128)(2,1)} %get-tuple-element.30), channel_id=1, source_target_pairs={{0,2},{1,3},{2,0},{3,1},{4,6},{5,7},{6,4},{7,5},{8,10},{9,11},{10,... | collective-permute-start | bytes 1572872 | tf_op jit(solution)/shard_map/ppermute | solution.py:366
  30.7 17.9 %all-to-all-start.1 = ((bf16[32,9,2,128]{3,2,1,0:T(2,128)(2,1)}), bf16[32,9,2,128]{3,2,1,0:T(2,128)(2,1)S(1)}, u32[]{:S(2)}, u32[]{:S(2)}) async-start(bf16[32,9,2,128]{3,2,1,0:T(2,128)(2,1)} %make_payload.1), calls=%async_computation.1 | async-start | bytes 294912 | tf_op jit(solution)/shard_map/all_to_all | solution.py:409
  48.7 0.8 copy-done.3
  49.5 1.6 %fusion.2 = (bf16[256,256]{1,0:T(8,128)(2,1)S(1)}, bf16[256,256]{1,0:T(8,128)(2,1)S(1)}, bf16[256,256]{1,0:T(8,128)(2,1)S(1)}, f32[256,256]{1,0:T(8,128)S(1)}) fusion(f32[4,256,256]{2,1,0:T(8,128)} %get-tuple-element.23, bf16[4,256,256]{2,1,0:T(8,128)(2,1)S(1)} %collective-permute-done.1, bf16[4,256,256]{2,1,0:T(8,128)(2,1)} %copy-done.3, ...), kind=kLoop, calls=%fused_computation.7 | loop fusion | flops 1376256 | bytes 2883584 | tf_op jit(solution)/shard_map/add | solution.py:420
  51.1 2.5 %collective-permute-start.3 = (bf16[256,256]{1,0:T(8,128)(2,1)S(1)}, bf16[256,256]{1,0:T(8,128)(2,1)S(1)}, u32[]{:S(2)}, u32[]{:S(2)}) collective-permute-start(bf16[256,256]{1,0:T(8,128)(2,1)S(1)} %get-tuple-element.37), channel_id=1, source_target_pairs={{0,4},{1,5},{2,6},{3,7},{4,8},{5,9},{6,10},{7,11},{8,12},{9,13},{1... | collective-permute-start | bytes 393224 | tf_op jit(solution)/shard_map/ppermute | solution.py:366
  53.6 4.6 %collective-permute-start.4 = (bf16[256,256]{1,0:T(8,128)(2,1)S(1)}, bf16[256,256]{1,0:T(8,128)(2,1)S(1)}, u32[]{:S(2)}, u32[]{:S(2)}) collective-permute-start(bf16[256,256]{1,0:T(8,128)(2,1)S(1)} %get-tuple-element.36), channel_id=1, source_target_pairs={{0,8},{1,9},{2,10},{3,11},{4,12},{5,13},{6,14},{7,15},{8,0},{9,1},... | collective-permute-start | bytes 393224 | tf_op jit(solution)/shard_map/ppermute | solution.py:366
  58.2 4.0 %collective-permute-start.5 = (bf16[256,256]{1,0:T(8,128)(2,1)S(1)}, bf16[256,256]{1,0:T(8,128)(2,1)S(1)}, u32[]{:S(2)}, u32[]{:S(2)}) collective-permute-start(bf16[256,256]{1,0:T(8,128)(2,1)S(1)} %get-tuple-element.35), channel_id=1, source_target_pairs={{0,12},{1,13},{2,14},{3,15},{4,0},{5,1},{6,2},{7,3},{8,4},{9,5},{1... | collective-permute-start | bytes 393224 | tf_op jit(solution)/shard_map/ppermute | solution.py:366
  62.2 3.0 %all-to-all-done.1.owned_ref = bf16[32,9,2,128]{3,2,1,0:T(2,128)(2,1)S(1)} async-done(((bf16[32,9,2,128]{3,2,1,0:T(2,128)(2,1)}), bf16[32,9,2,128]{3,2,1,0:T(2,128)(2,1)S(1)}, u32[]{:S(2)}, u32[]{:S(2)}) %all-to-all-start.1) | async-done | bytes 147488 | tf_op jit(solution)/shard_map/all_to_all | solution.py:409
  65.1 1.0 shrink_down.1
  66.2 5.0 %all-to-all-start.2 = ((bf16[16,16,256]{2,1,0:T(8,128)(2,1)}), bf16[16,16,256]{2,1,0:T(8,128)(2,1)S(1)}, u32[]{:S(2)}, u32[]{:S(2)}) async-start(bf16[16,16,256]{2,1,0:T(8,128)(2,1)} %get-tuple-element.25), calls=%async_computation.2 | async-start | bytes 262144 | tf_op jit(solution)/shard_map/all_to_all | solution.py:413
  71.2 0.9 slice_bitcast_fusion.3
  72.1 5.9 %all-to-all-done.2.partials_ref = bf16[16,16,256]{2,1,0:T(8,128)(2,1)S(1)} async-done(((bf16[16,16,256]{2,1,0:T(8,128)(2,1)}), bf16[16,16,256]{2,1,0:T(8,128)(2,1)S(1)}, u32[]{:S(2)}, u32[]{:S(2)}) %all-to-all-start.2) | async-done | bytes 131104 | tf_op jit(solution)/shard_map/all_to_all | solution.py:413
  78.0 1.1 expand_up.1
  79.1 10.6 %all-to-all-start.3 = ((bf16[32,8,256]{2,1,0:T(8,128)(2,1)}), bf16[32,8,256]{2,1,0:T(8,128)(2,1)S(1)}, u32[]{:S(2)}, u32[]{:S(2)}) async-start(bf16[32,8,256]{2,1,0:T(8,128)(2,1)} %bitcast.3), calls=%async_computation.3 | async-start | bytes 262144 | tf_op jit(solution)/shard_map/all_to_all | solution.py:415
  89.6 0.9 slice_bitcast_fusion.2
  90.6 0.1 add_add_fusion.base_ref
  90.7 14.8 %all-to-all-done.3 = bf16[32,8,256]{2,1,0:T(8,128)(2,1)S(1)} async-done(((bf16[32,8,256]{2,1,0:T(8,128)(2,1)}), bf16[32,8,256]{2,1,0:T(8,128)(2,1)S(1)}, u32[]{:S(2)}, u32[]{:S(2)}) %all-to-all-start.3) | async-done | bytes 131104 | tf_op jit(solution)/shard_map/all_to_all | solution.py:415
  105.5 0.9 finish.1
  (17 shorter events, 0.1 us)
Async XLA Ops:
  0.0 12.9 %copy-start.4 = (s32[64]{0:T(128)S(1)}, s32[64]{0:T(128)}, u32[]{:S(2)}) copy-start(s32[64]{0:T(128)} %param.12) | copy-start | bytes 772
  0.0 20.6 %copy-start = (bf16[256,4096]{1,0:T(8,128)(2,1)S(1)}, bf16[256,4096]{1,0:T(8,128)(2,1)}, u32[]{:S(2)}) copy-start(bf16[256,4096]{1,0:T(8,128)(2,1)} %wo_ref.1) | copy-start | bytes 6291460
  5.3 14.4 %all-to-all-start = ((bf16[16,16,256]{2,1,0:T(8,128)(2,1)}), bf16[16,16,256]{2,1,0:T(8,128)(2,1)S(1)}, u32[]{:S(2)}, u32[]{:S(2)}) async-start(bf16[16,16,256]{2,1,0:T(8,128)(2,1)} %attend.1), calls=%async_computation | async-start | bytes 262144 | tf_op jit(solution)/shard_map/all_to_all | solution.py:401
  22.1 43.0 %copy-start.1 = (bf16[32,16,256]{2,1,0:T(8,128)(2,1)S(1)}, bf16[32,16,256]{2,1,0:T(8,128)(2,1)}, u32[]{:S(2)}) copy-start(bf16[32,16,256]{2,1,0:T(8,128)(2,1)} %param.14) | copy-start | bytes 786436
  22.1 43.0 %copy-start.2 = (bf16[32,16,256]{2,1,0:T(8,128)(2,1)S(1)}, bf16[32,16,256]{2,1,0:T(8,128)(2,1)}, u32[]{:S(2)}) copy-start(bf16[32,16,256]{2,1,0:T(8,128)(2,1)} %param.15) | copy-start | bytes 786436
  22.2 26.5 %collective-permute-start = (bf16[4,256,256]{2,1,0:T(8,128)(2,1)S(1)}, bf16[4,256,256]{2,1,0:T(8,128)(2,1)}, u32[]{:S(2)}, u32[]{:S(2)}) collective-permute-start(bf16[4,256,256]{2,1,0:T(8,128)(2,1)S(1)} %get-tuple-element.26), channel_id=1, source_target_pairs={{0,1},{1,2},{2,3},{3,0},{4,5},{5,6},{6,7},{7,4},{8,9},{9,10},{10,1... | collective-permute-start | bytes 1572872 | tf_op jit(solution)/shard_map/ppermute | solution.py:366
  24.2 24.4 %collective-permute-start.1 = (bf16[4,256,256]{2,1,0:T(8,128)(2,1)S(1)}, bf16[4,256,256]{2,1,0:T(8,128)(2,1)S(1)}, u32[]{:S(2)}, u32[]{:S(2)}) collective-permute-start(bf16[4,256,256]{2,1,0:T(8,128)(2,1)S(1)} %get-tuple-element.27), channel_id=1, source_target_pairs={{0,3},{1,0},{2,1},{3,2},{4,7},{5,4},{6,5},{7,6},{8,11},{9,8},{10,9... | collective-permute-start | bytes 1572872 | tf_op jit(solution)/shard_map/ppermute | solution.py:366
  28.8 19.9 %collective-permute-start.2 = (bf16[4,256,256]{2,1,0:T(8,128)(2,1)}, bf16[4,256,256]{2,1,0:T(8,128)(2,1)S(1)}, u32[]{:S(2)}, u32[]{:S(2)}) collective-permute-start(bf16[4,256,256]{2,1,0:T(8,128)(2,1)} %get-tuple-element.30), channel_id=1, source_target_pairs={{0,2},{1,3},{2,0},{3,1},{4,6},{5,7},{6,4},{7,5},{8,10},{9,11},{10,... | collective-permute-start | bytes 1572872 | tf_op jit(solution)/shard_map/ppermute | solution.py:366
  30.7 34.4 %all-to-all-start.1 = ((bf16[32,9,2,128]{3,2,1,0:T(2,128)(2,1)}), bf16[32,9,2,128]{3,2,1,0:T(2,128)(2,1)S(1)}, u32[]{:S(2)}, u32[]{:S(2)}) async-start(bf16[32,9,2,128]{3,2,1,0:T(2,128)(2,1)} %make_payload.1), calls=%async_computation.1 | async-start | bytes 294912 | tf_op jit(solution)/shard_map/all_to_all | solution.py:409
  48.7 0.8 copy-start.3
  51.1 39.5 %collective-permute-start.3 = (bf16[256,256]{1,0:T(8,128)(2,1)S(1)}, bf16[256,256]{1,0:T(8,128)(2,1)S(1)}, u32[]{:S(2)}, u32[]{:S(2)}) collective-permute-start(bf16[256,256]{1,0:T(8,128)(2,1)S(1)} %get-tuple-element.37), channel_id=1, source_target_pairs={{0,4},{1,5},{2,6},{3,7},{4,8},{5,9},{6,10},{7,11},{8,12},{9,13},{1... | collective-permute-start | bytes 393224 | tf_op jit(solution)/shard_map/ppermute | solution.py:366
  53.6 37.1 %collective-permute-start.4 = (bf16[256,256]{1,0:T(8,128)(2,1)S(1)}, bf16[256,256]{1,0:T(8,128)(2,1)S(1)}, u32[]{:S(2)}, u32[]{:S(2)}) collective-permute-start(bf16[256,256]{1,0:T(8,128)(2,1)S(1)} %get-tuple-element.36), channel_id=1, source_target_pairs={{0,8},{1,9},{2,10},{3,11},{4,12},{5,13},{6,14},{7,15},{8,0},{9,1},... | collective-permute-start | bytes 393224 | tf_op jit(solution)/shard_map/ppermute | solution.py:366
  58.2 32.5 %collective-permute-start.5 = (bf16[256,256]{1,0:T(8,128)(2,1)S(1)}, bf16[256,256]{1,0:T(8,128)(2,1)S(1)}, u32[]{:S(2)}, u32[]{:S(2)}) collective-permute-start(bf16[256,256]{1,0:T(8,128)(2,1)S(1)} %get-tuple-element.35), channel_id=1, source_target_pairs={{0,12},{1,13},{2,14},{3,15},{4,0},{5,1},{6,2},{7,3},{8,4},{9,5},{1... | collective-permute-start | bytes 393224 | tf_op jit(solution)/shard_map/ppermute | solution.py:366
  66.2 11.9 %all-to-all-start.2 = ((bf16[16,16,256]{2,1,0:T(8,128)(2,1)}), bf16[16,16,256]{2,1,0:T(8,128)(2,1)S(1)}, u32[]{:S(2)}, u32[]{:S(2)}) async-start(bf16[16,16,256]{2,1,0:T(8,128)(2,1)} %get-tuple-element.25), calls=%async_computation.2 | async-start | bytes 262144 | tf_op jit(solution)/shard_map/all_to_all | solution.py:413
  79.1 26.4 %all-to-all-start.3 = ((bf16[32,8,256]{2,1,0:T(8,128)(2,1)}), bf16[32,8,256]{2,1,0:T(8,128)(2,1)S(1)}, u32[]{:S(2)}, u32[]{:S(2)}) async-start(bf16[32,8,256]{2,1,0:T(8,128)(2,1)} %bitcast.3), calls=%async_computation.3 | async-start | bytes 262144 | tf_op jit(solution)/shard_map/all_to_all | solution.py:415
